TPU v7x, 512 devices: a whole 4x8x8 slice. The times are simulated.
512 devices in a mesh: gy: 16 (over x_hi, y), gx: 16 (over x_lo, z), img: 2 (over core).
Axes of the slice: x: 4 (x_hi: 2, x_lo: 2; x = x_hi * 2 + x_lo), y: 8, z: 8, core: 2. Of those that a mesh axis runs over, the one named last changes fastest.
Arguments:
- heights: float32 [4096, 4096], P('gy', 'gx'), may hold values from -4 to 4
- albedo: float32 [4096, 4096], P('gy', 'gx'), may hold values from 0.5 to 1.2
- images: bfloat16 [8, 4096, 4096], P('img', 'gy', 'gx'), may hold values from 0 to 1.5
- weights: bfloat16 [8, 4096, 4096], P('img', 'gy', 'gx'), may hold values from 0 to 1
- sun_index: int32 [8], P('img'), may hold values from 0 to 7
- expo_index: int32 [8], P('img'), may hold values from 0 to 7
- sun_azimuth: float32 [8], replicated, may hold values from -3.140625 to 3.140625
- sun_elevation: float32 [8], replicated, may hold values from 0.005 to 0.05
- exposure: float32 [8], replicated, may hold values from 0.5 to 1.5
Outputs:
- refined_heights: float32 [4096, 4096], P('gy', 'gx')
- refined_albedo: float32 [4096, 4096], P('gy', 'gx')
All inputs are finite; a program needn't handle non-finite values.
Results may differ from a plain program's by a relative error of at most 0.0003.
Values sent between devices are 32-bit elements; how exact they have to be, the bound alone decides.
No kernel may reach another device: no remote copies, remote signals or barrier semaphores. Data moves between devices by JAX's collectives and lax.ppermute only.
A program may use at most 64 MiB of HBM per device.

v0:
```python
import jax
import jax.numpy as jnp
from jax import lax
from jax.sharding import PartitionSpec as P

ITERS = 3


def with_halo(x, sides, width):
    for axis, dim in sides:
        size, length = (lax.axis_size(axis), x.shape[dim])
        up = [(i, (i + 1) % size) for i in range(size - 1)]
        down = [(j, i) for i, j in up]
        last = lax.slice_in_dim(x, length - width, length, axis=dim)
        first = lax.slice_in_dim(x, 0, width, axis=dim)
        before = lax.ppermute(last, axis, up)
        after = lax.ppermute(first, axis, down)
        x = jnp.concatenate([before, x, after], axis=dim)
    return x


def lookup(index, table):
    hits = index[:, None] == jnp.arange(table.shape[0], dtype=jnp.int32)[None, :]
    return jnp.sum(jnp.where(hits, table[None, :], jnp.float32(0.0)), axis=1)


def border_flags():
    first_y = lax.axis_index("gy") == 0
    last_y = lax.axis_index("gy") == lax.axis_size("gy") - 1
    first_x = lax.axis_index("gx") == 0
    last_x = lax.axis_index("gx") == lax.axis_size("gx") - 1
    return (first_y, last_y, first_x, last_x)


def slopes(tile):
    first_y, last_y, first_x, last_x = border_flags()
    padded = with_halo(tile, (("gy", 0), ("gx", 1)), 1)
    upper = jnp.where(first_y, tile[0], padded[0, 1:-1])
    lower = jnp.where(last_y, tile[-1], padded[-1, 1:-1])
    left = jnp.where(first_x, tile[:, 0], padded[1:-1, 0])
    right = jnp.where(last_x, tile[:, -1], padded[1:-1, -1])
    east = jnp.concatenate([tile[:, 1:], right[:, None]], axis=1)
    west = jnp.concatenate([left[:, None], tile[:, :-1]], axis=1)
    below = jnp.concatenate([tile[1:], lower[None, :]], axis=0)
    above = jnp.concatenate([upper[None, :], tile[:-1]], axis=0)
    return (0.5 * (east - west), 0.5 * (below - above))


def adjoint(grad_p, grad_q):
    first_y, last_y, first_x, last_x = border_flags()
    wide = with_halo(grad_p, (("gx", 1),), 1)
    left = jnp.where(first_x, -grad_p[:, 0], wide[:, 0])
    right = jnp.where(last_x, -grad_p[:, -1], wide[:, -1])
    east = jnp.concatenate([grad_p[:, 1:], right[:, None]], axis=1)
    west = jnp.concatenate([left[:, None], grad_p[:, :-1]], axis=1)
    tall = with_halo(grad_q, (("gy", 0),), 1)
    upper = jnp.where(first_y, -grad_q[0], tall[0])
    lower = jnp.where(last_y, -grad_q[-1], tall[-1])
    below = jnp.concatenate([grad_q[1:], lower[None, :]], axis=0)
    above = jnp.concatenate([upper[None, :], grad_q[:-1]], axis=0)
    return 0.5 * (west - east) + 0.5 * (above - below)


def shards(
    heights, albedo, images, weights, sun_index, expo_index, sun_azimuth, sun_elevation, exposure
):
    azim = lookup(sun_index, sun_azimuth)
    elev = lookup(sun_index, sun_elevation)
    gains = lookup(expo_index, exposure)
    sun_x = jnp.cos(elev) * jnp.cos(azim)
    sun_y = jnp.cos(elev) * jnp.sin(azim)
    sun_z = jnp.sin(elev)
    count = images.shape[0]
    total = count * lax.axis_size("img")
    rate_h = 0.2 / total
    rate_a = 0.5 / total
    height = heights
    albedo_now = albedo
    for step in range(ITERS):
        slope_p, slope_q = slopes(height)
        scale = 1.0 / jnp.sqrt(1.0 + slope_p * slope_p + slope_q * slope_q)
        cubed = scale * scale * scale
        grad_p = jnp.zeros_like(height)
        grad_q = jnp.zeros_like(height)
        grad_a = jnp.zeros_like(height)
        for k in range(count):
            shade = sun_z[k] - slope_p * sun_x[k] - slope_q * sun_y[k]
            resid = (
                weights[k].astype(jnp.float32)
                * (gains[k] * albedo_now * shade * scale - images[k].astype(jnp.float32))
                * gains[k]
            )
            grad_p = grad_p + resid * albedo_now * (-sun_x[k] * scale - shade * slope_p * cubed)
            grad_q = grad_q + resid * albedo_now * (-sun_y[k] * scale - shade * slope_q * cubed)
            grad_a = grad_a + resid * shade * scale
        grad_p, grad_q, grad_a = lax.psum((grad_p, grad_q, grad_a), "img")
        grad_h = adjoint(grad_p + 0.3 * slope_p, grad_q + 0.3 * slope_q)
        height = height - rate_h * grad_h
        albedo_now = albedo_now - rate_a * grad_a
    return (height, albedo_now)


def solution(mesh):
    return jax.shard_map(
        shards,
        mesh=mesh,
        in_specs=(
            P("gy", "gx"),
            P("gy", "gx"),
            P("img", "gy", "gx"),
            P("img", "gy", "gx"),
            P("img"),
            P("img"),
            P(),
            P(),
            P(),
        ),
        out_specs=(P("gy", "gx"), P("gy", "gx")),
        check_vma=False,
    )
```

profile of v0, /device:TPU:7, one launch (start us, length us, event | category | flops | bytes accessed | tf_op | source)
XLA Modules:
  0.0 329.6 jit_solution(282833793810252078)
XLA Ops:
  7.9 5.9 %collective-permute-start.1 = (f32[1,256]{1,0:T(1,128)S(1)}, f32[1,256]{1,0:T(1,128)S(1)}, u32[]{:S(2)}, u32[]{:S(2)}) collective-permute-start(f32[1,256]{1,0:T(1,128)S(1)} %get-tuple-element.94), channel_id=1, source_target_pairs={{32,0},{64,32},{96,64},{128,96},{160,128},{192,160},{224,192},{256... | collective-permute-start | bytes 3080 | tf_op jit(solution)/shard_map/ppermute | solution.py:17
  13.9 1.9 collective-permute-start
  15.8 1.2 fusion.99
  30.6 10.2 %collective-permute-start.2 = (f32[258,1]{1,0:T(8,128)S(1)}, f32[258,1]{1,0:T(8,128)S(1)}, u32[]{:S(2)}, u32[]{:S(2)}) collective-permute-start(f32[258,1]{1,0:T(8,128)S(1)} %get-tuple-element.28), channel_id=1, source_target_pairs={{2,0},{4,2},{6,4},{8,6},{10,8},{12,10},{14,12},{16,14},{18,16},{20... | collective-permute-start | bytes 3104 | tf_op jit(solution)/shard_map/ppermute | solution.py:17
  40.8 1.9 collective-permute-start.3
  42.7 5.9 %collective-permute-done.3 = f32[258,1]{1,0:T(8,128)S(1)} collective-permute-done((f32[258,1]{1,0:T(8,128)S(1)}, f32[258,1]{1,0:T(8,128)S(1)}, u32[]{:S(2)}, u32[]{:S(2)}) %collective-permute-start.3) | collective-permute-done | bytes 1064 | tf_op jit(solution)/shard_map/ppermute | solution.py:16
  48.8 6.5 %add_multiply_fusion.2 = (f32[256,256]{1,0:T(8,128)}, f32[256,256]{1,0:T(8,128)S(1)}, f32[256,256]{1,0:T(8,128)S(1)}) fusion(f32[256,256]{1,0:T(8,128)S(1)} %copy-done.3, f32[]{:T(128)} %bitcast.25, f32[]{:T(128)} %bitcast.24, f32[]{:T(128)} %bitcast.23, f32[]{:T(128)} %bitcast.22, f32[]{:T(128)} %bitcast.18, f32[]{:T(128)} %bitcast.17, f32[]{:T(128)} %bitcast.16, ...), kind=kLoop, calls=%fused_computation.65 | loop fusion | flops 4456448 | bytes 3145792 | tf_op jit(solution)/shard_map/add | solution.py:95
  55.2 6.5 %fusion.59 = f32[256,256]{1,0:T(8,128)} fusion(f32[256,256]{1,0:T(8,128)S(1)} %get-tuple-element.23, f32[256,256]{1,0:T(8,128)S(1)} %copy-done.3, f32[256,256]{1,0:T(8,128)S(1)} %get-tuple-element.22, f32[]{:T(128)} %bitcast.27, f32[]{:T(128)} %bitcast.25, f32[]{:T(128)} %bitcast.24, f32[]{:T(128)} %bitcast.23, f32[]{:T(128)} %bitcast.22, f32[]{:T(128)} %bitcast.20, ...), kind=kLoop, calls=%fused_computation.125 | loop fusion | flops 5439488 | bytes 2097232 | tf_op jit(solution)/shard_map/add | solution.py:93
  61.7 6.5 %multiply_add_fusion.7 = f32[256,256]{1,0:T(8,128)} fusion(f32[256,256]{1,0:T(8,128)S(1)} %get-tuple-element.22, f32[256,256]{1,0:T(8,128)S(1)} %copy-done.3, f32[256,256]{1,0:T(8,128)S(1)} %get-tuple-element.23, f32[]{:T(128)} %bitcast.31, f32[]{:T(128)} %bitcast.30, f32[]{:T(128)} %bitcast.29, f32[]{:T(128)} %bitcast.28, f32[]{:T(128)} %bitcast.25, ...), kind=kLoop, calls=%fused_computation.116 | loop fusion | flops 5439488 | bytes 2097232 | tf_op jit(solution)/shard_map/add | solution.py:94
  68.2 32.4 %all-reduce.11.cloned.1.call-done = (f32[256,256]{1,0:T(8,128)}, f32[256,256]{1,0:T(8,128)}, f32[256,256]{1,0:T(8,128)}) async-done(((f32[256,256]{1,0:T(8,128)}, f32[256,256]{1,0:T(8,128)}, f32[256,256]{1,0:T(8,128)}), (f32[256,256]{1,0:T(8,128)}, f32[256,256]{1,0:T(8,128)}, f32[256,256]{1,0:T(8,128)})) %all-reduce.11.cloned.1.call-update) | async-done | bytes 786448 | tf_op jit(solution)/shard_map/psum | solution.py:96
  100.7 1.0 multiply_add_fusion.6
  102.7 5.3 %collective-permute-start.7 = (f32[1,256]{1,0:T(1,128)S(1)}, f32[1,256]{1,0:T(1,128)S(1)}, u32[]{:S(2)}, u32[]{:S(2)}) collective-permute-start(f32[1,256]{1,0:T(1,128)S(1)} %get-tuple-element.78), channel_id=1, source_target_pairs={{32,0},{64,32},{96,64},{128,96},{160,128},{192,160},{224,192},{256... | collective-permute-start | bytes 3080 | tf_op jit(solution)/shard_map/ppermute | solution.py:17
  108.0 1.9 collective-permute-start.6
  110.2 5.0 %collective-permute-start.5 = (f32[256,1]{1,0:T(8,128)S(1)}, f32[256,1]{1,0:T(8,128)S(1)}, u32[]{:S(2)}, u32[]{:S(2)}) collective-permute-start(f32[256,1]{1,0:T(8,128)S(1)} %get-tuple-element.84), channel_id=1, source_target_pairs={{2,0},{4,2},{6,4},{8,6},{10,8},{12,10},{14,12},{16,14},{18,16},{20... | collective-permute-start | bytes 3080 | tf_op jit(solution)/shard_map/ppermute | solution.py:17
  115.2 1.9 collective-permute-start.4
  117.5 5.9 %collective-permute-done.4 = f32[256,1]{1,0:T(8,128)S(1)} collective-permute-done((f32[256,1]{1,0:T(8,128)S(1)}, f32[256,1]{1,0:T(8,128)S(1)}, u32[]{:S(2)}, u32[]{:S(2)}) %collective-permute-start.4) | collective-permute-done | bytes 1056 | tf_op jit(solution)/shard_map/ppermute | solution.py:16
  123.7 7.2 %collective-permute-start.9 = (f32[1,256]{1,0:T(1,128)S(1)}, f32[1,256]{1,0:T(1,128)S(1)}, u32[]{:S(2)}, u32[]{:S(2)}) collective-permute-start(f32[1,256]{1,0:T(1,128)S(1)} %get-tuple-element.72), channel_id=1, source_target_pairs={{32,0},{64,32},{96,64},{128,96},{160,128},{192,160},{224,192},{256... | collective-permute-start | bytes 3080 | tf_op jit(solution)/shard_map/ppermute | solution.py:17
  130.9 1.9 collective-permute-start.8
  133.0 5.9 %collective-permute-done.8 = f32[1,256]{1,0:T(1,128)S(1)} collective-permute-done((f32[1,256]{1,0:T(1,128)S(1)}, f32[1,256]{1,0:T(1,128)S(1)}, u32[]{:S(2)}, u32[]{:S(2)}) %collective-permute-start.8) | collective-permute-done | bytes 1056 | tf_op jit(solution)/shard_map/ppermute | solution.py:16
  139.0 1.9 collective-permute-start.10
  140.9 3.4 %collective-permute-start.11 = (f32[258,1]{1,0:T(8,128)S(1)}, f32[258,1]{1,0:T(8,128)S(1)}, u32[]{:S(2)}, u32[]{:S(2)}) collective-permute-start(f32[258,1]{1,0:T(8,128)S(1)} %get-tuple-element.27), channel_id=1, source_target_pairs={{0,2},{2,4},{4,6},{6,8},{8,10},{10,12},{12,14},{14,16},{16,18},{18... | collective-permute-start | bytes 3104 | tf_op jit(solution)/shard_map/ppermute | solution.py:16
  144.7 4.0 %collective-permute-done.11 = f32[258,1]{1,0:T(8,128)S(1)} collective-permute-done((f32[258,1]{1,0:T(8,128)S(1)}, f32[258,1]{1,0:T(8,128)S(1)}, u32[]{:S(2)}, u32[]{:S(2)}) %collective-permute-start.11) | collective-permute-done | bytes 1064 | tf_op jit(solution)/shard_map/ppermute | solution.py:16
  148.9 6.5 %add_multiply_fusion.1 = (f32[256,256]{1,0:T(8,128)}, f32[256,256]{1,0:T(8,128)S(1)}, f32[256,256]{1,0:T(8,128)S(1)}, f32[256,256]{1,0:T(8,128)S(1)}) fusion(f32[]{:T(128)} %bitcast.25, f32[]{:T(128)} %bitcast.24, f32[]{:T(128)} %bitcast.23, f32[]{:T(128)} %bitcast.22, f32[]{:T(128)} %bitcast.18, f32[]{:T(128)} %bitcast.17, f32[]{:T(128)} %bitcast.16, ...), kind=kLoop, calls=%fused_computation.64 | loop fusion | flops 4587520 | bytes 3670080 | tf_op jit(solution)/shard_map/add | solution.py:95
  155.4 6.5 %fusion.44 = f32[256,256]{1,0:T(8,128)} fusion(f32[256,256]{1,0:T(8,128)S(1)} %get-tuple-element.20, f32[256,256]{1,0:T(8,128)S(1)} %get-tuple-element.19, f32[256,256]{1,0:T(8,128)S(1)} %get-tuple-element.18, f32[]{:T(128)} %bitcast.27, f32[]{:T(128)} %bitcast.25, f32[]{:T(128)} %bitcast.24, f32[]{:T(128)} %bitcast.23, f32[]{:T(128)} %bitcast.22, ...), kind=kLoop, calls=%fused_computation.101 | loop fusion | flops 5439488 | bytes 2097232 | tf_op jit(solution)/shard_map/add | solution.py:93
  161.8 6.5 %multiply_add_fusion.4 = f32[256,256]{1,0:T(8,128)} fusion(f32[256,256]{1,0:T(8,128)S(1)} %get-tuple-element.18, f32[256,256]{1,0:T(8,128)S(1)} %get-tuple-element.19, f32[256,256]{1,0:T(8,128)S(1)} %get-tuple-element.20, f32[]{:T(128)} %bitcast.31, f32[]{:T(128)} %bitcast.30, f32[]{:T(128)} %bitcast.29, f32[]{:T(128)} %bitcast.28, f32[]{:T(128)} %bitcast.25, ...), kind=kLoop, calls=%fused_computation.92 | loop fusion | flops 5439488 | bytes 2097232 | tf_op jit(solution)/shard_map/add | solution.py:94
  168.4 31.1 %all-reduce.9.cloned.1.call-done = (f32[256,256]{1,0:T(8,128)}, f32[256,256]{1,0:T(8,128)}, f32[256,256]{1,0:T(8,128)}) async-done(((f32[256,256]{1,0:T(8,128)}, f32[256,256]{1,0:T(8,128)}, f32[256,256]{1,0:T(8,128)}), (f32[256,256]{1,0:T(8,128)}, f32[256,256]{1,0:T(8,128)}, f32[256,256]{1,0:T(8,128)})) %all-reduce.9.cloned.1.call-update) | async-done | bytes 786448 | tf_op jit(solution)/shard_map/psum | solution.py:96
  199.5 1.0 multiply_add_fusion.3
  201.5 5.3 %collective-permute-start.15 = (f32[1,256]{1,0:T(1,128)S(1)}, f32[1,256]{1,0:T(1,128)S(1)}, u32[]{:S(2)}, u32[]{:S(2)}) collective-permute-start(f32[1,256]{1,0:T(1,128)S(1)} %get-tuple-element.56), channel_id=1, source_target_pairs={{32,0},{64,32},{96,64},{128,96},{160,128},{192,160},{224,192},{256... | collective-permute-start | bytes 3080 | tf_op jit(solution)/shard_map/ppermute | solution.py:17
  206.9 1.9 collective-permute-start.14
  209.0 5.0 %collective-permute-start.13 = (f32[256,1]{1,0:T(8,128)S(1)}, f32[256,1]{1,0:T(8,128)S(1)}, u32[]{:S(2)}, u32[]{:S(2)}) collective-permute-start(f32[256,1]{1,0:T(8,128)S(1)} %get-tuple-element.62), channel_id=1, source_target_pairs={{2,0},{4,2},{6,4},{8,6},{10,8},{12,10},{14,12},{16,14},{18,16},{20... | collective-permute-start | bytes 3080 | tf_op jit(solution)/shard_map/ppermute | solution.py:17
  214.0 1.9 collective-permute-start.12
  216.4 5.9 %collective-permute-done.12 = f32[256,1]{1,0:T(8,128)S(1)} collective-permute-done((f32[256,1]{1,0:T(8,128)S(1)}, f32[256,1]{1,0:T(8,128)S(1)}, u32[]{:S(2)}, u32[]{:S(2)}) %collective-permute-start.12) | collective-permute-done | bytes 1056 | tf_op jit(solution)/shard_map/ppermute | solution.py:16
  222.6 7.2 %collective-permute-start.17 = (f32[1,256]{1,0:T(1,128)S(1)}, f32[1,256]{1,0:T(1,128)S(1)}, u32[]{:S(2)}, u32[]{:S(2)}) collective-permute-start(f32[1,256]{1,0:T(1,128)S(1)} %get-tuple-element.50), channel_id=1, source_target_pairs={{32,0},{64,32},{96,64},{128,96},{160,128},{192,160},{224,192},{256... | collective-permute-start | bytes 3080 | tf_op jit(solution)/shard_map/ppermute | solution.py:17
  229.8 1.9 collective-permute-start.16
  231.9 5.9 %collective-permute-done.16 = f32[1,256]{1,0:T(1,128)S(1)} collective-permute-done((f32[1,256]{1,0:T(1,128)S(1)}, f32[1,256]{1,0:T(1,128)S(1)}, u32[]{:S(2)}, u32[]{:S(2)}) %collective-permute-start.16) | collective-permute-done | bytes 1056 | tf_op jit(solution)/shard_map/ppermute | solution.py:16
  237.8 1.9 collective-permute-start.18
  239.8 3.4 %collective-permute-start.19 = (f32[258,1]{1,0:T(8,128)S(1)}, f32[258,1]{1,0:T(8,128)S(1)}, u32[]{:S(2)}, u32[]{:S(2)}) collective-permute-start(f32[258,1]{1,0:T(8,128)S(1)} %get-tuple-element.25), channel_id=1, source_target_pairs={{0,2},{2,4},{4,6},{6,8},{8,10},{10,12},{12,14},{14,16},{16,18},{18... | collective-permute-start | bytes 3104 | tf_op jit(solution)/shard_map/ppermute | solution.py:16
  243.6 4.0 %collective-permute-done.19 = f32[258,1]{1,0:T(8,128)S(1)} collective-permute-done((f32[258,1]{1,0:T(8,128)S(1)}, f32[258,1]{1,0:T(8,128)S(1)}, u32[]{:S(2)}, u32[]{:S(2)}) %collective-permute-start.19) | collective-permute-done | bytes 1064 | tf_op jit(solution)/shard_map/ppermute | solution.py:16
  247.7 6.5 %add_multiply_fusion = (f32[256,256]{1,0:T(8,128)}, f32[256,256]{1,0:T(8,128)S(1)}, f32[256,256]{1,0:T(8,128)S(1)}, f32[256,256]{1,0:T(8,128)S(1)}) fusion(f32[]{:T(128)} %bitcast.25, f32[]{:T(128)} %bitcast.24, f32[]{:T(128)} %bitcast.23, f32[]{:T(128)} %bitcast.22, f32[]{:T(128)} %bitcast.18, f32[]{:T(128)} %bitcast.17, f32[]{:T(128)} %bitcast.16, ...), kind=kLoop, calls=%fused_computation.63 | loop fusion | flops 4587520 | bytes 3670080 | tf_op jit(solution)/shard_map/add | solution.py:95
  254.2 6.5 %fusion.29 = f32[256,256]{1,0:T(8,128)} fusion(f32[256,256]{1,0:T(8,128)S(1)} %get-tuple-element.16, f32[256,256]{1,0:T(8,128)S(1)} %get-tuple-element.15, f32[256,256]{1,0:T(8,128)S(1)} %get-tuple-element.14, f32[]{:T(128)} %bitcast.27, f32[]{:T(128)} %bitcast.25, f32[]{:T(128)} %bitcast.24, f32[]{:T(128)} %bitcast.23, f32[]{:T(128)} %bitcast.22, ...), kind=kLoop, calls=%fused_computation.77 | loop fusion | flops 5439488 | bytes 2097232 | tf_op jit(solution)/shard_map/add | solution.py:93
  260.7 6.5 %multiply_add_fusion.1 = f32[256,256]{1,0:T(8,128)} fusion(f32[256,256]{1,0:T(8,128)S(1)} %get-tuple-element.14, f32[256,256]{1,0:T(8,128)S(1)} %get-tuple-element.15, f32[256,256]{1,0:T(8,128)S(1)} %get-tuple-element.16, f32[]{:T(128)} %bitcast.31, f32[]{:T(128)} %bitcast.30, f32[]{:T(128)} %bitcast.29, f32[]{:T(128)} %bitcast.28, f32[]{:T(128)} %bitcast.25, ...), kind=kLoop, calls=%fused_computation.68 | loop fusion | flops 5439488 | bytes 2097232 | tf_op jit(solution)/shard_map/add | solution.py:94
  267.2 31.2 %all-reduce.7.cloned.1.call-done = (f32[256,256]{1,0:T(8,128)}, f32[256,256]{1,0:T(8,128)}, f32[256,256]{1,0:T(8,128)}) async-done(((f32[256,256]{1,0:T(8,128)}, f32[256,256]{1,0:T(8,128)}, f32[256,256]{1,0:T(8,128)}), (f32[256,256]{1,0:T(8,128)}, f32[256,256]{1,0:T(8,128)}, f32[256,256]{1,0:T(8,128)})) %all-reduce.7.cloned.1.call-update) | async-done | bytes 786448 | tf_op jit(solution)/shard_map/psum | solution.py:96
  298.4 1.0 multiply_add_fusion
  301.4 5.3 %collective-permute-start.23 = (f32[1,256]{1,0:T(1,128)S(1)}, f32[1,256]{1,0:T(1,128)S(1)}, u32[]{:S(2)}, u32[]{:S(2)}) collective-permute-start(f32[1,256]{1,0:T(1,128)S(1)} %get-tuple-element.34), channel_id=1, source_target_pairs={{32,0},{64,32},{96,64},{128,96},{160,128},{192,160},{224,192},{256... | collective-permute-start | bytes 3080 | tf_op jit(solution)/shard_map/ppermute | solution.py:17
  306.7 1.9 collective-permute-start.22
  308.9 5.0 %collective-permute-start.21 = (f32[256,1]{1,0:T(8,128)S(1)}, f32[256,1]{1,0:T(8,128)S(1)}, u32[]{:S(2)}, u32[]{:S(2)}) collective-permute-start(f32[256,1]{1,0:T(8,128)S(1)} %get-tuple-element.40), channel_id=1, source_target_pairs={{2,0},{4,2},{6,4},{8,6},{10,8},{12,10},{14,12},{16,14},{18,16},{20... | collective-permute-start | bytes 3080 | tf_op jit(solution)/shard_map/ppermute | solution.py:17
  313.9 1.9 collective-permute-start.20
  316.2 5.9 %collective-permute-done.20 = f32[256,1]{1,0:T(8,128)S(1)} collective-permute-done((f32[256,1]{1,0:T(8,128)S(1)}, f32[256,1]{1,0:T(8,128)S(1)}, u32[]{:S(2)}, u32[]{:S(2)}) %collective-permute-start.20) | collective-permute-done | bytes 1056 | tf_op jit(solution)/shard_map/ppermute | solution.py:16
  (104 shorter events, 13.2 us)
Async XLA Ops:
  7.2 93.5 %all-reduce.11.cloned.1.call-start = ((), (), s32[]{:S(2)}) async-start(), calls=%async_computation.2 | async-start | bytes 1572864 | tf_op jit(solution)/shard_map/psum | solution.py:96
  7.9 22.5 %collective-permute-start.1 = (f32[1,256]{1,0:T(1,128)S(1)}, f32[1,256]{1,0:T(1,128)S(1)}, u32[]{:S(2)}, u32[]{:S(2)}) collective-permute-start(f32[1,256]{1,0:T(1,128)S(1)} %get-tuple-element.94), channel_id=1, source_target_pairs={{32,0},{64,32},{96,64},{128,96},{160,128},{192,160},{224,192},{256... | collective-permute-start | bytes 3080 | tf_op jit(solution)/shard_map/ppermute | solution.py:17
  13.9 16.6 %collective-permute-start = (f32[1,256]{1,0:T(1,128)S(1)}, f32[1,256]{1,0:T(1,128)S(1)}, u32[]{:S(2)}, u32[]{:S(2)}) collective-permute-start(f32[1,256]{1,0:T(1,128)S(1)} %get-tuple-element.95), channel_id=1, source_target_pairs={{0,32},{32,64},{64,96},{96,128},{128,160},{160,192},{192,224},{224... | collective-permute-start | bytes 3080 | tf_op jit(solution)/shard_map/ppermute | solution.py:16
  15.8 1.2 copy-start.2
  17.1 0.7 copy-start.10
  17.1 0.7 copy-start.11
  17.1 0.7 copy-start.12
  18.0 0.7 copy-start.13
  18.0 0.7 copy-start.14
  30.5 18.3 %copy-start.1 = (bf16[4,256,256]{2,1,0:T(8,128)(2,1)S(1)}, bf16[4,256,256]{2,1,0:T(8,128)(2,1)}, u32[]{:S(2)}) copy-start(bf16[4,256,256]{2,1,0:T(8,128)(2,1)} %param.12) | copy-start | bytes 1572868
  30.6 18.2 %copy-start = (bf16[4,256,256]{2,1,0:T(8,128)(2,1)S(1)}, bf16[4,256,256]{2,1,0:T(8,128)(2,1)}, u32[]{:S(2)}) copy-start(bf16[4,256,256]{2,1,0:T(8,128)(2,1)} %param.11) | copy-start | bytes 1572868
  30.6 12.1 %collective-permute-start.2 = (f32[258,1]{1,0:T(8,128)S(1)}, f32[258,1]{1,0:T(8,128)S(1)}, u32[]{:S(2)}, u32[]{:S(2)}) collective-permute-start(f32[258,1]{1,0:T(8,128)S(1)} %get-tuple-element.28), channel_id=1, source_target_pairs={{2,0},{4,2},{6,4},{8,6},{10,8},{12,10},{14,12},{16,14},{18,16},{20... | collective-permute-start | bytes 3104 | tf_op jit(solution)/shard_map/ppermute | solution.py:17
  40.8 7.9 %collective-permute-start.3 = (f32[258,1]{1,0:T(8,128)S(1)}, f32[258,1]{1,0:T(8,128)S(1)}, u32[]{:S(2)}, u32[]{:S(2)}) collective-permute-start(f32[258,1]{1,0:T(8,128)S(1)} %get-tuple-element.29), channel_id=1, source_target_pairs={{0,2},{2,4},{4,6},{6,8},{8,10},{10,12},{12,14},{14,16},{16,18},{18... | collective-permute-start | bytes 3104 | tf_op jit(solution)/shard_map/ppermute | solution.py:16
  42.7 6.1 %copy-start.3 = (f32[256,256]{1,0:T(8,128)S(1)}, f32[256,256]{1,0:T(8,128)}, u32[]{:S(2)}) copy-start(f32[256,256]{1,0:T(8,128)} %param.10) | copy-start | bytes 786436
  68.2 131.3 %all-reduce.9.cloned.1.call-start = ((), (), s32[]{:S(2)}) async-start(), calls=%async_computation.1 | async-start | bytes 1572864 | tf_op jit(solution)/shard_map/psum | solution.py:96
  101.7 1.0 copy-start.7
  102.7 14.4 %collective-permute-start.7 = (f32[1,256]{1,0:T(1,128)S(1)}, f32[1,256]{1,0:T(1,128)S(1)}, u32[]{:S(2)}, u32[]{:S(2)}) collective-permute-start(f32[1,256]{1,0:T(1,128)S(1)} %get-tuple-element.78), channel_id=1, source_target_pairs={{32,0},{64,32},{96,64},{128,96},{160,128},{192,160},{224,192},{256... | collective-permute-start | bytes 3080 | tf_op jit(solution)/shard_map/ppermute | solution.py:17
  108.0 9.1 %collective-permute-start.6 = (f32[1,256]{1,0:T(1,128)S(1)}, f32[1,256]{1,0:T(1,128)S(1)}, u32[]{:S(2)}, u32[]{:S(2)}) collective-permute-start(f32[1,256]{1,0:T(1,128)S(1)} %get-tuple-element.79), channel_id=1, source_target_pairs={{0,32},{32,64},{64,96},{96,128},{128,160},{160,192},{192,224},{224... | collective-permute-start | bytes 3080 | tf_op jit(solution)/shard_map/ppermute | solution.py:16
  110.2 7.3 %collective-permute-start.5 = (f32[256,1]{1,0:T(8,128)S(1)}, f32[256,1]{1,0:T(8,128)S(1)}, u32[]{:S(2)}, u32[]{:S(2)}) collective-permute-start(f32[256,1]{1,0:T(8,128)S(1)} %get-tuple-element.84), channel_id=1, source_target_pairs={{2,0},{4,2},{6,4},{8,6},{10,8},{12,10},{14,12},{16,14},{18,16},{20... | collective-permute-start | bytes 3080 | tf_op jit(solution)/shard_map/ppermute | solution.py:17
  115.2 8.2 %collective-permute-start.4 = (f32[256,1]{1,0:T(8,128)S(1)}, f32[256,1]{1,0:T(8,128)S(1)}, u32[]{:S(2)}, u32[]{:S(2)}) collective-permute-start(f32[256,1]{1,0:T(8,128)S(1)} %get-tuple-element.85), channel_id=1, source_target_pairs={{0,2},{2,4},{4,6},{6,8},{8,10},{10,12},{12,14},{14,16},{16,18},{18... | collective-permute-start | bytes 3080 | tf_op jit(solution)/shard_map/ppermute | solution.py:16
  123.7 9.2 %collective-permute-start.9 = (f32[1,256]{1,0:T(1,128)S(1)}, f32[1,256]{1,0:T(1,128)S(1)}, u32[]{:S(2)}, u32[]{:S(2)}) collective-permute-start(f32[1,256]{1,0:T(1,128)S(1)} %get-tuple-element.72), channel_id=1, source_target_pairs={{32,0},{64,32},{96,64},{128,96},{160,128},{192,160},{224,192},{256... | collective-permute-start | bytes 3080 | tf_op jit(solution)/shard_map/ppermute | solution.py:17
  130.9 7.9 %collective-permute-start.8 = (f32[1,256]{1,0:T(1,128)S(1)}, f32[1,256]{1,0:T(1,128)S(1)}, u32[]{:S(2)}, u32[]{:S(2)}) collective-permute-start(f32[1,256]{1,0:T(1,128)S(1)} %get-tuple-element.73), channel_id=1, source_target_pairs={{0,32},{32,64},{64,96},{96,128},{128,160},{160,192},{192,224},{224... | collective-permute-start | bytes 3080 | tf_op jit(solution)/shard_map/ppermute | solution.py:16
  139.0 5.8 %collective-permute-start.10 = (f32[258,1]{1,0:T(8,128)S(1)}, f32[258,1]{1,0:T(8,128)S(1)}, u32[]{:S(2)}, u32[]{:S(2)}) collective-permute-start(f32[258,1]{1,0:T(8,128)S(1)} %get-tuple-element.26), channel_id=1, source_target_pairs={{2,0},{4,2},{6,4},{8,6},{10,8},{12,10},{14,12},{16,14},{18,16},{20... | collective-permute-start | bytes 3104 | tf_op jit(solution)/shard_map/ppermute | solution.py:17
  140.9 7.9 %collective-permute-start.11 = (f32[258,1]{1,0:T(8,128)S(1)}, f32[258,1]{1,0:T(8,128)S(1)}, u32[]{:S(2)}, u32[]{:S(2)}) collective-permute-start(f32[258,1]{1,0:T(8,128)S(1)} %get-tuple-element.27), channel_id=1, source_target_pairs={{0,2},{2,4},{4,6},{6,8},{8,10},{10,12},{12,14},{14,16},{16,18},{18... | collective-permute-start | bytes 3104 | tf_op jit(solution)/shard_map/ppermute | solution.py:16
  144.3 4.6 %copy-start.5 = (f32[256,256]{1,0:T(8,128)S(1)}, f32[256,256]{1,0:T(8,128)}, u32[]{:S(2)}) copy-start(f32[256,256]{1,0:T(8,128)} %get-tuple-element.12) | copy-start | bytes 786436
  168.3 130.0 %all-reduce.7.cloned.1.call-start = ((), (), s32[]{:S(2)}) async-start(), calls=%async_computation | async-start | bytes 1572864 | tf_op jit(solution)/shard_map/psum | solution.py:96
  200.5 1.0 copy-start.8
  201.5 14.4 %collective-permute-start.15 = (f32[1,256]{1,0:T(1,128)S(1)}, f32[1,256]{1,0:T(1,128)S(1)}, u32[]{:S(2)}, u32[]{:S(2)}) collective-permute-start(f32[1,256]{1,0:T(1,128)S(1)} %get-tuple-element.56), channel_id=1, source_target_pairs={{32,0},{64,32},{96,64},{128,96},{160,128},{192,160},{224,192},{256... | collective-permute-start | bytes 3080 | tf_op jit(solution)/shard_map/ppermute | solution.py:17
  206.9 9.1 %collective-permute-start.14 = (f32[1,256]{1,0:T(1,128)S(1)}, f32[1,256]{1,0:T(1,128)S(1)}, u32[]{:S(2)}, u32[]{:S(2)}) collective-permute-start(f32[1,256]{1,0:T(1,128)S(1)} %get-tuple-element.57), channel_id=1, source_target_pairs={{0,32},{32,64},{64,96},{96,128},{128,160},{160,192},{192,224},{224... | collective-permute-start | bytes 3080 | tf_op jit(solution)/shard_map/ppermute | solution.py:16
  209.0 7.3 %collective-permute-start.13 = (f32[256,1]{1,0:T(8,128)S(1)}, f32[256,1]{1,0:T(8,128)S(1)}, u32[]{:S(2)}, u32[]{:S(2)}) collective-permute-start(f32[256,1]{1,0:T(8,128)S(1)} %get-tuple-element.62), channel_id=1, source_target_pairs={{2,0},{4,2},{6,4},{8,6},{10,8},{12,10},{14,12},{16,14},{18,16},{20... | collective-permute-start | bytes 3080 | tf_op jit(solution)/shard_map/ppermute | solution.py:17
  214.0 8.2 %collective-permute-start.12 = (f32[256,1]{1,0:T(8,128)S(1)}, f32[256,1]{1,0:T(8,128)S(1)}, u32[]{:S(2)}, u32[]{:S(2)}) collective-permute-start(f32[256,1]{1,0:T(8,128)S(1)} %get-tuple-element.63), channel_id=1, source_target_pairs={{0,2},{2,4},{4,6},{6,8},{8,10},{10,12},{12,14},{14,16},{16,18},{18... | collective-permute-start | bytes 3080 | tf_op jit(solution)/shard_map/ppermute | solution.py:16
  222.6 9.2 %collective-permute-start.17 = (f32[1,256]{1,0:T(1,128)S(1)}, f32[1,256]{1,0:T(1,128)S(1)}, u32[]{:S(2)}, u32[]{:S(2)}) collective-permute-start(f32[1,256]{1,0:T(1,128)S(1)} %get-tuple-element.50), channel_id=1, source_target_pairs={{32,0},{64,32},{96,64},{128,96},{160,128},{192,160},{224,192},{256... | collective-permute-start | bytes 3080 | tf_op jit(solution)/shard_map/ppermute | solution.py:17
  229.8 7.9 %collective-permute-start.16 = (f32[1,256]{1,0:T(1,128)S(1)}, f32[1,256]{1,0:T(1,128)S(1)}, u32[]{:S(2)}, u32[]{:S(2)}) collective-permute-start(f32[1,256]{1,0:T(1,128)S(1)} %get-tuple-element.51), channel_id=1, source_target_pairs={{0,32},{32,64},{64,96},{96,128},{128,160},{160,192},{192,224},{224... | collective-permute-start | bytes 3080 | tf_op jit(solution)/shard_map/ppermute | solution.py:16
  237.8 5.8 %collective-permute-start.18 = (f32[258,1]{1,0:T(8,128)S(1)}, f32[258,1]{1,0:T(8,128)S(1)}, u32[]{:S(2)}, u32[]{:S(2)}) collective-permute-start(f32[258,1]{1,0:T(8,128)S(1)} %get-tuple-element.24), channel_id=1, source_target_pairs={{2,0},{4,2},{6,4},{8,6},{10,8},{12,10},{14,12},{16,14},{18,16},{20... | collective-permute-start | bytes 3104 | tf_op jit(solution)/shard_map/ppermute | solution.py:17
  239.8 7.9 %collective-permute-start.19 = (f32[258,1]{1,0:T(8,128)S(1)}, f32[258,1]{1,0:T(8,128)S(1)}, u32[]{:S(2)}, u32[]{:S(2)}) collective-permute-start(f32[258,1]{1,0:T(8,128)S(1)} %get-tuple-element.25), channel_id=1, source_target_pairs={{0,2},{2,4},{4,6},{6,8},{8,10},{10,12},{12,14},{14,16},{16,18},{18... | collective-permute-start | bytes 3104 | tf_op jit(solution)/shard_map/ppermute | solution.py:16
  243.1 4.6 %copy-start.4 = (f32[256,256]{1,0:T(8,128)S(1)}, f32[256,256]{1,0:T(8,128)}, u32[]{:S(2)}) copy-start(f32[256,256]{1,0:T(8,128)} %get-tuple-element.9) | copy-start | bytes 786436
  299.4 1.0 copy-start.9
  300.3 1.0 copy-start.6
  301.4 14.4 %collective-permute-start.23 = (f32[1,256]{1,0:T(1,128)S(1)}, f32[1,256]{1,0:T(1,128)S(1)}, u32[]{:S(2)}, u32[]{:S(2)}) collective-permute-start(f32[1,256]{1,0:T(1,128)S(1)} %get-tuple-element.34), channel_id=1, source_target_pairs={{32,0},{64,32},{96,64},{128,96},{160,128},{192,160},{224,192},{256... | collective-permute-start | bytes 3080 | tf_op jit(solution)/shard_map/ppermute | solution.py:17
  306.7 9.1 %collective-permute-start.22 = (f32[1,256]{1,0:T(1,128)S(1)}, f32[1,256]{1,0:T(1,128)S(1)}, u32[]{:S(2)}, u32[]{:S(2)}) collective-permute-start(f32[1,256]{1,0:T(1,128)S(1)} %get-tuple-element.35), channel_id=1, source_target_pairs={{0,32},{32,64},{64,96},{96,128},{128,160},{160,192},{192,224},{224... | collective-permute-start | bytes 3080 | tf_op jit(solution)/shard_map/ppermute | solution.py:16
  308.9 7.3 %collective-permute-start.21 = (f32[256,1]{1,0:T(8,128)S(1)}, f32[256,1]{1,0:T(8,128)S(1)}, u32[]{:S(2)}, u32[]{:S(2)}) collective-permute-start(f32[256,1]{1,0:T(8,128)S(1)} %get-tuple-element.40), channel_id=1, source_target_pairs={{2,0},{4,2},{6,4},{8,6},{10,8},{12,10},{14,12},{16,14},{18,16},{20... | collective-permute-start | bytes 3080 | tf_op jit(solution)/shard_map/ppermute | solution.py:17
  313.9 8.2 %collective-permute-start.20 = (f32[256,1]{1,0:T(8,128)S(1)}, f32[256,1]{1,0:T(8,128)S(1)}, u32[]{:S(2)}, u32[]{:S(2)}) collective-permute-start(f32[256,1]{1,0:T(8,128)S(1)} %get-tuple-element.41), channel_id=1, source_target_pairs={{0,2},{2,4},{4,6},{6,8},{8,10},{10,12},{12,14},{14,16},{16,18},{18... | collective-permute-start | bytes 3080 | tf_op jit(solution)/shard_map/ppermute | solution.py:16
Sparse Core Ops, SparseCore 0:
  68.3 32.3 all-reduce.10
  168.5 31.0 all-reduce.8
  267.3 31.0 all-reduce.6
where the time goes:
time: 334 us; the launch traced here: 330 us
  waiting for transfers between devices  140 us (42%)
  starting transfers between devices  91.3 us (27%)
  other arithmetic  64.4 us (19%)
  between operations  24.7 us (7%)
  local copies, waits for them, and re-layouts  9.07 us (3%)
    psum x3, waiting for transfers between devices, shards(): grad_p, grad_q, grad_a = lax.psum((grad_p, grad_q, grad_a), 'img')  94.8 us
    ppermute x12, starting transfers between devices, with_halo(): after = lax.ppermute(first, axis, down)  65.2 us
    ppermute x12, waiting for transfers between devices, with_halo(): before = lax.ppermute(last, axis, up)  43.4 us
    ppermute x12, starting transfers between devices, with_halo(): before = lax.ppermute(last, axis, up)  25.9 us
    add x3, other arithmetic, shards(): grad_a = grad_a + resid * shade * scale  19.4 us
    add x3, other arithmetic, shards(): grad_q + resid * albedo_now * (-sun_y[k] * scale - shade * slope_q * cubed)  19.4 us
    add x3, other arithmetic, shards(): grad_p + resid * albedo_now * (-sun_x[k] * scale - shade * slope_p * cubed)  19.4 us
  transfers between devices with their start and end apart: 27, of which 16 were waited for; matrix products, arithmetic and copies ran while one was open for 1% of the time, Pallas kernels for 0%

commit v1 on v0

v1 whole, which is shorter than its diff:
```python
import functools

import jax
import jax.numpy as jnp
from jax import lax
from jax.experimental import pallas as pl
from jax.experimental.pallas import tpu as pltpu
from jax.sharding import PartitionSpec as P

ITERS = 3
AXES = ("gy", "gx", "img")
LANES = 128
ROW = 8
MOMENTS = 9
PLANES = 2 + MOMENTS
WIDTHS = (6,) + (5,) * (PLANES - 1)
STARTS = tuple(6 if k == 0 else 17 + 10 * (k - 1) for k in range(PLANES))
F32 = jnp.float32


def lane_ids(rows):
    return lax.broadcasted_iota(jnp.int32, (rows, LANES), 1)


def east_lanes(lane):
    hit = lane < 0
    for start, width in zip(STARTS, WIDTHS):
        hit = hit | ((lane >= start) & (lane < start + width))
    return hit


def moments_kernel(
    sun_index, expo_index, azimuth, elevation, exposure, height, albedo, images, weights, sums, edges
):
    count, rows, _ = images.shape
    line = lax.broadcasted_iota(jnp.int32, (ROW, LANES), 0)
    azim = jnp.zeros((ROW, LANES), F32)
    elev = jnp.zeros((ROW, LANES), F32)
    gain = jnp.zeros((ROW, LANES), F32)
    for k in range(count):
        azim = jnp.where(line == k, azimuth[sun_index[k]], azim)
        elev = jnp.where(line == k, elevation[sun_index[k]], elev)
        gain = jnp.where(line == k, exposure[expo_index[k]], gain)
    flat = jnp.cos(elev)
    sx = gain * flat * jnp.cos(azim)
    sy = gain * flat * jnp.sin(azim)
    sz = gain * jnp.sin(elev)
    pairs = (sx * sx, sx * sy, sx * sz, sy * sy, sy * sz, sz * sz)
    singles = (sx, sy, sz)
    step = 16
    lane = lane_ids(step)
    masks = [(lane >= s - w) & (lane < s + w) for s, w in zip(STARTS, WIDTHS)]

    def block(i, carry):
        at = pl.ds(pl.multiple_of(i * step, step), step)
        acc = [None] * MOMENTS
        for k in range(count):
            w = weights[k, at, :].astype(F32)
            u = w * images[k, at, :].astype(F32)
            for m, table in enumerate(pairs):
                term = w * table[k : k + 1, :1]
                acc[m] = term if k == 0 else acc[m] + term
            for m, table in enumerate(singles):
                term = u * table[k : k + 1, :1]
                acc[6 + m] = term if k == 0 else acc[6 + m] + term
        for m in range(MOMENTS):
            sums[m, at, :] = acc[m]
        packed = jnp.zeros((step, LANES), F32)
        planes = [0.5 * height[at, :], 0.5 * albedo[at, :]] + acc
        for start, mask, plane in zip(STARTS, masks, planes):
            ends = jnp.where(lane < LANES // 2, plane[:, :LANES], plane[:, -LANES:])
            packed = jnp.where(mask, pltpu.roll(ends, start, 1), packed)
        edges[at, :] = packed
        return carry

    lax.fori_loop(0, rows // step, block, 0)


def rows_kernel(height, albedo, mine, theirs, sides, out):
    rows = height.shape[0]
    start = pl.multiple_of(lax.axis_index("img") * (rows - ROW), ROW)
    at = pl.ds(start, ROW)
    out[pl.ds(0, ROW), :] = height[at, :]
    out[pl.ds(ROW, ROW), :] = albedo[at, :]
    for m in range(MOMENTS):
        out[pl.ds((2 + m) * ROW, ROW), :] = mine[m, at, :] + theirs[m, at, :]
    both = jnp.where(east_lanes(lane_ids(ROW)), sides[1, at, :], sides[0, at, :])
    out[pl.ds(PLANES * ROW, ROW), :] = jnp.concatenate([both, both], axis=1)


def steps_kernel(rates, height, albedo, mine, theirs, sides, ends, out_h, out_a, hs, al, mo, gps, gqs):
    rows, cols = height.shape
    first_y = lax.axis_index("gy") == 0
    last_y = lax.axis_index("gy") == lax.axis_size("gy") - 1
    first_x = lax.axis_index("gx") == 0
    last_x = lax.axis_index("gx") == lax.axis_size("gx") - 1
    rate_h, rate_a = rates
    top = 2 * ROW
    bottom = top + rows
    step = 16

    def plane(k):
        return hs if k == 0 else al if k == 1 else mo.at[k - 2]

    east = east_lanes(lane_ids(step))

    def fill(i, carry):
        src = pl.ds(pl.multiple_of(i * step, step), step)
        dst = pl.ds(pl.multiple_of(i * step + top, ROW), step)
        both = jnp.where(east, sides[1, src, :], sides[0, src, :])
        for k in range(PLANES):
            if k == 0:
                body = height[src, :]
            elif k == 1:
                body = albedo[src, :]
            else:
                body = mine[k - 2, src, :] + theirs[k - 2, src, :]
            ref = plane(k)
            ref[0, dst, :] = body[:, :LANES]
            ref[1, dst, :] = body[:, LANES:]
            ref[2, dst, :] = pltpu.roll(both, LANES - STARTS[k], 1)
        return carry

    lax.fori_loop(0, rows // step, fill, 0)
    for side, row in ((0, top - ROW), (1, bottom)):
        both = ends[side, pl.ds(PLANES * ROW, ROW), :LANES]
        for k in range(PLANES):
            ref = plane(k)
            body = ends[side, pl.ds(k * ROW, ROW), :]
            ref[0, pl.ds(row, ROW), :] = body[:, :LANES]
            ref[1, pl.ds(row, ROW), :] = body[:, LANES:]
            ref[2, pl.ds(row, ROW), :] = pltpu.roll(both, LANES - STARTS[k], 1)

    lane = lane_ids(ROW)
    head = lane == 0
    tail = lane == LANES - 1
    wall_w = head & first_x
    wall_e = tail & last_x

    def beside(blocks, sign):
        fore = [pltpu.roll(b, LANES - 1, 1) for b in blocks]
        back = [pltpu.roll(b, 1, 1) for b in blocks]
        easts = [jnp.where(tail, fore[(t + 1) % 3], fore[t]) for t in range(3)]
        wests = [jnp.where(head, back[(t + 2) % 3], back[t]) for t in range(3)]
        easts[1] = jnp.where(wall_e, sign * blocks[1], easts[1])
        wests[0] = jnp.where(wall_w, sign * blocks[0], wests[0])
        return easts, wests

    def borders(ref, sign):
        @pl.when(first_y)
        def _():
            ref[:, pl.ds(top - 1, 1), :] = sign * ref[:, pl.ds(top, 1), :]

        @pl.when(last_y)
        def _():
            ref[:, pl.ds(bottom, 1), :] = sign * ref[:, pl.ds(bottom - 1, 1), :]

    def slopes(i, carry):
        base = pl.multiple_of(i * ROW, ROW)
        at = pl.ds(pl.multiple_of(base + ROW, ROW), ROW)
        tall = [hs[t, pl.ds(base, 3 * ROW), :] for t in range(3)]
        easts, wests = beside([v[ROW : 2 * ROW] for v in tall], 1.0)
        for t in range(3):
            p = 0.5 * (easts[t] - wests[t])
            q = 0.5 * (tall[t][ROW + 1 : 2 * ROW + 1] - tall[t][ROW - 1 : 2 * ROW - 1])
            scale = lax.rsqrt(1.0 + p * p + q * q)
            xx, xy, xz, yy, yz, zz, vx, vy, vz = [mo[m, t, at, :] for m in range(MOMENTS)]
            alb = al[t, at, :]
            lit = alb * scale
            gx = lit * (xz - p * xx - q * xy) - vx
            gy = lit * (yz - p * xy - q * yy) - vy
            gz = lit * (zz - p * xz - q * yz) - vz
            grad_a = scale * (gz - p * gx - q * gy)
            turn = scale * grad_a
            gps[t, at, :] = 0.3 * p - lit * (gx + p * turn)
            gqs[t, at, :] = 0.3 * q - lit * (gy + q * turn)
            al[t, at, :] = alb - rate_a * grad_a
        return carry

    def descend(i, carry):
        base = pl.multiple_of(i * ROW, ROW)
        at = pl.ds(pl.multiple_of(base + ROW, ROW), ROW)
        easts, wests = beside([gps[t, at, :] for t in range(3)], -1.0)
        for t in range(3):
            tall = gqs[t, pl.ds(base, 3 * ROW), :]
            grad_h = 0.5 * (wests[t] - easts[t]) + 0.5 * (
                tall[ROW - 1 : 2 * ROW - 1] - tall[ROW + 1 : 2 * ROW + 1]
            )
            hs[t, at, :] = hs[t, at, :] - rate_h * grad_h
        return carry

    blocks = (rows + 2 * ROW) // ROW
    borders(hs, 1.0)

    def iterate(n, carry):
        lax.fori_loop(0, blocks, slopes, 0)
        borders(gqs, -1.0)
        lax.fori_loop(0, blocks, descend, 0)
        borders(hs, 1.0)
        return carry

    lax.fori_loop(0, ITERS, iterate, 0)
    center = pl.ds(top, rows)
    for t in range(2):
        lanes = pl.ds(t * LANES, LANES)
        out_h[:, lanes] = hs[t, center, :]
        out_a[:, lanes] = al[t, center, :]


def pair_groups(sizes, axis):
    ny, nx = sizes

    def flat(y, x, core):
        return (y % ny * nx + x % nx) * 2 + core

    dy, dx = (1, 0) if axis == "gy" else (0, 1)
    return [[flat(y, x, 1), flat(y + dy, x + dx, 0)] for y in range(ny) for x in range(nx)]


def from_next(x, axis, core):
    groups = pair_groups((lax.axis_size("gy"), lax.axis_size("gx")), axis)
    both = lax.all_gather(x, AXES, axis_index_groups=groups)
    return lax.dynamic_index_in_dim(both, core, 0, keepdims=False)


VMEM = pl.BlockSpec(memory_space=pltpu.VMEM)
SMEM = pl.BlockSpec(memory_space=pltpu.SMEM)


def shards(
    heights, albedo, images, weights, sun_index, expo_index, sun_azimuth, sun_elevation, exposure
):
    rows, cols = heights.shape
    core = lax.axis_index("img")
    total = images.shape[0] * lax.axis_size("img")
    shape = jax.ShapeDtypeStruct
    mine, edges = pl.pallas_call(
        moments_kernel,
        out_shape=(shape((MOMENTS, rows, cols), F32), shape((rows, LANES), F32)),
        in_specs=[SMEM] * 5 + [VMEM] * 4,
        out_specs=(VMEM, VMEM),
        compiler_params=pltpu.CompilerParams(vmem_limit_bytes=24 << 20),
        name="moments",
    )(sun_index, expo_index, sun_azimuth, sun_elevation, exposure, heights, albedo, images, weights)
    swap = [(i, i ^ 1) for i in range(2)]
    theirs = lax.ppermute(mine, "img", swap)
    edges = jnp.sum(lax.all_gather(edges, "img"), axis=0)
    sides = lax.all_gather(from_next(edges, "gx", core), "img")
    ends = pl.pallas_call(
        rows_kernel,
        out_shape=shape(((PLANES + 1) * ROW, cols), F32),
        in_specs=[VMEM] * 5,
        out_specs=VMEM,
        compiler_params=pltpu.CompilerParams(vmem_limit_bytes=24 << 20),
        name="edge_rows",
    )(heights, albedo, mine, theirs, sides)
    ends = lax.all_gather(from_next(ends, "gy", core), "img")
    tall = rows + 4 * ROW
    return pl.pallas_call(
        functools.partial(steps_kernel, (0.2 / total, 0.5 / total)),
        out_shape=(shape((rows, cols), F32), shape((rows, cols), F32)),
        in_specs=[VMEM] * 6,
        out_specs=(VMEM, VMEM),
        scratch_shapes=[
            pltpu.VMEM((3, tall, LANES), F32),
            pltpu.VMEM((3, tall, LANES), F32),
            pltpu.VMEM((MOMENTS, 3, tall, LANES), F32),
            pltpu.VMEM((3, tall, LANES), F32),
            pltpu.VMEM((3, tall, LANES), F32),
        ],
        compiler_params=pltpu.CompilerParams(vmem_limit_bytes=24 << 20),
        name="gradient_steps",
    )(heights, albedo, mine, theirs, sides, ends)


def solution(mesh):
    return jax.shard_map(
        shards,
        mesh=mesh,
        in_specs=(
            P("gy", "gx"),
            P("gy", "gx"),
            P("img", "gy", "gx"),
            P("img", "gy", "gx"),
            P("img"),
            P("img"),
            P(),
            P(),
            P(),
        ),
        out_specs=(P("gy", "gx"), P("gy", "gx")),
        check_vma=False,
    )
```

time: 334 us -> 68.7 us (0.21)
  the two profiles are of different devices: /device:TPU:7 before, /device:TPU:1 now
where the time goes in v1:
time: 68.7 us; the launch traced here: 68.3 us
  Pallas kernels  27.3 us (40%)
  blocking collectives  24.3 us (35%)
  starting transfers between devices  8.79 us (13%)
  local copies, waits for them, and re-layouts  7.27 us (11%)
    pallas_call x1, Pallas kernels, shards(): pl.pallas_call(functools.partial(steps_kernel, (0.2 / total, 0.5 / total)...  23 us
    all_gather x2, blocking collectives, from_next(): both = lax.all_gather(x, AXES, axis_index_groups=groups)  10.1 us
    ppermute x1, starting transfers between devices, shards(): theirs = lax.ppermute(mine, 'img', swap)  8.79 us
    unnamed x22, local copies, waits for them, and re-layouts  7.26 us
    all_gather x1, blocking collectives, shards(): ends = lax.all_gather(from_next(ends, 'gy', core), 'img')  5.58 us
    all_gather x1, blocking collectives, shards(): edges = jnp.sum(lax.all_gather(edges, 'img'), axis=0)  4.32 us
    all_gather x1, blocking collectives, shards(): sides = lax.all_gather(from_next(edges, 'gx', core), 'img')  4.28 us
    pallas_call x1, Pallas kernels, shards(): pl.pallas_call(moments_kernel, out_shape=(shape((MOMENTS, rows, cols), F3...  2.55 us
  transfers between devices with their start and end apart: 1, of which 0 were waited for; matrix products, arithmetic and copies ran while one was open for 0% of the time, Pallas kernels for 0%

profile of v1, /device:TPU:1, one launch (start us, length us, event | category | flops | bytes accessed | tf_op | source)
XLA Modules:
  0.0 68.3 jit_solution(10173173238314181945)
XLA Ops:
  0.6 0.0 copy-start
  0.6 0.9 %copy-done = f32[256,256]{1,0:T(8,128)S(1)} copy-done((f32[256,256]{1,0:T(8,128)S(1)}, f32[256,256]{1,0:T(8,128)}, u32[]{:S(2)}) %copy-start) | copy-done | bytes 262168
  1.6 0.0 copy-start.2
  1.6 0.9 %copy-done.2 = f32[256,256]{1,0:T(8,128)S(1)} copy-done((f32[256,256]{1,0:T(8,128)S(1)}, f32[256,256]{1,0:T(8,128)}, u32[]{:S(2)}) %copy-start.2) | copy-done | bytes 262168
  2.5 0.0 copy-start.4
  2.5 1.0 %copy-done.4 = bf16[4,256,256]{2,1,0:T(8,128)(2,1)S(1)} copy-done((bf16[4,256,256]{2,1,0:T(8,128)(2,1)S(1)}, bf16[4,256,256]{2,1,0:T(8,128)(2,1)}, u32[]{:S(2)}) %copy-start.4) | copy-done | bytes 524312
  3.6 0.0 copy-start.5
  3.6 1.0 %copy-done.5 = bf16[4,256,256]{2,1,0:T(8,128)(2,1)S(1)} copy-done((bf16[4,256,256]{2,1,0:T(8,128)(2,1)S(1)}, bf16[4,256,256]{2,1,0:T(8,128)(2,1)}, u32[]{:S(2)}) %copy-start.5) | copy-done | bytes 524312
  4.6 0.0 copy-start.6
  4.6 0.7 copy-done.6
  5.3 0.0 copy-start.7
  5.3 0.7 copy-done.7
  5.9 0.0 copy-start.8
  5.9 0.7 copy-done.8
  6.6 0.0 copy-start.9
  6.6 0.7 copy-done.9
  7.2 0.0 copy-start.10
  7.2 0.7 copy-done.10
  7.9 0.0 copy-start.1
  7.9 0.0 copy-start.3
  7.9 2.6 %moments.1 = (f32[9,256,256]{2,1,0:T(8,128)S(1)}, f32[256,128]{1,0:T(8,128)S(1)}) custom-call(s32[4]{0:T(128)S(1)} %copy-done.6, s32[4]{0:T(128)S(1)} %copy-done.7, f32[8]{0:T(128)S(1)} %copy-done.8, f32[8]{0:T(128)S(1)} %copy-done.9, f32[8]{0:T(128)S(1)} %copy-done.10, f32[256,256]{1,0:T(8,128)S(1)} %copy-done, f32[256,256]{1,0:T(8,128)S(1)} %copy-done.2, ...), custom_call_target="tpu_custom_call" | custom-call | tf_op jit(solution)/shard_map/moments/pallas_call | solution.py:237
  10.5 8.8 %collective-permute-start = (f32[9,256,256]{2,1,0:T(8,128)S(1)}, f32[9,256,256]{2,1,0:T(8,128)}, u32[]{:S(2)}, u32[]{:S(2)}) collective-permute-start(f32[9,256,256]{2,1,0:T(8,128)S(1)} %get-tuple-element.4.mine), channel_id=1, source_target_pairs={{0,1},{1,0},{2,3},{3,2},{4,5},{5,4},{6,7},{7,6},{8,9},{9,8},{10,11... | collective-permute-start | bytes 7077896 | tf_op jit(solution)/shard_map/ppermute | solution.py:246
  19.3 4.3 %all-gather = f32[512,128]{1,0:T(8,128)S(1)} all-gather(f32[256,128]{1,0:T(8,128)S(1)} %get-tuple-element.5), channel_id=2, replica_groups=mesh['gy'=16,'gx'=16,'img'=2] {'img'}, dimensions={0}, use_global_device_ids=true | all-gather | bytes 393216 | tf_op jit(solution)/shard_map/all_gather | solution.py:247
  23.6 5.4 %all-gather.1 = f32[512,128]{1,0:T(8,128)S(1)} all-gather(f32[256,128]{1,0:T(8,128)S(1)} %reduce_sum.9), channel_id=3, replica_groups={{1,2},{3,4},{5,6},{7,8},{9,10},{11,12},{13,14},{15,16},{17,18},{19,20},..., dimensions={0}, use_global_device_ids=true | all-gather | bytes 393216 | tf_op jit(solution)/shard_map/all_gather | solution.py:222
  29.0 4.3 %all_gather.30.sides = f32[2,256,128]{2,1,0:T(8,128)S(1)} all-gather(f32[1,256,128]{2,1,0:T(8,128)S(1)} %constant_dynamic-slice_fusion.1), channel_id=1, replica_groups=mesh['gy'=16,'gx'=16,'img'=2] {'img'}, dimensions={0}, use_global_device_ids=true | all-gather | bytes 393216 | tf_op jit(solution)/shard_map/all_gather | solution.py:248
  33.3 0.0 collective-permute-done.theirs
  33.3 0.0 copy-done.1
  33.3 0.0 copy-done.3
  33.3 1.7 %edge_rows.1 = f32[96,256]{1,0:T(8,128)S(1)} custom-call(f32[256,256]{1,0:T(8,128)S(1)} %copy-done.1, f32[256,256]{1,0:T(8,128)S(1)} %copy-done.3, f32[9,256,256]{2,1,0:T(8,128)S(1)} %get-tuple-element.4.mine, f32[9,256,256]{2,1,0:T(8,128)} %collective-permute-done.theirs, f32[2,256,128]{2,1,0:T(8,128)S(1)} %all_gather.30.sides), custom_call_target="tpu_custom_call" | custom-call | tf_op jit(solution)/shard_map/edge_rows/pallas_call | solution.py:249
  35.0 4.7 %all-gather.2 = f32[192,256]{1,0:T(8,128)S(1)} all-gather(f32[96,256]{1,0:T(8,128)S(1)} %edge_rows.1), channel_id=4, replica_groups={{1,32},{3,34},{5,36},{7,38},{9,40},{11,42},{13,44},{15,46},{17,48},{19,..., dimensions={0}, use_global_device_ids=true | all-gather | bytes 294912 | tf_op jit(solution)/shard_map/all_gather | solution.py:222
  39.7 5.6 %all_gather.33.ends = f32[2,96,256]{2,1,0:T(8,128)S(1)} all-gather(f32[1,96,256]{2,1,0:T(8,128)S(1)} %constant_dynamic-slice_fusion), channel_id=1, replica_groups=mesh['gy'=16,'gx'=16,'img'=2] {'img'}, dimensions={0}, use_global_device_ids=true | all-gather | bytes 294912 | tf_op jit(solution)/shard_map/all_gather | solution.py:257
  45.3 23.0 %gradient_steps.1 = (f32[256,256]{1,0:T(8,128)}, f32[256,256]{1,0:T(8,128)}) custom-call(f32[256,256]{1,0:T(8,128)S(1)} %copy-done.1, f32[256,256]{1,0:T(8,128)S(1)} %copy-done.3, f32[9,256,256]{2,1,0:T(8,128)S(1)} %get-tuple-element.4.mine, f32[9,256,256]{2,1,0:T(8,128)} %collective-permute-done.theirs, f32[2,256,128]{2,1,0:T(8,128)S(1)} %all_gather.30.sides, ...), custom_call_target="tpu_custom_call" | custom-call | tf_op jit(solution)/shard_map/gradient_steps/pallas_call | solution.py:259
  (3 shorter events, 0.0 us)
Async XLA Ops:
  0.6 1.0 %copy-start = (f32[256,256]{1,0:T(8,128)S(1)}, f32[256,256]{1,0:T(8,128)}, u32[]{:S(2)}) copy-start(f32[256,256]{1,0:T(8,128)} %height.5) | copy-start | bytes 786436
  1.6 0.9 %copy-start.2 = (f32[256,256]{1,0:T(8,128)S(1)}, f32[256,256]{1,0:T(8,128)}, u32[]{:S(2)}) copy-start(f32[256,256]{1,0:T(8,128)} %albedo.5) | copy-start | bytes 786436
  2.5 1.0 %copy-start.4 = (bf16[4,256,256]{2,1,0:T(8,128)(2,1)S(1)}, bf16[4,256,256]{2,1,0:T(8,128)(2,1)}, u32[]{:S(2)}) copy-start(bf16[4,256,256]{2,1,0:T(8,128)(2,1)} %images.1) | copy-start | bytes 1572868
  3.6 1.0 %copy-start.5 = (bf16[4,256,256]{2,1,0:T(8,128)(2,1)S(1)}, bf16[4,256,256]{2,1,0:T(8,128)(2,1)}, u32[]{:S(2)}) copy-start(bf16[4,256,256]{2,1,0:T(8,128)(2,1)} %weights.1) | copy-start | bytes 1572868
  4.6 0.7 copy-start.6
  5.3 0.7 copy-start.7
  5.9 0.7 copy-start.8
  6.6 0.7 copy-start.9
  7.2 0.7 copy-start.10
  7.9 25.4 %copy-start.1 = (f32[256,256]{1,0:T(8,128)S(1)}, f32[256,256]{1,0:T(8,128)}, u32[]{:S(2)}) copy-start(f32[256,256]{1,0:T(8,128)} %height.5) | copy-start | bytes 786436
  7.9 25.4 %copy-start.3 = (f32[256,256]{1,0:T(8,128)S(1)}, f32[256,256]{1,0:T(8,128)}, u32[]{:S(2)}) copy-start(f32[256,256]{1,0:T(8,128)} %albedo.5) | copy-start | bytes 786436
  10.5 22.8 %collective-permute-start = (f32[9,256,256]{2,1,0:T(8,128)S(1)}, f32[9,256,256]{2,1,0:T(8,128)}, u32[]{:S(2)}, u32[]{:S(2)}) collective-permute-start(f32[9,256,256]{2,1,0:T(8,128)S(1)} %get-tuple-element.4.mine), channel_id=1, source_target_pairs={{0,1},{1,0},{2,3},{3,2},{4,5},{5,4},{6,7},{7,6},{8,9},{9,8},{10,11... | collective-permute-start | bytes 7077896 | tf_op jit(solution)/shard_map/ppermute | solution.py:246

commit v2 on v1

v2 whole, which is shorter than its diff:
```python
import functools

import jax
import jax.numpy as jnp
from jax import lax
from jax.experimental import pallas as pl
from jax.experimental.pallas import tpu as pltpu
from jax.sharding import PartitionSpec as P

ITERS = 3
AXES = ("gy", "gx", "img")
LANES = 128
ROW = 8
CHUNKS = 4
MOMENTS = 9
PLANES = 2 + MOMENTS
WIDTHS = (6,) + (5,) * (PLANES - 1)
STARTS = tuple(6 if k == 0 else 17 + 10 * (k - 1) for k in range(PLANES))
F32 = jnp.float32


def lane_ids(rows):
    return lax.broadcasted_iota(jnp.int32, (rows, LANES), 1)


def east_lanes(lane):
    hit = lane < 0
    for start, width in zip(STARTS, WIDTHS):
        hit = hit | ((lane >= start) & (lane < start + width))
    return hit


def moments_kernel(
    sun_index_hbm, expo_index_hbm, azimuth_hbm, elevation_hbm, exposure_hbm, height_hbm, albedo_hbm, images_hbm,
    weights_hbm, height, albedo, keep, send, edges, sun_index, expo_index, azimuth, elevation, exposure, images,
    weights, sums, small_sems, large_sems
):
    count, rows, _ = images.shape
    small = [
        pltpu.make_async_copy(src, dst, small_sems.at[n])
        for n, (src, dst) in enumerate((
            (sun_index_hbm, sun_index), (expo_index_hbm, expo_index), (azimuth_hbm, azimuth),
            (elevation_hbm, elevation), (exposure_hbm, exposure),
        ))
    ]
    for copy in small:
        copy.start()
    part = rows // CHUNKS
    large = []
    for c in range(CHUNKS):
        at = pl.ds(c * part, part)
        large.append([
            pltpu.make_async_copy(weights_hbm.at[:, at, :], weights.at[:, at, :], large_sems.at[c, 0]),
            pltpu.make_async_copy(images_hbm.at[:, at, :], images.at[:, at, :], large_sems.at[c, 1]),
            pltpu.make_async_copy(height_hbm.at[at, :], height.at[at, :], large_sems.at[c, 2]),
            pltpu.make_async_copy(albedo_hbm.at[at, :], albedo.at[at, :], large_sems.at[c, 3]),
        ])
        for copy in large[c]:
            copy.start()
    for copy in small:
        copy.wait()
    line = lax.broadcasted_iota(jnp.int32, (ROW, LANES), 0)
    azim = jnp.zeros((ROW, LANES), F32)
    elev = jnp.zeros((ROW, LANES), F32)
    gain = jnp.zeros((ROW, LANES), F32)
    for k in range(count):
        azim = jnp.where(line == k, azimuth[sun_index[k]], azim)
        elev = jnp.where(line == k, elevation[sun_index[k]], elev)
        gain = jnp.where(line == k, exposure[expo_index[k]], gain)
    flat = jnp.cos(elev)
    sx = gain * flat * jnp.cos(azim)
    sy = gain * flat * jnp.sin(azim)
    sz = gain * jnp.sin(elev)
    factors = (sx * sx, sx * sy, sx * sz, sy * sy, sy * sz, sz * sz, sx, sy, sz)
    step = 16
    lane = lane_ids(step)
    masks = [(lane >= s - w) & (lane < s + w) for s, w in zip(STARTS, WIDTHS)]

    for c in range(CHUNKS):
        for copy in large[c]:
            copy.wait()
        for i in range(c * part, (c + 1) * part, step):
            at = pl.ds(i, step)
            acc = [None] * MOMENTS
            for k in range(count):
                w = weights[k, at, :].astype(F32)
                u = w * images[k, at, :].astype(F32)
                for m, factor in enumerate(factors):
                    term = (w if m < 6 else u) * factor[k : k + 1, :1]
                    acc[m] = term if k == 0 else acc[m] + term
            for m in range(MOMENTS):
                sums[m, at, :] = acc[m]
            packed = jnp.zeros((step, LANES), F32)
            planes = [0.5 * height[at, :], 0.5 * albedo[at, :]] + acc
            for start, mask, plane in zip(STARTS, masks, planes):
                ends = jnp.where(lane < LANES // 2, plane[:, :LANES], plane[:, -LANES:])
                packed = jnp.where(mask, pltpu.roll(ends, start, 1), packed)
            edges[at, :] = packed
    core = lax.axis_index("img")
    for out, first in ((keep, core), (send, 1 - core)):
        first = first * (rows - out.shape[1])
        for m in range(MOMENTS):
            for i in range(0, out.shape[1], ROW):
                out[m, pl.ds(i, ROW), :] = sums[m, pl.ds(pl.multiple_of(first + i, ROW), ROW), :]


def place_kernel(halves, height, albedo, sems):
    half = halves.shape[2]
    copies = [
        pltpu.make_async_copy(halves.at[c, n], out.at[pl.ds(c * half, half), :], sems.at[c, n])
        for c in range(2)
        for n, out in enumerate((height, albedo))
    ]
    for copy in copies:
        copy.start()
    for copy in copies:
        copy.wait()


def rows_kernel(height, albedo, sums, sides, out):
    rows = height.shape[0]
    core = lax.axis_index("img")
    at = pl.ds(pl.multiple_of(core * (rows - ROW), ROW), ROW)
    of_sums = pl.ds(pl.multiple_of(core * (sums.shape[1] - ROW), ROW), ROW)
    out[pl.ds(0, ROW), :] = height[at, :]
    out[pl.ds(ROW, ROW), :] = albedo[at, :]
    for m in range(MOMENTS):
        out[pl.ds((2 + m) * ROW, ROW), :] = sums[m, of_sums, :]
    both = jnp.where(east_lanes(lane_ids(ROW)), sides[1, at, :], sides[0, at, :])
    out[pl.ds(PLANES * ROW, ROW), :] = jnp.concatenate([both, both], axis=1)


def steps_kernel(rates, height, albedo, sums, sides, ends, out, hs, al, mo, gps, gqs):
    rows, cols = height.shape
    own = sums.shape[1]
    half = rows // 2
    core = lax.axis_index("img")
    first_y = (lax.axis_index("gy") == 0) & (core == 0)
    last_y = (lax.axis_index("gy") == lax.axis_size("gy") - 1) & (core == 1)
    first_x = lax.axis_index("gx") == 0
    last_x = lax.axis_index("gx") == lax.axis_size("gx") - 1
    rate_h, rate_a = rates
    top = 2 * ROW
    bottom = top + half

    def plane(k):
        return hs if k == 0 else al if k == 1 else mo.at[k - 2]

    east = east_lanes(lane_ids(ROW))
    first = core * (rows - own)
    place = top - core * ROW
    for i in range(0, own, ROW):
        src = pl.ds(pl.multiple_of(first + i, ROW), ROW)
        dst = pl.ds(pl.multiple_of(place + i, ROW), ROW)
        both = jnp.where(east, sides[1, src, :], sides[0, src, :])
        for k in range(PLANES):
            if k == 0:
                body = height[src, :]
            elif k == 1:
                body = albedo[src, :]
            else:
                body = sums[k - 2, pl.ds(i, ROW), :]
            ref = plane(k)
            ref[0, dst, :] = body[:, :LANES]
            ref[1, dst, :] = body[:, LANES:]
            ref[2, dst, :] = pltpu.roll(both, LANES - STARTS[k], 1)
    dst = pl.ds(pl.multiple_of(ROW + core * own, ROW), ROW)
    both = ends[pl.ds(PLANES * ROW, ROW), :LANES]
    for k in range(PLANES):
        ref = plane(k)
        body = ends[pl.ds(k * ROW, ROW), :]
        ref[0, dst, :] = body[:, :LANES]
        ref[1, dst, :] = body[:, LANES:]
        ref[2, dst, :] = pltpu.roll(both, LANES - STARTS[k], 1)

    lane = lane_ids(ROW)
    head = lane == 0
    tail = lane == LANES - 1
    wall_w = head & first_x
    wall_e = tail & last_x

    def beside(blocks, sign):
        fore = [pltpu.roll(b, LANES - 1, 1) for b in blocks]
        back = [pltpu.roll(b, 1, 1) for b in blocks]
        easts = [jnp.where(tail, fore[(t + 1) % 3], fore[t]) for t in range(3)]
        wests = [jnp.where(head, back[(t + 2) % 3], back[t]) for t in range(3)]
        easts[1] = jnp.where(wall_e, sign * blocks[1], easts[1])
        wests[0] = jnp.where(wall_w, sign * blocks[0], wests[0])
        return easts, wests

    def borders(ref, sign):
        @pl.when(first_y)
        def _():
            ref[:, pl.ds(top - 1, 1), :] = sign * ref[:, pl.ds(top, 1), :]

        @pl.when(last_y)
        def _():
            ref[:, pl.ds(bottom, 1), :] = sign * ref[:, pl.ds(bottom - 1, 1), :]

    def slopes(i, carry):
        base = pl.multiple_of(i * ROW, ROW)
        at = pl.ds(pl.multiple_of(base + ROW, ROW), ROW)
        easts, wests = beside([hs[t, at, :] for t in range(3)], 1.0)
        for t in range(3):
            p = 0.5 * (easts[t] - wests[t])
            q = 0.5 * (hs[t, pl.ds(base + ROW + 1, ROW), :] - hs[t, pl.ds(base + ROW - 1, ROW), :])
            scale = lax.rsqrt(1.0 + p * p + q * q)
            xx, xy, xz, yy, yz, zz, vx, vy, vz = [mo[m, t, at, :] for m in range(MOMENTS)]
            alb = al[t, at, :]
            lit = alb * scale
            gx = lit * (xz - p * xx - q * xy) - vx
            gy = lit * (yz - p * xy - q * yy) - vy
            gz = lit * (zz - p * xz - q * yz) - vz
            grad_a = scale * (gz - p * gx - q * gy)
            turn = scale * grad_a
            bend = 0.3 - lit * turn
            gps[t, at, :] = p * bend - lit * gx
            gqs[t, at, :] = q * bend - lit * gy
            al[t, at, :] = alb - rate_a * grad_a
        return carry

    def descend(i, carry):
        base = pl.multiple_of(i * ROW, ROW)
        at = pl.ds(pl.multiple_of(base + ROW, ROW), ROW)
        easts, wests = beside([gps[t, at, :] for t in range(3)], -1.0)
        for t in range(3):
            grad_h = 0.5 * (wests[t] - easts[t]) + 0.5 * (
                gqs[t, pl.ds(base + ROW - 1, ROW), :] - gqs[t, pl.ds(base + ROW + 1, ROW), :]
            )
            hs[t, at, :] = hs[t, at, :] - rate_h * grad_h
        return carry

    blocks = half // ROW + 2
    borders(hs, 1.0)

    def iterate(n, carry):
        lax.fori_loop(0, blocks, slopes, 0, unroll=blocks)
        borders(gqs, -1.0)
        lax.fori_loop(0, blocks, descend, 0, unroll=blocks)
        borders(hs, 1.0)
        return carry

    lax.fori_loop(0, ITERS, iterate, 0)
    center = pl.ds(top, half)
    for t in range(2):
        lanes = pl.ds(t * LANES, LANES)
        out[0, :, lanes] = hs[t, center, :]
        out[1, :, lanes] = al[t, center, :]


def pair_groups(sizes, axis):
    ny, nx = sizes

    def flat(y, x, core):
        return (y * nx + x) * 2 + core

    if axis == "gx":
        groups = [[flat(y, x, 1), flat(y, x + 1, 0)] for y in range(ny) for x in range(nx - 1)]
        for y in range(0, ny, 2):
            groups += [[flat(y, x, core), flat(y + 1, x, core)] for x, core in ((0, 0), (nx - 1, 1))]
    else:
        groups = [[flat(y, x, 1), flat(y + 1, x, 0)] for y in range(ny - 1) for x in range(nx)]
        for x in range(0, nx, 2):
            groups += [[flat(y, x, core), flat(y, x + 1, core)] for y, core in ((0, 0), (ny - 1, 1))]
    return groups


def from_next(x, axis, core):
    groups = pair_groups((lax.axis_size("gy"), lax.axis_size("gx")), axis)
    both = lax.all_gather(x, AXES, axis_index_groups=groups)
    return lax.dynamic_index_in_dim(both, core, 0, keepdims=False)


VMEM = pl.BlockSpec(memory_space=pltpu.VMEM)
HBM = pl.BlockSpec(memory_space=pltpu.HBM)


def in_vmem(*args):
    return tuple(pltpu.with_memory_space_constraint(x, pltpu.VMEM) for x in args)


def params(mib):
    return pltpu.CompilerParams(vmem_limit_bytes=mib << 20)


def run_moments(*args):
    args = tuple(pltpu.with_memory_space_constraint(x, pltpu.HBM) for x in args)
    rows, cols = args[5].shape
    part = pltpu.VMEM((MOMENTS, rows // 2 + ROW, cols), F32)
    return pl.pallas_call(
        moments_kernel,
        out_shape=tuple(pltpu.VMEM(x.shape, x.dtype) for x in args[5:7])
        + (part, part, pltpu.VMEM((rows, LANES), F32)),
        in_specs=[HBM] * len(args),
        out_specs=(VMEM,) * 5,
        scratch_shapes=[pltpu.SMEM(x.shape, x.dtype) for x in args[:5]]
        + [pltpu.VMEM(x.shape, x.dtype) for x in args[7:]]
        + [pltpu.VMEM((MOMENTS, rows, cols), F32)]
        + [pltpu.SemaphoreType.DMA((5,)), pltpu.SemaphoreType.DMA((CHUNKS, 4))],
        compiler_params=params(8),
        name="moments",
    )(*args)


def run_rows(heights, albedo, sums, sides):
    return pl.pallas_call(
        rows_kernel,
        out_shape=pltpu.VMEM(((PLANES + 1) * ROW, heights.shape[1]), F32),
        in_specs=[VMEM] * 4,
        out_specs=VMEM,
        compiler_params=params(8),
        name="edge_rows",
    )(*in_vmem(heights, albedo, sums, sides))


def run_steps(total, heights, albedo, sums, sides, ends):
    rows, cols = heights.shape
    block = pltpu.VMEM((3, rows // 2 + 4 * ROW, LANES), F32)
    return pl.pallas_call(
        functools.partial(steps_kernel, (0.2 / total, 0.5 / total)),
        out_shape=pltpu.VMEM((2, rows // 2, cols), F32),
        in_specs=[VMEM] * 5,
        out_specs=VMEM,
        scratch_shapes=[block, block, pltpu.VMEM((MOMENTS, *block.shape), F32), block, block],
        compiler_params=params(12),
        name="gradient_steps",
    )(*in_vmem(heights, albedo, sums, sides, ends))


def run_place(halves):
    _, _, half, cols = halves.shape
    out = jax.ShapeDtypeStruct((2 * half, cols), F32)
    return pl.pallas_call(
        place_kernel,
        out_shape=(out, out),
        in_specs=[VMEM],
        out_specs=(HBM, HBM),
        scratch_shapes=[pltpu.SemaphoreType.DMA((2, 2))],
        compiler_params=params(8),
        name="place",
    )(*in_vmem(halves))


def shards(
    heights, albedo, images, weights, sun_index, expo_index, sun_azimuth, sun_elevation, exposure
):
    total = images.shape[0] * lax.axis_size("img")
    core = lax.axis_index("img")
    heights, albedo, keep, send, edges = run_moments(
        sun_index, expo_index, sun_azimuth, sun_elevation, exposure, heights, albedo, images, weights
    )
    edges, send = lax.optimization_barrier((lax.all_gather(edges, "img"), send))
    theirs = lax.ppermute(send, "img", [(0, 1), (1, 0)])
    edges = jnp.sum(edges, axis=0)
    sides = lax.all_gather(from_next(edges, "gx", core), "img")
    sums = keep + theirs
    ends = from_next(run_rows(heights, albedo, sums, sides), "gy", core)
    halves = run_steps(total, heights, albedo, sums, sides, ends)
    return run_place(lax.all_gather(halves, "img"))


def solution(mesh):
    return jax.shard_map(
        shards,
        mesh=mesh,
        in_specs=(
            P("gy", "gx"),
            P("gy", "gx"),
            P("img", "gy", "gx"),
            P("img", "gy", "gx"),
            P("img"),
            P("img"),
            P(),
            P(),
            P(),
        ),
        out_specs=(P("gy", "gx"), P("gy", "gx")),
        check_vma=False,
    )
```

time: 68.7 us -> 37.4 us (0.54)
  the two profiles are of different devices: /device:TPU:1 before, /device:TPU:7 now
where the time goes in v2:
time: 37.4 us; the launch traced here: 37.1 us
  blocking collectives  27.2 us (73%)
  Pallas kernels  5.53 us (15%)
  starting transfers between devices  2.26 us (6%)
  other arithmetic  1.47 us (4%)
  between operations  0.69 us (2%)
    all_gather x2, blocking collectives, from_next(): both = lax.all_gather(x, AXES, axis_index_groups=groups)  10.2 us
    all_gather x1, blocking collectives, shards(): sides = lax.all_gather(from_next(edges, 'gx', core), 'img')  8.93 us
    all_gather x1, blocking collectives, shards(): return run_place(lax.all_gather(halves, 'img'))  5.79 us
    pallas_call x1, Pallas kernels, run_moments(): pl.pallas_call(moments_kernel, out_shape=tuple((pltpu.VMEM(x.shape, x.dty...  2.44 us
    all_gather x1, blocking collectives, shards(): edges, send = lax.optimization_barrier((lax.all_gather(edges, 'img'), send))  2.31 us
    ppermute x1, starting transfers between devices, shards(): theirs = lax.ppermute(send, 'img', [(0, 1), (1, 0)])  2.26 us
    pallas_call x1, Pallas kernels, run_steps(): pl.pallas_call(functools.partial(steps_kernel, (0.2 / total, 0.5 / total)...  2.25 us
    add x1, other arithmetic, shards(): sums = keep + theirs  1.46 us
  transfers between devices with their start and end apart: 1, of which 0 were waited for; matrix products, arithmetic and copies ran while one was open for 0% of the time, Pallas kernels for 0%

profile of v2, /device:TPU:7, one launch (start us, length us, event | category | flops | bytes accessed | tf_op | source)
XLA Modules:
  0.0 37.1 jit_solution(7854882275345077973)
XLA Ops:
  0.6 2.4 %moments.1 = (f32[256,256]{1,0:T(8,128)S(1)}, f32[256,256]{1,0:T(8,128)S(1)}, f32[9,136,256]{2,1,0:T(8,128)S(1)}, f32[9,136,256]{2,1,0:T(8,128)S(1)}, f32[256,128]{1,0:T(8,128)S(1)}) custom-call(s32[4]{0:T(128)} %sun_index_hbm.1, s32[4]{0:T(128)} %expo_index_hbm.1, f32[8]{0:T(128)} %azimuth_hbm.1, f32[8]{0:T(128)} %elevation_hbm.1, f32[8]{0:T(128)} %exposure_hbm.1, ...), custom_call_target="tpu_custom_call" | custom-call | tf_op jit(solution)/shard_map/moments/pallas_call | solution.py:290
  3.1 2.3 %all-gather = f32[512,128]{1,0:T(8,128)S(1)} all-gather(f32[256,128]{1,0:T(8,128)S(1)} %get-tuple-element.12), channel_id=2, replica_groups=mesh['gy'=16,'gx'=16,'img'=2] {'img'}, dimensions={0}, use_global_device_ids=true | all-gather | bytes 393216 | tf_op jit(solution)/shard_map/all_gather | solution.py:352
  5.4 2.3 %collective-permute-start = (f32[9,136,256]{2,1,0:T(8,128)S(1)}, f32[9,136,256]{2,1,0:T(8,128)}, u32[]{:S(2)}, u32[]{:S(2)}) collective-permute-start(f32[9,136,256]{2,1,0:T(8,128)S(1)} %get-tuple-element.14), channel_id=1, source_target_pairs={{0,1},{1,0},{2,3},{3,2},{4,5},{5,4},{6,7},{7,6},{8,9},{9,8},{10,11... | collective-permute-start | bytes 3760136 | tf_op jit(solution)/shard_map/ppermute | solution.py:353
  7.7 5.4 %all-gather.1 = f32[512,128]{1,0:T(8,128)S(1)} all-gather(f32[256,128]{1,0:T(8,128)S(1)} %reduce_sum.9), channel_id=3, replica_groups={{1,2},{3,4},{5,6},{7,8},{9,10},{11,12},{13,14},{15,16},{17,18},{19,20},..., dimensions={0}, use_global_device_ids=true | all-gather | bytes 393216 | tf_op jit(solution)/shard_map/all_gather | solution.py:270
  13.1 8.9 %all_gather.32.sides = f32[2,256,128]{2,1,0:T(8,128)S(1)} all-gather(f32[1,256,128]{2,1,0:T(8,128)S(1)} %constant_dynamic-slice_fusion), channel_id=1, replica_groups=mesh['gy'=16,'gx'=16,'img'=2] {'img'}, dimensions={0}, use_global_device_ids=true | all-gather | bytes 393216 | tf_op jit(solution)/shard_map/all_gather | solution.py:355
  22.1 0.0 collective-permute-done
  22.1 1.5 %add.9.sums = f32[9,136,256]{2,1,0:T(8,128)S(1)} add(f32[9,136,256]{2,1,0:T(8,128)S(1)} %get-tuple-element.11, f32[9,136,256]{2,1,0:T(8,128)} %collective-permute-done) | non-fusion elementwise | flops 313344 | bytes 3760128 | tf_op jit(solution)/shard_map/add | solution.py:356
  23.6 4.7 %all-gather.2 = f32[192,256]{1,0:T(8,128)S(1)} all-gather(f32[96,256]{1,0:T(8,128)S(1)} %edge_rows.1), channel_id=4, replica_groups={{1,32},{3,34},{5,36},{7,38},{9,40},{11,42},{13,44},{15,46},{17,48},{19,..., dimensions={0}, use_global_device_ids=true | all-gather | bytes 294912 | tf_op jit(solution)/shard_map/all_gather | solution.py:270
  28.3 2.2 %gradient_steps.1 = f32[2,128,256]{2,1,0:T(8,128)S(1)} custom-call(f32[256,256]{1,0:T(8,128)S(1)} %get-tuple-element.9.height, f32[256,256]{1,0:T(8,128)S(1)} %get-tuple-element.10.albedo, f32[9,136,256]{2,1,0:T(8,128)S(1)} %add.9.sums, f32[2,256,128]{2,1,0:T(8,128)S(1)} %all_gather.32.sides, f32[96,256]{1,0:T(8,128)S(1)} %dynamic-slice_bitcast_fusion.ends), custom_call_target="tpu_custom_call" | custom-call | tf_op jit(solution)/shard_map/gradient_steps/pallas_call | solution.py:319
  30.5 5.8 %all-gather.3 = f32[4,128,256]{2,1,0:T(8,128)S(1)} all-gather(f32[2,128,256]{2,1,0:T(8,128)S(1)} %gradient_steps.1), channel_id=5, replica_groups=mesh['gy'=16,'gx'=16,'img'=2] {'img'}, dimensions={0}, use_global_device_ids=true | all-gather | bytes 786432 | tf_op jit(solution)/shard_map/all_gather | solution.py:359
  36.3 0.8 %place.1 = (f32[256,256]{1,0:T(8,128)}, f32[256,256]{1,0:T(8,128)}) custom-call(f32[2,2,128,256]{3,2,1,0:T(8,128)S(1)} %bitcast.6), custom_call_target="tpu_custom_call" | custom-call | tf_op jit(solution)/shard_map/place/pallas_call | solution.py:333
  (4 shorter events, 0.1 us)
Async XLA Ops:
  5.4 16.7 %collective-permute-start = (f32[9,136,256]{2,1,0:T(8,128)S(1)}, f32[9,136,256]{2,1,0:T(8,128)}, u32[]{:S(2)}, u32[]{:S(2)}) collective-permute-start(f32[9,136,256]{2,1,0:T(8,128)S(1)} %get-tuple-element.14), channel_id=1, source_target_pairs={{0,1},{1,0},{2,3},{3,2},{4,5},{5,4},{6,7},{7,6},{8,9},{9,8},{10,11... | collective-permute-start | bytes 3760136 | tf_op jit(solution)/shard_map/ppermute | solution.py:353

commit v3 on v2

v3 whole, which is shorter than its diff:
```python
import functools

import jax
import jax.numpy as jnp
from jax import lax
from jax.experimental import pallas as pl
from jax.experimental.pallas import tpu as pltpu
from jax.sharding import PartitionSpec as P

ITERS = 3
AXES = ("gy", "gx", "img")
LANES = 128
ROW = 8
CHUNKS = 4
MOMENTS = 9
PLANES = 2 + MOMENTS
WIDTHS = (6,) + (5,) * (PLANES - 1)
STARTS = tuple(6 if k == 0 else 17 + 10 * (k - 1) for k in range(PLANES))
ROW_STARTS = tuple(sum(WIDTHS[:k]) for k in range(PLANES + 1))
F32 = jnp.float32


def lane_ids(rows):
    return lax.broadcasted_iota(jnp.int32, (rows, LANES), 1)


def east_lanes(lane):
    hit = lane < 0
    for start, width in zip(STARTS, WIDTHS):
        hit = hit | ((lane >= start) & (lane < start + width))
    return hit


def edges_kernel(
    sun_index_hbm, expo_index_hbm, azimuth_hbm, elevation_hbm, exposure_hbm, height_hbm, albedo_hbm, images_hbm,
    weights_hbm, height, albedo, images, weights, tables, own_fold, own_rows, pack, sun_index, expo_index, azimuth,
    elevation, exposure, folds, ends_of_rows, small_sems, large_sems
):
    count, _, half, _ = images.shape
    small = [
        pltpu.make_async_copy(src, dst, small_sems.at[n])
        for n, (src, dst) in enumerate((
            (sun_index_hbm, sun_index), (expo_index_hbm, expo_index), (azimuth_hbm, azimuth),
            (elevation_hbm, elevation), (exposure_hbm, exposure),
        ))
    ]
    for copy in small:
        copy.start()
    part = half // CHUNKS
    large = []
    for c in range(CHUNKS):
        at = pl.ds(c * part, part)
        large.append([
            pltpu.make_async_copy(weights_hbm.at[:, :, at, :], weights.at[:, :, at, :], large_sems.at[c, 0]),
            pltpu.make_async_copy(images_hbm.at[:, :, at, :], images.at[:, :, at, :], large_sems.at[c, 1]),
            pltpu.make_async_copy(height_hbm.at[:, at, :], height.at[:, at, :], large_sems.at[c, 2]),
            pltpu.make_async_copy(albedo_hbm.at[:, at, :], albedo.at[:, at, :], large_sems.at[c, 3]),
        ])
        for copy in large[c]:
            copy.start()
    for copy in small:
        copy.wait()
    line = lax.broadcasted_iota(jnp.int32, (ROW, LANES), 0)
    azim = jnp.zeros((ROW, LANES), F32)
    elev = jnp.zeros((ROW, LANES), F32)
    gain = jnp.zeros((ROW, LANES), F32)
    for k in range(count):
        azim = jnp.where(line == k, azimuth[sun_index[k]], azim)
        elev = jnp.where(line == k, elevation[sun_index[k]], elev)
        gain = jnp.where(line == k, exposure[expo_index[k]], gain)
    flat = jnp.cos(elev)
    sx = gain * flat * jnp.cos(azim)
    sy = gain * flat * jnp.sin(azim)
    sz = gain * jnp.sin(elev)
    factors = (sx * sx, sx * sy, sx * sz, sy * sy, sy * sz, sz * sz, sx, sy, sz)
    for m, factor in enumerate(factors):
        tables[m] = factor
    step = 16
    lane = lane_ids(step)

    def sums(s, at, view):
        return add_moments(
            lambda k: view(weights[k, s, at, :].astype(F32)), lambda k: view(images[k, s, at, :].astype(F32)), count,
            lambda m, k: factors[m][k : k + 1, :1]
        )

    def ends(x):
        return jnp.where(lane < LANES // 2, x[:, :LANES], x[:, -LANES:])

    for c in range(CHUNKS):
        for copy in large[c]:
            copy.wait()
        for i in range(c * part, (c + 1) * part, step):
            at = pl.ds(i, step)
            upper, lower = (
                [ends(0.5 * height[s, at, :]), ends(0.5 * albedo[s, at, :])] + sums(s, at, ends) for s in range(2)
            )
            west = jnp.zeros((step, LANES), F32)
            east = jnp.zeros((step, LANES), F32)
            for start, width, above, below in zip(STARTS, WIDTHS, upper, lower):
                low = (lane >= start - width) & (lane < start)
                high = (lane >= start) & (lane < start + width)
                above = pltpu.roll(above, start, 1)
                west = jnp.where(high, above, jnp.where(low, pltpu.roll(below, start - width, 1), west))
                east = jnp.where(low, above, jnp.where(high, pltpu.roll(below, start + width, 1), east))
            folds[0, at, :] = west
            folds[1, at, :] = east
    for side, first in enumerate((0, half - step)):
        acc = sums(side, pl.ds(first, step), lambda x: x)
        for m in range(MOMENTS):
            ends_of_rows[side, m] = acc[m][:ROW] if side == 0 else acc[m][-ROW:]
    core = lax.axis_index("img")
    own_fold[...] = folds[core]
    pack[pl.ds(0, half), :] = folds[1 - core]
    for m in range(MOMENTS):
        own_rows[pl.ds(m * ROW, ROW), :] = ends_of_rows[core, m]
        for t in range(2):
            pack[pl.ds(half + (2 * m + t) * ROW, ROW), :] = ends_of_rows[1 - core, m, :, t * LANES : (t + 1) * LANES]


def add_moments(weight, image, count, factor):
    acc = [None] * MOMENTS
    for k in range(count):
        w = weight(k)
        u = w * image(k)
        for m in range(MOMENTS):
            term = (w if m < 6 else u) * factor(m, k)
            acc[m] = term if k == 0 else acc[m] + term
    return acc


def moments_kernel(images, weights, tables, keep, send, sums):
    count, rows, _ = images.shape
    step = 16
    for i in range(0, rows, step):
        at = pl.ds(i, step)
        acc = add_moments(
            lambda k: weights[k, at, :].astype(F32), lambda k: images[k, at, :].astype(F32), count,
            lambda m, k: tables[m, k : k + 1, :1]
        )
        for m in range(MOMENTS):
            sums[m, at, :] = acc[m]
    core = lax.axis_index("img")
    for out, first in ((keep, core), (send, 1 - core)):
        first = first * (rows - out.shape[1])
        for m in range(MOMENTS):
            for i in range(0, out.shape[1], ROW):
                out[m, pl.ds(i, ROW), :] = sums[m, pl.ds(pl.multiple_of(first + i, ROW), ROW), :]


def place_kernel(halves, height, albedo, sems):
    half = halves.shape[2]
    copies = [
        pltpu.make_async_copy(halves.at[c, n], out.at[pl.ds(c * half, half), :], sems.at[c, n])
        for c in range(2)
        for n, out in enumerate((height, albedo))
    ]
    for copy in copies:
        copy.start()
    for copy in copies:
        copy.wait()


def rows_kernel(height, albedo, own_rows, packs, sides, both, out):
    rows = height.shape[0]
    half = rows // 2
    core = lax.axis_index("img")
    lane = lane_ids(ROW)
    east = east_lanes(lane)
    wide = lane < STARTS[0] + WIDTHS[0]
    for i in range(0, half, ROW):
        at = pl.ds(i, ROW)
        west_side, east_side = sides[0, at, :], sides[1, at, :]
        both[at, :] = jnp.where(east, east_side, west_side)
        moved_e, moved_w = (
            jnp.where(wide, pltpu.roll(x, 6 * d % LANES, 1), pltpu.roll(x, 5 * d % LANES, 1))
            for x, d in ((east_side, 1), (west_side, -1))
        )
        both[pl.ds(half + i, ROW), :] = jnp.where(east, moved_e, moved_w)
    at = pl.ds(pl.multiple_of(core * (rows - ROW), ROW), ROW)
    upper = core == 0

    def edge(x, n):
        return jnp.where(upper, x[:n], x[ROW - n :])

    out[pl.ds(0, WIDTHS[0]), :] = edge(height[at, :], WIDTHS[0])
    for k in range(1, PLANES):
        if k == 1:
            plane = albedo[at, :]
        else:
            m = k - 2
            theirs = [packs[1 - core, pl.ds(half + (2 * m + t) * ROW, ROW), :] for t in range(2)]
            plane = own_rows[pl.ds(m * ROW, ROW), :] + jnp.concatenate(theirs, axis=1)
        out[pl.ds(ROW_STARTS[k], WIDTHS[k]), :] = edge(plane, WIDTHS[k])
    corner = both[at, :]
    out[pl.ds(ROW_STARTS[PLANES], ROW), :] = jnp.concatenate([corner, corner], axis=1)


def fill_kernel(height, albedo, keep, both, ends, hs, al, mo):
    rows = height.shape[0]
    own = keep.shape[1]
    core = lax.axis_index("img")

    def plane(k):
        return hs if k == 0 else al if k == 1 else mo.at[k - 2]

    first = core * (rows - own)
    place = 2 * ROW - core * ROW
    for i in range(0, own, ROW):
        src = pl.ds(pl.multiple_of(first + i, ROW), ROW)
        dst = pl.ds(pl.multiple_of(place + i, ROW), ROW)
        sides = both[src, :]
        for k in range(PLANES):
            body = height[src, :] if k == 0 else albedo[src, :] if k == 1 else keep[k - 2, pl.ds(i, ROW), :]
            ref = plane(k)
            ref[0, dst, :] = body[:, :LANES]
            ref[1, dst, :] = body[:, LANES:]
            ref[2, dst, :] = pltpu.roll(sides, LANES - STARTS[k], 1)
    dst = pl.ds(pl.multiple_of(ROW + core * own, ROW), ROW)
    sides = ends[pl.ds(ROW_STARTS[PLANES], ROW), :LANES]
    for k in range(PLANES):
        ref = plane(k)
        begin, spare = ROW_STARTS[k], ROW - WIDTHS[k]
        after = ends[pl.ds(begin, ROW), :]
        before = pltpu.roll(after, spare, 0) if k == 0 else ends[pl.ds(begin - spare, ROW), :]
        body = jnp.where(core == 0, before, after)
        ref[0, dst, :] = body[:, :LANES]
        ref[1, dst, :] = body[:, LANES:]
        ref[2, dst, :] = pltpu.roll(sides, LANES - STARTS[k], 1)


def steps_kernel(rates, hs_in, al_in, mo_in, theirs, out, hs, al, mo, gps, gqs):
    own = theirs.shape[1]
    half = out.shape[1]
    core = lax.axis_index("img")
    first_y = (lax.axis_index("gy") == 0) & (core == 0)
    last_y = (lax.axis_index("gy") == lax.axis_size("gy") - 1) & (core == 1)
    first_x = lax.axis_index("gx") == 0
    last_x = lax.axis_index("gx") == lax.axis_size("gx") - 1
    rate_h, rate_a = rates
    top = 2 * ROW
    bottom = top + half
    place = top - core * ROW
    for i in range(0, own, ROW):
        dst = pl.ds(pl.multiple_of(place + i, ROW), ROW)
        for m in range(MOMENTS):
            for t in range(2):
                mo[m, t, dst, :] += theirs[m, pl.ds(i, ROW), t * LANES : (t + 1) * LANES]

    lane = lane_ids(ROW)
    head = lane == 0
    tail = lane == LANES - 1
    wall_w = head & first_x
    wall_e = tail & last_x

    def beside(blocks, sign):
        fore = [pltpu.roll(b, LANES - 1, 1) for b in blocks]
        back = [pltpu.roll(b, 1, 1) for b in blocks]
        easts = [jnp.where(tail, fore[(t + 1) % 3], fore[t]) for t in range(3)]
        wests = [jnp.where(head, back[(t + 2) % 3], back[t]) for t in range(3)]
        easts[1] = jnp.where(wall_e, sign * blocks[1], easts[1])
        wests[0] = jnp.where(wall_w, sign * blocks[0], wests[0])
        return easts, wests

    def borders(ref, sign):
        @pl.when(first_y)
        def _():
            ref[:, pl.ds(top - 1, 1), :] = sign * ref[:, pl.ds(top, 1), :]

        @pl.when(last_y)
        def _():
            ref[:, pl.ds(bottom, 1), :] = sign * ref[:, pl.ds(bottom - 1, 1), :]

    def slopes(i, carry):
        base = pl.multiple_of(i * ROW, ROW)
        at = pl.ds(pl.multiple_of(base + ROW, ROW), ROW)
        easts, wests = beside([hs[t, at, :] for t in range(3)], 1.0)
        for t in range(3):
            p = 0.5 * (easts[t] - wests[t])
            q = 0.5 * (hs[t, pl.ds(base + ROW + 1, ROW), :] - hs[t, pl.ds(base + ROW - 1, ROW), :])
            scale = lax.rsqrt(1.0 + p * p + q * q)
            xx, xy, xz, yy, yz, zz, vx, vy, vz = [mo[m, t, at, :] for m in range(MOMENTS)]
            alb = al[t, at, :]
            lit = alb * scale
            gx = lit * (xz - p * xx - q * xy) - vx
            gy = lit * (yz - p * xy - q * yy) - vy
            gz = lit * (zz - p * xz - q * yz) - vz
            grad_a = scale * (gz - p * gx - q * gy)
            turn = scale * grad_a
            bend = 0.3 - lit * turn
            gps[t, at, :] = p * bend - lit * gx
            gqs[t, at, :] = q * bend - lit * gy
            al[t, at, :] = alb - rate_a * grad_a
        return carry

    def descend(i, carry):
        base = pl.multiple_of(i * ROW, ROW)
        at = pl.ds(pl.multiple_of(base + ROW, ROW), ROW)
        easts, wests = beside([gps[t, at, :] for t in range(3)], -1.0)
        for t in range(3):
            grad_h = 0.5 * (wests[t] - easts[t]) + 0.5 * (
                gqs[t, pl.ds(base + ROW - 1, ROW), :] - gqs[t, pl.ds(base + ROW + 1, ROW), :]
            )
            hs[t, at, :] = hs[t, at, :] - rate_h * grad_h
        return carry

    blocks = half // ROW + 2
    borders(hs, 1.0)

    def iterate(n, carry):
        lax.fori_loop(0, blocks, slopes, 0, unroll=blocks)
        borders(gqs, -1.0)
        lax.fori_loop(0, blocks, descend, 0, unroll=blocks)
        borders(hs, 1.0)
        return carry

    lax.fori_loop(0, ITERS, iterate, 0)
    center = pl.ds(top, half)
    for t in range(2):
        lanes = pl.ds(t * LANES, LANES)
        out[0, :, lanes] = hs[t, center, :]
        out[1, :, lanes] = al[t, center, :]


def pair_groups(sizes):
    ny, nx = sizes

    def flat(y, x, core):
        return (y * nx + x) * 2 + core

    groups = [[flat(y, x, 1), flat(y, x + 1, 0)] for y in range(ny) for x in range(nx - 1)]
    for y in range(0, ny, 2):
        groups += [[flat(y, x, core), flat(y + 1, x, core)] for x, core in ((0, 0), (nx - 1, 1))]
    return groups


def from_next(x, core):
    groups = pair_groups((lax.axis_size("gy"), lax.axis_size("gx")))
    both = lax.all_gather(x, AXES, axis_index_groups=groups)
    return lax.dynamic_index_in_dim(both, core, 0, keepdims=False)


def neighbours(sizes):
    ny, nx = sizes

    def flat(y, x, core):
        return (y * nx + x) * 2 + core

    pairs = [(flat(y, x, 1), flat(y + 1, x, 0)) for y in range(ny - 1) for x in range(nx)]
    return pairs + [(b, a) for a, b in pairs]


VMEM = pl.BlockSpec(memory_space=pltpu.VMEM)
HBM = pl.BlockSpec(memory_space=pltpu.HBM)


def in_vmem(*args):
    return tuple(pltpu.with_memory_space_constraint(x, pltpu.VMEM) for x in args)


def cost(mib):
    return pl.CostEstimate(flops=1 << 20, bytes_accessed=mib << 20, transcendentals=0)


def params(mib):
    return pltpu.CompilerParams(vmem_limit_bytes=mib << 20)


def run_edges(sun_index, expo_index, azimuth, elevation, exposure, heights, albedo, images, weights):
    rows, cols = heights.shape
    half = rows // 2
    tiles = [x.reshape(*x.shape[:-2], 2, half, cols) for x in (heights, albedo, images, weights)]
    args = [
        pltpu.with_memory_space_constraint(x, pltpu.HBM)
        for x in (sun_index, expo_index, azimuth, elevation, exposure, *tiles)
    ]
    out = pl.pallas_call(
        edges_kernel,
        out_shape=tuple(pltpu.VMEM(x.shape, x.dtype) for x in tiles)
        + (
            pltpu.VMEM((MOMENTS, ROW, LANES), F32),
            pltpu.VMEM((half, LANES), F32),
            pltpu.VMEM((MOMENTS * ROW, cols), F32),
            pltpu.VMEM((half + 2 * MOMENTS * ROW, LANES), F32),
        ),
        in_specs=[HBM] * len(args),
        out_specs=(VMEM,) * 8,
        scratch_shapes=[pltpu.SMEM(x.shape, x.dtype) for x in args[:5]]
        + [pltpu.VMEM((2, half, LANES), F32), pltpu.VMEM((2, MOMENTS, ROW, cols), F32)]
        + [pltpu.SemaphoreType.DMA((5,)), pltpu.SemaphoreType.DMA((CHUNKS, 4))],
        compiler_params=params(8),
        name="edges",
    )(*args)
    return tuple(x.reshape(*x.shape[:-3], rows, cols) for x in out[:4]) + out[4:]


def run_moments(images, weights, tables):
    _, rows, cols = images.shape
    part = pltpu.VMEM((MOMENTS, rows // 2 + ROW, cols), F32)
    return pl.pallas_call(
        moments_kernel,
        out_shape=(part, part),
        in_specs=[VMEM] * 3,
        out_specs=(VMEM, VMEM),
        scratch_shapes=[pltpu.VMEM((MOMENTS, rows, cols), F32)],
        compiler_params=params(8),
        cost_estimate=cost(4),
        name="moments",
    )(*in_vmem(images, weights, tables))


def run_rows(heights, albedo, own_rows, packs, sides):
    rows, cols = heights.shape
    return pl.pallas_call(
        rows_kernel,
        out_shape=(pltpu.VMEM((rows, LANES), F32), pltpu.VMEM((ROW_STARTS[PLANES] + ROW, cols), F32)),
        in_specs=[VMEM] * 5,
        out_specs=(VMEM,) * 2,
        compiler_params=params(8),
        name="edge_rows",
    )(*in_vmem(heights, albedo, own_rows, packs, sides))


def frame(rows):
    return (3, rows // 2 + 4 * ROW, LANES)


def run_fill(heights, albedo, keep, both, ends):
    block = pltpu.VMEM(frame(heights.shape[0]), F32)
    return pl.pallas_call(
        fill_kernel,
        out_shape=(block, block, pltpu.VMEM((MOMENTS, *block.shape), F32)),
        in_specs=[VMEM] * 5,
        out_specs=(VMEM,) * 3,
        compiler_params=params(8),
        cost_estimate=pl.CostEstimate(flops=1 << 34, bytes_accessed=1 << 20, transcendentals=0),
        name="fill",
    )(*in_vmem(heights, albedo, keep, both, ends))


def run_steps(total, hs, al, mo, theirs):
    _, tall, _ = hs.shape
    half = tall - 4 * ROW
    block = pltpu.VMEM(hs.shape, F32)
    return pl.pallas_call(
        functools.partial(steps_kernel, (0.2 / total, 0.5 / total)),
        out_shape=(pltpu.VMEM((2, half, 2 * LANES), F32), block, block, pltpu.VMEM(mo.shape, F32)),
        in_specs=[VMEM] * 4,
        out_specs=(VMEM,) * 4,
        scratch_shapes=[block, block],
        input_output_aliases={0: 1, 1: 2, 2: 3},
        compiler_params=params(8),
        name="gradient_steps",
    )(*in_vmem(hs, al, mo, theirs))[0]


def run_place(halves):
    _, _, half, cols = halves.shape
    out = jax.ShapeDtypeStruct((2 * half, cols), F32)
    return pl.pallas_call(
        place_kernel,
        out_shape=(out, out),
        in_specs=[VMEM],
        out_specs=(HBM, HBM),
        scratch_shapes=[pltpu.SemaphoreType.DMA((2, 2))],
        compiler_params=params(8),
        name="place",
    )(*in_vmem(halves))


def shards(
    heights, albedo, images, weights, sun_index, expo_index, sun_azimuth, sun_elevation, exposure
):
    total = images.shape[0] * lax.axis_size("img")
    core = lax.axis_index("img")
    heights, albedo, images, weights, tables, own_fold, own_rows, pack = run_edges(
        sun_index, expo_index, sun_azimuth, sun_elevation, exposure, heights, albedo, images, weights
    )
    packs = lax.all_gather(pack, "img")
    fold = own_fold + lax.dynamic_index_in_dim(packs, 1 - core, 0, keepdims=False)[: own_fold.shape[0]]
    sides = lax.all_gather(from_next(fold, core), "img")
    both, ends = run_rows(heights, albedo, own_rows, packs, sides)
    ends, images = lax.optimization_barrier((ends, images))
    ends = lax.ppermute(ends, AXES, neighbours((lax.axis_size("gy"), lax.axis_size("gx"))))
    keep, send = run_moments(images, weights, tables)
    theirs = lax.ppermute(send, "img", [(0, 1), (1, 0)])
    halves = run_steps(total, *run_fill(heights, albedo, keep, both, ends), theirs)
    return run_place(lax.all_gather(halves, "img"))


def solution(mesh):
    return jax.shard_map(
        shards,
        mesh=mesh,
        in_specs=(
            P("gy", "gx"),
            P("gy", "gx"),
            P("img", "gy", "gx"),
            P("img", "gy", "gx"),
            P("img"),
            P("img"),
            P(),
            P(),
            P(),
        ),
        out_specs=(P("gy", "gx"), P("gy", "gx")),
        check_vma=False,
    )
```

time: 37.4 us -> 35.6 us (0.952)
  blocking collectives: 27.2 us -> 18.1 us
  starting transfers between devices: 2.26 us -> 7.95 us
  waiting for transfers between devices: 0.01 us -> 2.2 us
  other arithmetic: 1.47 us -> 0.01 us
  Pallas kernels: 5.53 us -> 6.53 us
    all_gather x2 -> x1, blocking collectives: 10.2 us -> 4.94 us  [from_next(): both = lax.all_gather(x, AXES, axis_index_groups=groups)]
    all_gather x1, blocking collectives: 5.79 us -> 2.18 us  [shards(): return run_place(lax.all_gather(halves, 'img'))]
    ppermute x0 -> x1, starting transfers between devices: none -> 3.44 us  [shards(): lax.ppermute(ends, AXES, neighbours((lax.axis_size('gy'), lax.axis_size('...]
    ppermute x1, starting transfers between devices: 2.26 us -> 4.51 us  [shards(): theirs = lax.ppermute(send, 'img', [(0, 1), (1, 0)])]
    ppermute x1, waiting for transfers between devices: 0.01 us -> 2.2 us  [shards(): theirs = lax.ppermute(send, 'img', [(0, 1), (1, 0)])]
    add x1, other arithmetic: 1.46 us -> 0.01 us  [shards(): own_fold + lax.dynamic_index_in_dim(packs, 1 - core, 0, keepdims=False)[:...]
    pallas_call x2 -> x4, Pallas kernels: 2.46 us -> 3.52 us  [the longest x1 2.08 us: run_edges(): pl.pallas_call(edges_kernel, out_shape=tuple((pltpu.VMEM(x.shape, x.dtype...]
  transfers between devices with their start and end apart: 1 -> 2, of which waited for: 0 -> 1; matrix products, arithmetic and copies ran while one was open for 0% -> 0% of each run, Pallas kernels for 0% -> 4%
where the time goes in v3:
time: 35.6 us; the launch traced here: 35.5 us
  blocking collectives  18.1 us (51%)
  starting transfers between devices  7.95 us (22%)
  Pallas kernels  6.53 us (18%)
  waiting for transfers between devices  2.2 us (6%)
  between operations  0.7 us (2%)
    all_gather x1, blocking collectives, shards(): sides = lax.all_gather(from_next(fold, core), 'img')  8.61 us
    all_gather x1, blocking collectives, from_next(): both = lax.all_gather(x, AXES, axis_index_groups=groups)  4.94 us
    ppermute x1, starting transfers between devices, shards(): theirs = lax.ppermute(send, 'img', [(0, 1), (1, 0)])  4.51 us
    ppermute x1, starting transfers between devices, shards(): lax.ppermute(ends, AXES, neighbours((lax.axis_size('gy'), lax.axis_size('...  3.44 us
    all_gather x1, blocking collectives, shards(): packs = lax.all_gather(pack, 'img')  2.32 us
    ppermute x1, waiting for transfers between devices, shards(): theirs = lax.ppermute(send, 'img', [(0, 1), (1, 0)])  2.2 us
    pallas_call x1, Pallas kernels, run_steps(): pl.pallas_call(functools.partial(steps_kernel, (0.2 / total, 0.5 / total)...  2.19 us
    all_gather x1, blocking collectives, shards(): return run_place(lax.all_gather(halves, 'img'))  2.18 us
  transfers between devices with their start and end apart: 2, of which 1 were waited for; matrix products, arithmetic and copies ran while one was open for 0% of the time, Pallas kernels for 4%

profile of v3, /device:TPU:7, one launch (start us, length us, event | category | flops | bytes accessed | tf_op | source)
XLA Modules:
  0.0 35.5 jit_solution(1321560671077585612)
XLA Ops:
  0.6 2.1 %edges.1 = (f32[2,128,256]{2,1,0:T(8,128)S(1)}, f32[2,128,256]{2,1,0:T(8,128)S(1)}, bf16[4,2,128,256]{3,2,1,0:T(8,128)(2,1)S(1)}, bf16[4,2,128,256]{3,2,1,0:T(8,...) custom-call(s32[4]{0:T(128)} %sun_index_hbm.1, ...), custom_call_target="tpu_custom_call" | custom-call | tf_op jit(solution)/shard_map/edges/pallas_call | solution.py:377
  2.7 2.3 %all-gather = f32[544,128]{1,0:T(8,128)S(1)} all-gather(f32[272,128]{1,0:T(8,128)S(1)} %get-tuple-element.23), channel_id=2, replica_groups=mesh['gy'=16,'gx'=16,'img'=2] {'img'}, dimensions={0}, use_global_device_ids=true | all-gather | bytes 417792 | tf_op jit(solution)/shard_map/all_gather | solution.py:479
  5.1 4.9 %all-gather.1 = f32[256,128]{1,0:T(8,128)S(1)} all-gather(f32[128,128]{1,0:T(8,128)S(1)} %fusion), channel_id=3, replica_groups={{1,2},{3,4},{5,6},{7,8},{9,10},{11,12},{13,14},{15,16},{17,18},{19,20},..., dimensions={0}, use_global_device_ids=true | all-gather | bytes 196608 | tf_op jit(solution)/shard_map/all_gather | solution.py:339
  10.0 8.6 %all_gather.26.sides = f32[2,128,128]{2,1,0:T(8,128)S(1)} all-gather(f32[1,128,128]{2,1,0:T(8,128)S(1)} %constant_dynamic-slice_fusion), channel_id=1, replica_groups=mesh['gy'=16,'gx'=16,'img'=2] {'img'}, dimensions={0}, use_global_device_ids=true | all-gather | bytes 196608 | tf_op jit(solution)/shard_map/all_gather | solution.py:481
  18.6 0.1 edge_rows.1
  18.8 3.4 %collective-permute-start = (f32[64,256]{1,0:T(8,128)S(1)}, f32[64,256]{1,0:T(8,128)S(1)}, u32[]{:S(2)}, u32[]{:S(2)}) collective-permute-start(f32[64,256]{1,0:T(8,128)S(1)} %get-tuple-element.32), channel_id=1, source_target_pairs={{1,32},{3,34},{5,36},{7,38},{9,40},{11,42},{13,44},{15,46},{17,48}... | collective-permute-start | bytes 196616 | tf_op jit(solution)/shard_map/ppermute | solution.py:484
  22.2 1.0 %moments.1 = (f32[9,136,256]{2,1,0:T(8,128)S(1)}, f32[9,136,256]{2,1,0:T(8,128)S(1)}) custom-call(bf16[4,256,256]{2,1,0:T(8,128)(2,1)S(1)} %bitcast.18, bf16[4,256,256]{2,1,0:T(8,128)(2,1)S(1)} %bitcast.19, f32[9,8,128]{2,1,0:T(8,128)S(1)} %get-tuple-element.29.tables), custom_call_target="tpu_custom_call" | custom-call | flops 1048576 | bytes 4194304 | tf_op jit(solution)/shard_map/moments/pallas_call | solution.py:400
  23.2 4.5 %collective-permute-start.1 = (f32[9,136,256]{2,1,0:T(8,128)S(1)}, f32[9,136,256]{2,1,0:T(8,128)S(1)}, u32[]{:S(2)}, u32[]{:S(2)}) collective-permute-start(f32[9,136,256]{2,1,0:T(8,128)S(1)} %get-tuple-element.36), channel_id=1, source_target_pairs={{0,1},{1,0},{2,3},{3,2},{4,5},{5,4},{6,7},{7,6},{8,9},{9,8},{10,11... | collective-permute-start | bytes 3760136 | tf_op jit(solution)/shard_map/ppermute | solution.py:486
  27.7 0.0 collective-permute-done.ends
  27.7 0.3 fill.1
  28.1 2.2 %collective-permute-done.1.theirs = f32[9,136,256]{2,1,0:T(8,128)S(1)} collective-permute-done((f32[9,136,256]{2,1,0:T(8,128)S(1)}, f32[9,136,256]{2,1,0:T(8,128)S(1)}, u32[]{:S(2)}, u32[]{:S(2)}) %collective-permute-start.1) | collective-permute-done | bytes 1253408 | tf_op jit(solution)/shard_map/ppermute | solution.py:486
  30.3 2.2 %gradient_steps.1 = (f32[2,128,256]{2,1,0:T(8,128)S(1)}, f32[3,160,128]{2,1,0:T(8,128)S(1)}, f32[3,160,128]{2,1,0:T(8,128)S(1)}, f32[9,3,160,128]{3,2,1,0:T(8,128)S(1)}) custom-call(f32[3,160,128]{2,1,0:T(8,128)S(1)} %get-tuple-element.33.hs_in, ...), custom_call_target="tpu_custom_call", output_to_operand_aliasing={{1}: (0, {}), {2}: (1, {}), {3}: (2, {})} | custom-call | tf_op jit(solution)/shard_map/gradient_steps/pallas_call | solution.py:445
  32.5 2.2 %all-gather.2 = f32[4,128,256]{2,1,0:T(8,128)S(1)} all-gather(f32[2,128,256]{2,1,0:T(8,128)S(1)} %get-tuple-element.37), channel_id=4, replica_groups=mesh['gy'=16,'gx'=16,'img'=2] {'img'}, dimensions={0}, use_global_device_ids=true | all-gather | bytes 786432 | tf_op jit(solution)/shard_map/all_gather | solution.py:488
  34.6 0.8 %place.1 = (f32[256,256]{1,0:T(8,128)}, f32[256,256]{1,0:T(8,128)}) custom-call(f32[2,2,128,256]{3,2,1,0:T(8,128)S(1)} %bitcast.15), custom_call_target="tpu_custom_call" | custom-call | tf_op jit(solution)/shard_map/place/pallas_call | solution.py:460
  (2 shorter events, 0.0 us)
Async XLA Ops:
  18.8 8.9 %collective-permute-start = (f32[64,256]{1,0:T(8,128)S(1)}, f32[64,256]{1,0:T(8,128)S(1)}, u32[]{:S(2)}, u32[]{:S(2)}) collective-permute-start(f32[64,256]{1,0:T(8,128)S(1)} %get-tuple-element.32), channel_id=1, source_target_pairs={{1,32},{3,34},{5,36},{7,38},{9,40},{11,42},{13,44},{15,46},{17,48}... | collective-permute-start | bytes 196616 | tf_op jit(solution)/shard_map/ppermute | solution.py:484
  23.2 7.1 %collective-permute-start.1 = (f32[9,136,256]{2,1,0:T(8,128)S(1)}, f32[9,136,256]{2,1,0:T(8,128)S(1)}, u32[]{:S(2)}, u32[]{:S(2)}) collective-permute-start(f32[9,136,256]{2,1,0:T(8,128)S(1)} %get-tuple-element.36), channel_id=1, source_target_pairs={{0,1},{1,0},{2,3},{3,2},{4,5},{5,4},{6,7},{7,6},{8,9},{9,8},{10,11... | collective-permute-start | bytes 3760136 | tf_op jit(solution)/shard_map/ppermute | solution.py:486

commit v4 on v3

--- a/solution.py
+++ b/solution.py
@@ -11,7 +11,7 @@
 AXES = ("gy", "gx", "img")
 LANES = 128
 ROW = 8
-CHUNKS = 4
+CHUNKS = 2
 MOMENTS = 9
 PLANES = 2 + MOMENTS
 WIDTHS = (6,) + (5,) * (PLANES - 1)
@@ -53,10 +53,13 @@
         large.append([
             pltpu.make_async_copy(weights_hbm.at[:, :, at, :], weights.at[:, :, at, :], large_sems.at[c, 0]),
             pltpu.make_async_copy(images_hbm.at[:, :, at, :], images.at[:, :, at, :], large_sems.at[c, 1]),
-            pltpu.make_async_copy(height_hbm.at[:, at, :], height.at[:, at, :], large_sems.at[c, 2]),
-            pltpu.make_async_copy(albedo_hbm.at[:, at, :], albedo.at[:, at, :], large_sems.at[c, 3]),
         ])
-        for copy in large[c]:
+    large.append([
+        pltpu.make_async_copy(height_hbm, height, large_sems.at[CHUNKS, 0]),
+        pltpu.make_async_copy(albedo_hbm, albedo, large_sems.at[CHUNKS, 1]),
+    ])
+    for copies in large:
+        for copy in copies:
             copy.start()
     for copy in small:
         copy.wait()
@@ -75,6 +78,11 @@
     factors = (sx * sx, sx * sy, sx * sz, sy * sy, sy * sz, sz * sz, sx, sy, sz)
     for m, factor in enumerate(factors):
         tables[m] = factor
+    lane = lane_ids(ROW)
+    block = jnp.zeros((ROW, LANES), F32)
+    for m, factor in enumerate(factors):
+        block = jnp.where(lane == m, factor, block)
+    pack[pl.ds(half + 2 * MOMENTS * ROW, ROW), :] = block
     step = 16
     lane = lane_ids(step)
 
@@ -87,35 +95,44 @@
     def ends(x):
         return jnp.where(lane < LANES // 2, x[:, :LANES], x[:, -LANES:])
 
+    def fold(planes, first, west, east):
+        for above, below, start, width in zip(*planes, STARTS[first:], WIDTHS[first:]):
+            low = (lane >= start - width) & (lane < start)
+            high = (lane >= start) & (lane < start + width)
+            above = pltpu.roll(above, start, 1)
+            west = jnp.where(high, above, jnp.where(low, pltpu.roll(below, start - width, 1), west))
+            east = jnp.where(low, above, jnp.where(high, pltpu.roll(below, start + width, 1), east))
+        return west, east
+
+    def edge_rows(side, first):
+        acc = sums(side, pl.ds(first, step), lambda x: x)
+        for m in range(MOMENTS):
+            ends_of_rows[side, m] = acc[m][:ROW] if side == 0 else acc[m][-ROW:]
+
+    zero = jnp.zeros((step, LANES), F32)
     for c in range(CHUNKS):
         for copy in large[c]:
             copy.wait()
         for i in range(c * part, (c + 1) * part, step):
             at = pl.ds(i, step)
-            upper, lower = (
-                [ends(0.5 * height[s, at, :]), ends(0.5 * albedo[s, at, :])] + sums(s, at, ends) for s in range(2)
-            )
-            west = jnp.zeros((step, LANES), F32)
-            east = jnp.zeros((step, LANES), F32)
-            for start, width, above, below in zip(STARTS, WIDTHS, upper, lower):
-                low = (lane >= start - width) & (lane < start)
-                high = (lane >= start) & (lane < start + width)
-                above = pltpu.roll(above, start, 1)
-                west = jnp.where(high, above, jnp.where(low, pltpu.roll(below, start - width, 1), west))
-                east = jnp.where(low, above, jnp.where(high, pltpu.roll(below, start + width, 1), east))
-            folds[0, at, :] = west
-            folds[1, at, :] = east
-    for side, first in enumerate((0, half - step)):
-        acc = sums(side, pl.ds(first, step), lambda x: x)
-        for m in range(MOMENTS):
-            ends_of_rows[side, m] = acc[m][:ROW] if side == 0 else acc[m][-ROW:]
+            folds[0, at, :], folds[1, at, :] = fold([sums(s, at, ends) for s in range(2)], 2, zero, zero)
+        if c == 0:
+            edge_rows(0, 0)
+        if c == CHUNKS - 1:
+            edge_rows(1, half - step)
     core = lax.axis_index("img")
-    own_fold[...] = folds[core]
-    pack[pl.ds(0, half), :] = folds[1 - core]
     for m in range(MOMENTS):
         own_rows[pl.ds(m * ROW, ROW), :] = ends_of_rows[core, m]
         for t in range(2):
             pack[pl.ds(half + (2 * m + t) * ROW, ROW), :] = ends_of_rows[1 - core, m, :, t * LANES : (t + 1) * LANES]
+    for copy in large[CHUNKS]:
+        copy.wait()
+    for i in range(0, half, step):
+        at = pl.ds(i, step)
+        planes = [[ends(0.5 * height[s, at, :]), ends(0.5 * albedo[s, at, :])] for s in range(2)]
+        west, east = fold(planes, 0, folds[0, at, :], folds[1, at, :])
+        own_fold[at, :] = jnp.where(core == 0, west, east)
+        pack[at, :] = jnp.where(core == 0, east, west)
 
 
 def add_moments(weight, image, count, factor):
@@ -129,23 +146,47 @@
     return acc
 
 
-def moments_kernel(images, weights, tables, keep, send, sums):
-    count, rows, _ = images.shape
+def part_rows(core, half):
     step = 16
-    for i in range(0, rows, step):
-        at = pl.ds(i, step)
+    near = pl.multiple_of(core * (half - step), step)
+    yield 1 - core, pl.ds(near, step), None
+    for i in range(0, half, step):
+        yield core, pl.ds(i, step), pl.ds(ROW + i, step)
+
+
+def put(out, plane, dst, value, core):
+    if dst is None:
+        out[plane, pl.ds(0, ROW), :] = jnp.where(core == 0, value[:ROW], value[-ROW:])
+    else:
+        out[plane, dst, :] = value
+
+
+def sent_kernel(images, weights, tables, out):
+    count, _, half, _ = images.shape
+    core = 1 - lax.axis_index("img")
+    for s, at, dst in part_rows(core, half):
+        acc = [None] * 3
+        for k in range(count):
+            w = weights[k, s, at, :].astype(F32)
+            put(out, k, dst, w, core)
+            u = w * images[k, s, at, :].astype(F32)
+            for m in range(3):
+                term = u * tables[6 + m, k : k + 1, :1]
+                acc[m] = term if k == 0 else acc[m] + term
+        for m in range(3):
+            put(out, count + m, dst, acc[m], core)
+
+
+def own_kernel(images, weights, tables, out):
+    count, _, half, _ = images.shape
+    core = lax.axis_index("img")
+    for s, at, dst in part_rows(core, half):
         acc = add_moments(
-            lambda k: weights[k, at, :].astype(F32), lambda k: images[k, at, :].astype(F32), count,
+            lambda k: weights[k, s, at, :].astype(F32), lambda k: images[k, s, at, :].astype(F32), count,
             lambda m, k: tables[m, k : k + 1, :1]
         )
         for m in range(MOMENTS):
-            sums[m, at, :] = acc[m]
-    core = lax.axis_index("img")
-    for out, first in ((keep, core), (send, 1 - core)):
-        first = first * (rows - out.shape[1])
-        for m in range(MOMENTS):
-            for i in range(0, out.shape[1], ROW):
-                out[m, pl.ds(i, ROW), :] = sums[m, pl.ds(pl.multiple_of(first + i, ROW), ROW), :]
+            put(out, m, dst, acc[m], core)
 
 
 def place_kernel(halves, height, albedo, sems):
@@ -196,27 +237,32 @@
     out[pl.ds(ROW_STARTS[PLANES], ROW), :] = jnp.concatenate([corner, corner], axis=1)
 
 
+def inner_row(core, half):
+    return ROW + (1 - core) * (half + ROW)
+
+
 def fill_kernel(height, albedo, keep, both, ends, hs, al, mo):
     rows = height.shape[0]
-    own = keep.shape[1]
     core = lax.axis_index("img")
 
     def plane(k):
         return hs if k == 0 else al if k == 1 else mo.at[k - 2]
 
-    first = core * (rows - own)
-    place = 2 * ROW - core * ROW
-    for i in range(0, own, ROW):
-        src = pl.ds(pl.multiple_of(first + i, ROW), ROW)
-        dst = pl.ds(pl.multiple_of(place + i, ROW), ROW)
+    half = rows // 2
+    inner = core * (half - ROW) + (1 - core) * half
+    for i in range(-ROW, half, ROW):
+        if i < 0:
+            src, dst = pl.ds(pl.multiple_of(inner, ROW), ROW), pl.ds(pl.multiple_of(inner_row(core, half), ROW), ROW)
+        else:
+            src, dst = pl.ds(pl.multiple_of(core * half + i, ROW), ROW), pl.ds(2 * ROW + i, ROW)
         sides = both[src, :]
         for k in range(PLANES):
-            body = height[src, :] if k == 0 else albedo[src, :] if k == 1 else keep[k - 2, pl.ds(i, ROW), :]
+            body = height[src, :] if k == 0 else albedo[src, :] if k == 1 else keep[k - 2, pl.ds(ROW + i, ROW), :]
             ref = plane(k)
             ref[0, dst, :] = body[:, :LANES]
             ref[1, dst, :] = body[:, LANES:]
             ref[2, dst, :] = pltpu.roll(sides, LANES - STARTS[k], 1)
-    dst = pl.ds(pl.multiple_of(ROW + core * own, ROW), ROW)
+    dst = pl.ds(pl.multiple_of(inner_row(1 - core, half), ROW), ROW)
     sides = ends[pl.ds(ROW_STARTS[PLANES], ROW), :LANES]
     for k in range(PLANES):
         ref = plane(k)
@@ -229,8 +275,7 @@
         ref[2, dst, :] = pltpu.roll(sides, LANES - STARTS[k], 1)
 
 
-def steps_kernel(rates, hs_in, al_in, mo_in, theirs, out, hs, al, mo, gps, gqs):
-    own = theirs.shape[1]
+def steps_kernel(rates, hs_in, al_in, mo_in, theirs, packs, out, hs, al, mo, gps, gqs):
     half = out.shape[1]
     core = lax.axis_index("img")
     first_y = (lax.axis_index("gy") == 0) & (core == 0)
@@ -240,12 +285,27 @@
     rate_h, rate_a = rates
     top = 2 * ROW
     bottom = top + half
-    place = top - core * ROW
-    for i in range(0, own, ROW):
-        dst = pl.ds(pl.multiple_of(place + i, ROW), ROW)
+    hs[...] = 0.5 * hs_in[...]
+    al[...] = al_in[...]
+    outer = pl.ds(pl.multiple_of(inner_row(1 - core, half), ROW), ROW)
+    inner = pl.ds(pl.multiple_of(inner_row(core, half), ROW), ROW)
+    count = theirs.shape[0] - 3
+    table = packs[1 - core, packs.shape[1] - ROW :, :]
+    factors = [[jnp.broadcast_to(table[k : k + 1, m : m + 1], (ROW, LANES)) for k in range(count)] for m in range(6)]
+    for t in range(2):
+        lanes = slice(t * LANES, (t + 1) * LANES)
+        for i in range(-ROW, half, ROW):
+            src = pl.ds(ROW + i, ROW)
+            at = inner if i < 0 else pl.ds(top + i, ROW)
+            w = [theirs[k, src, lanes] for k in range(count)]
+            for m in range(MOMENTS):
+                if m < 6:
+                    extra = sum((w[k] * factors[m][k] for k in range(1, count)), w[0] * factors[m][0])
+                else:
+                    extra = theirs[count + m - 6, src, lanes]
+                mo[m, t, at, :] = mo_in[m, t, at, :] + extra
         for m in range(MOMENTS):
-            for t in range(2):
-                mo[m, t, dst, :] += theirs[m, pl.ds(i, ROW), t * LANES : (t + 1) * LANES]
+            mo[m, t, outer, :] = mo_in[m, t, outer, :]
 
     lane = lane_ids(ROW)
     head = lane == 0
@@ -276,10 +336,10 @@
         at = pl.ds(pl.multiple_of(base + ROW, ROW), ROW)
         easts, wests = beside([hs[t, at, :] for t in range(3)], 1.0)
         for t in range(3):
-            p = 0.5 * (easts[t] - wests[t])
-            q = 0.5 * (hs[t, pl.ds(base + ROW + 1, ROW), :] - hs[t, pl.ds(base + ROW - 1, ROW), :])
+            p = easts[t] - wests[t]
+            q = hs[t, pl.ds(base + ROW + 1, ROW), :] - hs[t, pl.ds(base + ROW - 1, ROW), :]
             scale = lax.rsqrt(1.0 + p * p + q * q)
-            xx, xy, xz, yy, yz, zz, vx, vy, vz = [mo[m, t, at, :] for m in range(MOMENTS)]
+            xx, xy, xz, yy, yz, zz, vx, vy, vz = [(mo if t < 2 else mo_in)[m, t, at, :] for m in range(MOMENTS)]
             alb = al[t, at, :]
             lit = alb * scale
             gx = lit * (xz - p * xx - q * xy) - vx
@@ -298,27 +358,22 @@
         at = pl.ds(pl.multiple_of(base + ROW, ROW), ROW)
         easts, wests = beside([gps[t, at, :] for t in range(3)], -1.0)
         for t in range(3):
-            grad_h = 0.5 * (wests[t] - easts[t]) + 0.5 * (
-                gqs[t, pl.ds(base + ROW - 1, ROW), :] - gqs[t, pl.ds(base + ROW + 1, ROW), :]
-            )
-            hs[t, at, :] = hs[t, at, :] - rate_h * grad_h
+            fall = (wests[t] - easts[t]) + (gqs[t, pl.ds(base + ROW - 1, ROW), :] - gqs[t, pl.ds(base + ROW + 1, ROW), :])
+            hs[t, at, :] = hs[t, at, :] - (0.25 * rate_h) * fall
         return carry
 
     blocks = half // ROW + 2
     borders(hs, 1.0)
 
-    def iterate(n, carry):
+    for _ in range(ITERS):
         lax.fori_loop(0, blocks, slopes, 0, unroll=blocks)
         borders(gqs, -1.0)
         lax.fori_loop(0, blocks, descend, 0, unroll=blocks)
         borders(hs, 1.0)
-        return carry
-
-    lax.fori_loop(0, ITERS, iterate, 0)
     center = pl.ds(top, half)
     for t in range(2):
         lanes = pl.ds(t * LANES, LANES)
-        out[0, :, lanes] = hs[t, center, :]
+        out[0, :, lanes] = 2.0 * hs[t, center, :]
         out[1, :, lanes] = al[t, center, :]
 
 
@@ -381,31 +436,29 @@
             pltpu.VMEM((MOMENTS, ROW, LANES), F32),
             pltpu.VMEM((half, LANES), F32),
             pltpu.VMEM((MOMENTS * ROW, cols), F32),
-            pltpu.VMEM((half + 2 * MOMENTS * ROW, LANES), F32),
+            pltpu.VMEM((half + 2 * MOMENTS * ROW + ROW, LANES), F32),
         ),
         in_specs=[HBM] * len(args),
         out_specs=(VMEM,) * 8,
         scratch_shapes=[pltpu.SMEM(x.shape, x.dtype) for x in args[:5]]
         + [pltpu.VMEM((2, half, LANES), F32), pltpu.VMEM((2, MOMENTS, ROW, cols), F32)]
-        + [pltpu.SemaphoreType.DMA((5,)), pltpu.SemaphoreType.DMA((CHUNKS, 4))],
+        + [pltpu.SemaphoreType.DMA((5,)), pltpu.SemaphoreType.DMA((CHUNKS + 1, 2))],
         compiler_params=params(8),
         name="edges",
     )(*args)
-    return tuple(x.reshape(*x.shape[:-3], rows, cols) for x in out[:4]) + out[4:]
-
-
-def run_moments(images, weights, tables):
-    _, rows, cols = images.shape
-    part = pltpu.VMEM((MOMENTS, rows // 2 + ROW, cols), F32)
+    return tuple(x.reshape(rows, cols) for x in out[:2]) + out[2:]
+
+
+def run_moments(kernel, planes, images, weights, tables):
+    _, _, half, cols = images.shape
     return pl.pallas_call(
-        moments_kernel,
-        out_shape=(part, part),
+        kernel,
+        out_shape=pltpu.VMEM((planes, half + ROW, cols), F32),
         in_specs=[VMEM] * 3,
-        out_specs=(VMEM, VMEM),
-        scratch_shapes=[pltpu.VMEM((MOMENTS, rows, cols), F32)],
+        out_specs=VMEM,
         compiler_params=params(8),
         cost_estimate=cost(4),
-        name="moments",
+        name=kernel.__name__,
     )(*in_vmem(images, weights, tables))
 
 
@@ -438,20 +491,19 @@
     )(*in_vmem(heights, albedo, keep, both, ends))
 
 
-def run_steps(total, hs, al, mo, theirs):
+def run_steps(total, hs, al, mo, theirs, packs):
     _, tall, _ = hs.shape
     half = tall - 4 * ROW
     block = pltpu.VMEM(hs.shape, F32)
     return pl.pallas_call(
         functools.partial(steps_kernel, (0.2 / total, 0.5 / total)),
-        out_shape=(pltpu.VMEM((2, half, 2 * LANES), F32), block, block, pltpu.VMEM(mo.shape, F32)),
-        in_specs=[VMEM] * 4,
-        out_specs=(VMEM,) * 4,
-        scratch_shapes=[block, block],
-        input_output_aliases={0: 1, 1: 2, 2: 3},
+        out_shape=pltpu.VMEM((2, half, 2 * LANES), F32),
+        in_specs=[VMEM] * 5,
+        out_specs=VMEM,
+        scratch_shapes=[block, block, pltpu.VMEM((MOMENTS, 2, tall, LANES), F32), block, block],
         compiler_params=params(8),
         name="gradient_steps",
-    )(*in_vmem(hs, al, mo, theirs))[0]
+    )(*in_vmem(hs, al, mo, theirs, packs))
 
 
 def run_place(halves):
@@ -482,9 +534,10 @@
     both, ends = run_rows(heights, albedo, own_rows, packs, sides)
     ends, images = lax.optimization_barrier((ends, images))
     ends = lax.ppermute(ends, AXES, neighbours((lax.axis_size("gy"), lax.axis_size("gx"))))
-    keep, send = run_moments(images, weights, tables)
+    send = run_moments(sent_kernel, images.shape[0] + 3, images, weights, tables)
     theirs = lax.ppermute(send, "img", [(0, 1), (1, 0)])
-    halves = run_steps(total, *run_fill(heights, albedo, keep, both, ends), theirs)
+    keep = run_moments(own_kernel, MOMENTS, images, weights, tables)
+    halves = run_steps(total, *run_fill(heights, albedo, keep, both, ends), theirs, packs)
     return run_place(lax.all_gather(halves, "img"))
 
 

time: 35.6 us -> 34.3 us (0.963)
  waiting for transfers between devices: 2.2 us -> 1.34 us
  Pallas kernels: 6.53 us -> 6.07 us
    ppermute x1, waiting for transfers between devices: 2.2 us -> 1.34 us  [shards(): theirs = lax.ppermute(send, 'img', [(0, 1), (1, 0)])]
    pallas_call x1 -> x2, Pallas kernels: 0.97 us -> 0.65 us  [run_moments(): pl.pallas_call(kernel, out_shape=pltpu.VMEM((planes, half + ROW, cols), F...]
  transfers between devices with their start and end apart: 2 -> 2, of which waited for: 1 -> 1; matrix products, arithmetic and copies ran while one was open for 0% -> 0% of each run, Pallas kernels for 4% -> 3%
where the time goes in v4:
time: 34.3 us; the launch traced here: 34.2 us
  blocking collectives  18.1 us (53%)
  starting transfers between devices  7.95 us (23%)
  Pallas kernels  6.07 us (18%)
  waiting for transfers between devices  1.34 us (4%)
  between operations  0.71 us (2%)
    all_gather x1, blocking collectives, shards(): sides = lax.all_gather(from_next(fold, core), 'img')  8.61 us
    all_gather x1, blocking collectives, from_next(): both = lax.all_gather(x, AXES, axis_index_groups=groups)  4.94 us
    ppermute x1, starting transfers between devices, shards(): theirs = lax.ppermute(send, 'img', [(0, 1), (1, 0)])  4.51 us
    ppermute x1, starting transfers between devices, shards(): lax.ppermute(ends, AXES, neighbours((lax.axis_size('gy'), lax.axis_size('...  3.44 us
    all_gather x1, blocking collectives, shards(): packs = lax.all_gather(pack, 'img')  2.32 us
    all_gather x1, blocking collectives, shards(): return run_place(lax.all_gather(halves, 'img'))  2.18 us
    pallas_call x1, Pallas kernels, run_steps(): pl.pallas_call(functools.partial(steps_kernel, (0.2 / total, 0.5 / total)...  2.16 us
    pallas_call x1, Pallas kernels, run_edges(): pl.pallas_call(edges_kernel, out_shape=tuple((pltpu.VMEM(x.shape, x.dtype...  1.97 us
  transfers between devices with their start and end apart: 2, of which 1 were waited for; matrix products, arithmetic and copies ran while one was open for 0% of the time, Pallas kernels for 3%

profile of v4, /device:TPU:7, one launch (start us, length us, event | category | flops | bytes accessed | tf_op | source)
XLA Modules:
  0.0 34.2 jit_solution(15683332051233442054)
XLA Ops:
  0.6 2.0 %edges.1 = (f32[2,128,256]{2,1,0:T(8,128)S(1)}, f32[2,128,256]{2,1,0:T(8,128)S(1)}, bf16[4,2,128,256]{3,2,1,0:T(8,128)(2,1)S(1)}, bf16[4,2,128,256]{3,2,1,0:T(8,...) custom-call(s32[4]{0:T(128)} %sun_index_hbm.1, ...), custom_call_target="tpu_custom_call" | custom-call | tf_op jit(solution)/shard_map/edges/pallas_call | solution.py:432
  2.6 2.3 %all-gather = f32[560,128]{1,0:T(8,128)S(1)} all-gather(f32[280,128]{1,0:T(8,128)S(1)} %get-tuple-element.20), channel_id=2, replica_groups=mesh['gy'=16,'gx'=16,'img'=2] {'img'}, dimensions={0}, use_global_device_ids=true | all-gather | bytes 430080 | tf_op jit(solution)/shard_map/all_gather | solution.py:531
  4.9 4.9 %all-gather.1 = f32[256,128]{1,0:T(8,128)S(1)} all-gather(f32[128,128]{1,0:T(8,128)S(1)} %fusion), channel_id=3, replica_groups={{1,2},{3,4},{5,6},{7,8},{9,10},{11,12},{13,14},{15,16},{17,18},{19,20},..., dimensions={0}, use_global_device_ids=true | all-gather | bytes 196608 | tf_op jit(solution)/shard_map/all_gather | solution.py:394
  9.9 8.6 %all_gather.26.sides = f32[2,128,128]{2,1,0:T(8,128)S(1)} all-gather(f32[1,128,128]{2,1,0:T(8,128)S(1)} %constant_dynamic-slice_fusion), channel_id=1, replica_groups=mesh['gy'=16,'gx'=16,'img'=2] {'img'}, dimensions={0}, use_global_device_ids=true | all-gather | bytes 196608 | tf_op jit(solution)/shard_map/all_gather | solution.py:533
  18.5 0.1 edge_rows.1
  18.7 3.4 %collective-permute-start = (f32[64,256]{1,0:T(8,128)S(1)}, f32[64,256]{1,0:T(8,128)S(1)}, u32[]{:S(2)}, u32[]{:S(2)}) collective-permute-start(f32[64,256]{1,0:T(8,128)S(1)} %get-tuple-element.28), channel_id=1, source_target_pairs={{1,32},{3,34},{5,36},{7,38},{9,40},{11,42},{13,44},{15,46},{17,48}... | collective-permute-start | bytes 196616 | tf_op jit(solution)/shard_map/ppermute | solution.py:536
  22.1 0.2 sent_kernel.1
  22.3 4.5 %collective-permute-start.1 = (f32[7,136,256]{2,1,0:T(8,128)S(1)}, f32[7,136,256]{2,1,0:T(8,128)S(1)}, u32[]{:S(2)}, u32[]{:S(2)}) collective-permute-start(f32[7,136,256]{2,1,0:T(8,128)S(1)} %sent_kernel.1), channel_id=1, source_target_pairs={{0,1},{1,0},{2,3},{3,2},{4,5},{5,4},{6,7},{7,6},{8,9},{9,8},{10,11... | collective-permute-start | bytes 2924552 | tf_op jit(solution)/shard_map/ppermute | solution.py:538
  26.8 0.4 %own_kernel.1.keep = f32[9,136,256]{2,1,0:T(8,128)S(1)} custom-call(bf16[4,2,128,256]{3,2,1,0:T(8,128)(2,1)S(1)} %get-tuple-element.24.images, bf16[4,2,128,256]{3,2,1,0:T(8,128)(2,1)S(1)} %get-tuple-element.25.weights, f32[9,8,128]{2,1,0:T(8,128)S(1)} %get-tuple-element.26.tables), custom_call_target="tpu_custom_call" | custom-call | flops 1048576 | bytes 4194304 | tf_op jit(solution)/shard_map/own_kernel/pallas_call | solution.py:454
  27.3 0.0 collective-permute-done.ends
  27.3 0.4 %fill.1 = (f32[3,160,128]{2,1,0:T(8,128)S(1)}, f32[3,160,128]{2,1,0:T(8,128)S(1)}, f32[9,3,160,128]{3,2,1,0:T(8,128)S(1)}) custom-call(f32[256,256]{1,0:T(8,128)S(1)} %bitcast.18, f32[256,256]{1,0:T(8,128)S(1)} %bitcast.20, f32[9,136,256]{2,1,0:T(8,128)S(1)} %own_kernel.1.keep, f32[256,128]{1,0:T(8,128)S(1)} %get-tuple-element.27.both, ...), custom_call_target="tpu_custom_call" | custom-call | flops 17179869184 | bytes 1048576 | tf_op jit(solution)/shard_map/fill/pallas_call | solution.py:483
  27.6 1.3 %collective-permute-done.1.theirs = f32[7,136,256]{2,1,0:T(8,128)S(1)} collective-permute-done((f32[7,136,256]{2,1,0:T(8,128)S(1)}, f32[7,136,256]{2,1,0:T(8,128)S(1)}, u32[]{:S(2)}, u32[]{:S(2)}) %collective-permute-start.1) | collective-permute-done | bytes 974880 | tf_op jit(solution)/shard_map/ppermute | solution.py:538
  29.0 2.2 %gradient_steps.1 = f32[2,128,256]{2,1,0:T(8,128)S(1)} custom-call(f32[3,160,128]{2,1,0:T(8,128)S(1)} %get-tuple-element.29.hs_in, f32[3,160,128]{2,1,0:T(8,128)S(1)} %get-tuple-element.30.al_in, f32[9,3,160,128]{3,2,1,0:T(8,128)S(1)} %get-tuple-element.31.mo_in, f32[7,136,256]{2,1,0:T(8,128)S(1)} %collective-permute-done.1.theirs, f32[2,280,128]{2,1,0:T(8,128)S(1)} %bitcast.15), custom_call_target="tpu_custom_call" | custom-call | tf_op jit(solution)/shard_map/gradient_steps/pallas_call | solution.py:498
  31.1 2.2 %all-gather.2 = f32[4,128,256]{2,1,0:T(8,128)S(1)} all-gather(f32[2,128,256]{2,1,0:T(8,128)S(1)} %gradient_steps.1), channel_id=4, replica_groups=mesh['gy'=16,'gx'=16,'img'=2] {'img'}, dimensions={0}, use_global_device_ids=true | all-gather | bytes 786432 | tf_op jit(solution)/shard_map/all_gather | solution.py:541
  33.3 0.8 %place.1 = (f32[256,256]{1,0:T(8,128)}, f32[256,256]{1,0:T(8,128)}) custom-call(f32[2,2,128,256]{3,2,1,0:T(8,128)S(1)} %bitcast.16), custom_call_target="tpu_custom_call" | custom-call | tf_op jit(solution)/shard_map/place/pallas_call | solution.py:512
  (2 shorter events, 0.0 us)
Async XLA Ops:
  18.7 8.6 %collective-permute-start = (f32[64,256]{1,0:T(8,128)S(1)}, f32[64,256]{1,0:T(8,128)S(1)}, u32[]{:S(2)}, u32[]{:S(2)}) collective-permute-start(f32[64,256]{1,0:T(8,128)S(1)} %get-tuple-element.28), channel_id=1, source_target_pairs={{1,32},{3,34},{5,36},{7,38},{9,40},{11,42},{13,44},{15,46},{17,48}... | collective-permute-start | bytes 196616 | tf_op jit(solution)/shard_map/ppermute | solution.py:536
  22.3 6.7 %collective-permute-start.1 = (f32[7,136,256]{2,1,0:T(8,128)S(1)}, f32[7,136,256]{2,1,0:T(8,128)S(1)}, u32[]{:S(2)}, u32[]{:S(2)}) collective-permute-start(f32[7,136,256]{2,1,0:T(8,128)S(1)} %sent_kernel.1), channel_id=1, source_target_pairs={{0,1},{1,0},{2,3},{3,2},{4,5},{5,4},{6,7},{7,6},{8,9},{9,8},{10,11... | collective-permute-start | bytes 2924552 | tf_op jit(solution)/shard_map/ppermute | solution.py:538

commit v5 on v4

--- a/solution.py
+++ b/solution.py
@@ -34,7 +34,7 @@
 def edges_kernel(
     sun_index_hbm, expo_index_hbm, azimuth_hbm, elevation_hbm, exposure_hbm, height_hbm, albedo_hbm, images_hbm,
     weights_hbm, height, albedo, images, weights, tables, own_fold, own_rows, pack, sun_index, expo_index, azimuth,
-    elevation, exposure, folds, ends_of_rows, small_sems, large_sems
+    elevation, exposure, spreads, ends_of_rows, small_sems, large_sems
 ):
     count, _, half, _ = images.shape
     small = [
@@ -44,8 +44,6 @@
             (elevation_hbm, elevation), (exposure_hbm, exposure),
         ))
     ]
-    for copy in small:
-        copy.start()
     part = half // CHUNKS
     large = []
     for c in range(CHUNKS):
@@ -61,6 +59,8 @@
     for copies in large:
         for copy in copies:
             copy.start()
+    for copy in small:
+        copy.start()
     for copy in small:
         copy.wait()
     line = lax.broadcasted_iota(jnp.int32, (ROW, LANES), 0)
@@ -86,28 +86,28 @@
     step = 16
     lane = lane_ids(step)
 
-    def sums(s, at, view):
-        return add_moments(
-            lambda k: view(weights[k, s, at, :].astype(F32)), lambda k: view(images[k, s, at, :].astype(F32)), count,
-            lambda m, k: factors[m][k : k + 1, :1]
-        )
+    def sums(view):
+        return add_moments(lambda k: view(weights, k), lambda k: view(images, k), count, lambda m, k: factors[m][k : k + 1, :1])
 
     def ends(x):
         return jnp.where(lane < LANES // 2, x[:, :LANES], x[:, -LANES:])
 
-    def fold(planes, first, west, east):
-        for above, below, start, width in zip(*planes, STARTS[first:], WIDTHS[first:]):
-            low = (lane >= start - width) & (lane < start)
-            high = (lane >= start) & (lane < start + width)
-            above = pltpu.roll(above, start, 1)
-            west = jnp.where(high, above, jnp.where(low, pltpu.roll(below, start - width, 1), west))
-            east = jnp.where(low, above, jnp.where(high, pltpu.roll(below, start + width, 1), east))
-        return west, east
-
-    def edge_rows(side, first):
-        acc = sums(side, pl.ds(first, step), lambda x: x)
-        for m in range(MOMENTS):
-            ends_of_rows[side, m] = acc[m][:ROW] if side == 0 else acc[m][-ROW:]
+    middle = (lane >= LANES // 4) & (lane < 3 * LANES // 4)
+
+    def all_ends(upper, lower):
+        return jnp.where(middle, pltpu.roll(ends(lower), LANES // 2, 1), ends(upper)).astype(F32)
+
+    def spread(planes, first, upper, lower):
+        for plane, start, width in zip(planes, STARTS[first:], WIDTHS[first:]):
+            plane = pltpu.roll(plane, start, 1)
+            upper = jnp.where((lane >= start - width) & (lane < start + width), plane, upper)
+            away = (lane - start - LANES // 2 + width) & (LANES - 1)
+            lower = jnp.where(away < 2 * width, plane, lower)
+        return upper, lower
+
+    def edge_rows(side):
+        at = pl.ds(side * (half - step), step)
+        ends_of_rows[side] = jnp.stack(sums(lambda ref, k: ref[k, side, at, :].astype(F32)[side * ROW : (side + 1) * ROW]))
 
     zero = jnp.zeros((step, LANES), F32)
     for c in range(CHUNKS):
@@ -115,11 +115,12 @@
             copy.wait()
         for i in range(c * part, (c + 1) * part, step):
             at = pl.ds(i, step)
-            folds[0, at, :], folds[1, at, :] = fold([sums(s, at, ends) for s in range(2)], 2, zero, zero)
+            planes = sums(lambda ref, k: all_ends(ref[k, 0, at, :], ref[k, 1, at, :]))
+            spreads[0, at, :], spreads[1, at, :] = spread(planes, 2, zero, zero)
         if c == 0:
-            edge_rows(0, 0)
+            edge_rows(0)
         if c == CHUNKS - 1:
-            edge_rows(1, half - step)
+            edge_rows(1)
     core = lax.axis_index("img")
     for m in range(MOMENTS):
         own_rows[pl.ds(m * ROW, ROW), :] = ends_of_rows[core, m]
@@ -127,10 +128,18 @@
             pack[pl.ds(half + (2 * m + t) * ROW, ROW), :] = ends_of_rows[1 - core, m, :, t * LANES : (t + 1) * LANES]
     for copy in large[CHUNKS]:
         copy.wait()
+    high = east_lanes(lane)
+    wide = lane < STARTS[0] + WIDTHS[0]
     for i in range(0, half, step):
         at = pl.ds(i, step)
-        planes = [[ends(0.5 * height[s, at, :]), ends(0.5 * albedo[s, at, :])] for s in range(2)]
-        west, east = fold(planes, 0, folds[0, at, :], folds[1, at, :])
+        planes = [0.5 * all_ends(x[0, at, :], x[1, at, :]) for x in (height, albedo)]
+        upper, lower = spread(planes, 0, spreads[0, at, :], spreads[1, at, :])
+        to_west, to_east = (
+            jnp.where(wide, pltpu.roll(lower, (64 + 6 * d) % LANES, 1), pltpu.roll(lower, (64 + 5 * d) % LANES, 1))
+            for d in (-1, 1)
+        )
+        west = jnp.where(high, upper, to_west)
+        east = jnp.where(high, to_east, upper)
         own_fold[at, :] = jnp.where(core == 0, west, east)
         pack[at, :] = jnp.where(core == 0, east, west)
 
@@ -287,8 +296,6 @@
     bottom = top + half
     hs[...] = 0.5 * hs_in[...]
     al[...] = al_in[...]
-    outer = pl.ds(pl.multiple_of(inner_row(1 - core, half), ROW), ROW)
-    inner = pl.ds(pl.multiple_of(inner_row(core, half), ROW), ROW)
     count = theirs.shape[0] - 3
     table = packs[1 - core, packs.shape[1] - ROW :, :]
     factors = [[jnp.broadcast_to(table[k : k + 1, m : m + 1], (ROW, LANES)) for k in range(count)] for m in range(6)]
@@ -296,48 +303,44 @@
         lanes = slice(t * LANES, (t + 1) * LANES)
         for i in range(-ROW, half, ROW):
             src = pl.ds(ROW + i, ROW)
-            at = inner if i < 0 else pl.ds(top + i, ROW)
             w = [theirs[k, src, lanes] for k in range(count)]
             for m in range(MOMENTS):
                 if m < 6:
                     extra = sum((w[k] * factors[m][k] for k in range(1, count)), w[0] * factors[m][0])
                 else:
                     extra = theirs[count + m - 6, src, lanes]
-                mo[m, t, at, :] = mo_in[m, t, at, :] + extra
-        for m in range(MOMENTS):
-            mo[m, t, outer, :] = mo_in[m, t, outer, :]
-
-    lane = lane_ids(ROW)
-    head = lane == 0
-    tail = lane == LANES - 1
-    wall_w = head & first_x
-    wall_e = tail & last_x
+                if i >= 0:
+                    at = pl.ds(top + i, ROW)
+                    mo[m, t, at, :] = mo_in[m, t, at, :] + extra
+                else:
+                    for at, owner in ((pl.ds(ROW, ROW), 1), (pl.ds(bottom, ROW), 0)):
+                        halo = mo_in[m, t, at, :]
+                        mo[m, t, at, :] = jnp.where(core == owner, halo + extra, halo)
 
     def beside(blocks, sign):
+        lane = lane_ids(blocks[0].shape[0])
+        head = lane == 0
+        tail = lane == LANES - 1
         fore = [pltpu.roll(b, LANES - 1, 1) for b in blocks]
         back = [pltpu.roll(b, 1, 1) for b in blocks]
         easts = [jnp.where(tail, fore[(t + 1) % 3], fore[t]) for t in range(3)]
         wests = [jnp.where(head, back[(t + 2) % 3], back[t]) for t in range(3)]
-        easts[1] = jnp.where(wall_e, sign * blocks[1], easts[1])
-        wests[0] = jnp.where(wall_w, sign * blocks[0], wests[0])
+        easts[1] = jnp.where(tail & last_x, sign * blocks[1], easts[1])
+        wests[0] = jnp.where(head & first_x, sign * blocks[0], wests[0])
         return easts, wests
 
     def borders(ref, sign):
-        @pl.when(first_y)
-        def _():
-            ref[:, pl.ds(top - 1, 1), :] = sign * ref[:, pl.ds(top, 1), :]
-
-        @pl.when(last_y)
-        def _():
-            ref[:, pl.ds(bottom, 1), :] = sign * ref[:, pl.ds(bottom - 1, 1), :]
-
-    def slopes(i, carry):
-        base = pl.multiple_of(i * ROW, ROW)
-        at = pl.ds(pl.multiple_of(base + ROW, ROW), ROW)
+        for flag, out_row, row in ((first_y, top - 1, top), (last_y, bottom, bottom - 1)):
+            for t in range(3):
+                at = pl.ds(out_row, 1)
+                ref[t, at, :] = jnp.where(flag, sign * ref[t, pl.ds(row, 1), :], ref[t, at, :])
+
+    def slopes(row, size, last):
+        at = pl.ds(row, size)
         easts, wests = beside([hs[t, at, :] for t in range(3)], 1.0)
         for t in range(3):
             p = easts[t] - wests[t]
-            q = hs[t, pl.ds(base + ROW + 1, ROW), :] - hs[t, pl.ds(base + ROW - 1, ROW), :]
+            q = hs[t, pl.ds(row + 1, size), :] - hs[t, pl.ds(row - 1, size), :]
             scale = lax.rsqrt(1.0 + p * p + q * q)
             xx, xy, xz, yy, yz, zz, vx, vy, vz = [(mo if t < 2 else mo_in)[m, t, at, :] for m in range(MOMENTS)]
             alb = al[t, at, :]
@@ -349,32 +352,36 @@
             turn = scale * grad_a
             bend = 0.3 - lit * turn
             gps[t, at, :] = p * bend - lit * gx
-            gqs[t, at, :] = q * bend - lit * gy
-            al[t, at, :] = alb - rate_a * grad_a
-        return carry
-
-    def descend(i, carry):
-        base = pl.multiple_of(i * ROW, ROW)
-        at = pl.ds(pl.multiple_of(base + ROW, ROW), ROW)
+            if not (last and t == 2):
+                gqs[t, at, :] = q * bend - lit * gy
+                al[t, at, :] = alb - rate_a * grad_a
+
+    def descend(row, size, last):
+        at = pl.ds(row, size)
         easts, wests = beside([gps[t, at, :] for t in range(3)], -1.0)
-        for t in range(3):
-            fall = (wests[t] - easts[t]) + (gqs[t, pl.ds(base + ROW - 1, ROW), :] - gqs[t, pl.ds(base + ROW + 1, ROW), :])
-            hs[t, at, :] = hs[t, at, :] - (0.25 * rate_h) * fall
-        return carry
-
-    blocks = half // ROW + 2
+        for t in range(2 if last else 3):
+            fall = (wests[t] - easts[t]) + (gqs[t, pl.ds(row - 1, size), :] - gqs[t, pl.ds(row + 1, size), :])
+            now = hs[t, at, :] - (0.25 * rate_h) * fall
+            if last:
+                lanes = slice(t * LANES, (t + 1) * LANES)
+                out[0, row - top : row - top + size, lanes] = 2.0 * now
+                out[1, row - top : row - top + size, lanes] = al[t, at, :]
+            else:
+                hs[t, at, :] = now
+
     borders(hs, 1.0)
-
-    for _ in range(ITERS):
-        lax.fori_loop(0, blocks, slopes, 0, unroll=blocks)
+    for n in range(ITERS):
+        last = n == ITERS - 1
+        for row in range(ROW, bottom + ROW, 16):
+            slopes(row, 16, last)
         borders(gqs, -1.0)
-        lax.fori_loop(0, blocks, descend, 0, unroll=blocks)
-        borders(hs, 1.0)
-    center = pl.ds(top, half)
-    for t in range(2):
-        lanes = pl.ds(t * LANES, LANES)
-        out[0, :, lanes] = 2.0 * hs[t, center, :]
-        out[1, :, lanes] = al[t, center, :]
+        if last:
+            for row in range(top, bottom, 16):
+                descend(row, 16, True)
+        else:
+            for row in range(ROW, bottom + ROW, 16):
+                descend(row, 16, False)
+            borders(hs, 1.0)
 
 
 def pair_groups(sizes):

time: 34.3 us -> 33.8 us (0.985)
  Pallas kernels: 6.07 us -> 5.58 us
    pallas_call x1, Pallas kernels: 2.16 us -> 1.69 us  [run_steps(): pl.pallas_call(functools.partial(steps_kernel, (0.2 / total, 0.5 / total)...]
where the time goes in v5:
time: 33.8 us; the launch traced here: 33.7 us
  blocking collectives  18.1 us (54%)
  starting transfers between devices  7.95 us (24%)
  Pallas kernels  5.58 us (17%)
  waiting for transfers between devices  1.34 us (4%)
  between operations  0.71 us (2%)
    all_gather x1, blocking collectives, shards(): sides = lax.all_gather(from_next(fold, core), 'img')  8.61 us
    all_gather x1, blocking collectives, from_next(): both = lax.all_gather(x, AXES, axis_index_groups=groups)  4.94 us
    ppermute x1, starting transfers between devices, shards(): theirs = lax.ppermute(send, 'img', [(0, 1), (1, 0)])  4.51 us
    ppermute x1, starting transfers between devices, shards(): lax.ppermute(ends, AXES, neighbours((lax.axis_size('gy'), lax.axis_size('...  3.44 us
    all_gather x1, blocking collectives, shards(): packs = lax.all_gather(pack, 'img')  2.32 us
    all_gather x1, blocking collectives, shards(): return run_place(lax.all_gather(halves, 'img'))  2.18 us
    pallas_call x1, Pallas kernels, run_edges(): pl.pallas_call(edges_kernel, out_shape=tuple((pltpu.VMEM(x.shape, x.dtype...  1.94 us
    pallas_call x1, Pallas kernels, run_steps(): pl.pallas_call(functools.partial(steps_kernel, (0.2 / total, 0.5 / total)...  1.69 us
  transfers between devices with their start and end apart: 2, of which 1 were waited for; matrix products, arithmetic and copies ran while one was open for 0% of the time, Pallas kernels for 3%

profile of v5, /device:TPU:7, one launch (start us, length us, event | category | flops | bytes accessed | tf_op | source)
XLA Modules:
  0.0 33.7 jit_solution(6300263626387113837)
XLA Ops:
  0.6 1.9 %edges.1 = (f32[2,128,256]{2,1,0:T(8,128)S(1)}, f32[2,128,256]{2,1,0:T(8,128)S(1)}, bf16[4,2,128,256]{3,2,1,0:T(8,128)(2,1)S(1)}, bf16[4,2,128,256]{3,2,1,0:T(8,...) custom-call(s32[4]{0:T(128)} %sun_index_hbm.1, ...), custom_call_target="tpu_custom_call" | custom-call | tf_op jit(solution)/shard_map/edges/pallas_call | solution.py:439
  2.6 2.3 %all-gather = f32[560,128]{1,0:T(8,128)S(1)} all-gather(f32[280,128]{1,0:T(8,128)S(1)} %get-tuple-element.20), channel_id=2, replica_groups=mesh['gy'=16,'gx'=16,'img'=2] {'img'}, dimensions={0}, use_global_device_ids=true | all-gather | bytes 430080 | tf_op jit(solution)/shard_map/all_gather | solution.py:538
  4.9 4.9 %all-gather.1 = f32[256,128]{1,0:T(8,128)S(1)} all-gather(f32[128,128]{1,0:T(8,128)S(1)} %fusion), channel_id=3, replica_groups={{1,2},{3,4},{5,6},{7,8},{9,10},{11,12},{13,14},{15,16},{17,18},{19,20},..., dimensions={0}, use_global_device_ids=true | all-gather | bytes 196608 | tf_op jit(solution)/shard_map/all_gather | solution.py:401
  9.9 8.6 %all_gather.26.sides = f32[2,128,128]{2,1,0:T(8,128)S(1)} all-gather(f32[1,128,128]{2,1,0:T(8,128)S(1)} %constant_dynamic-slice_fusion), channel_id=1, replica_groups=mesh['gy'=16,'gx'=16,'img'=2] {'img'}, dimensions={0}, use_global_device_ids=true | all-gather | bytes 196608 | tf_op jit(solution)/shard_map/all_gather | solution.py:540
  18.5 0.1 edge_rows.1
  18.6 3.4 %collective-permute-start = (f32[64,256]{1,0:T(8,128)S(1)}, f32[64,256]{1,0:T(8,128)S(1)}, u32[]{:S(2)}, u32[]{:S(2)}) collective-permute-start(f32[64,256]{1,0:T(8,128)S(1)} %get-tuple-element.28), channel_id=1, source_target_pairs={{1,32},{3,34},{5,36},{7,38},{9,40},{11,42},{13,44},{15,46},{17,48}... | collective-permute-start | bytes 196616 | tf_op jit(solution)/shard_map/ppermute | solution.py:543
  22.1 0.2 sent_kernel.1
  22.3 4.5 %collective-permute-start.1 = (f32[7,136,256]{2,1,0:T(8,128)S(1)}, f32[7,136,256]{2,1,0:T(8,128)S(1)}, u32[]{:S(2)}, u32[]{:S(2)}) collective-permute-start(f32[7,136,256]{2,1,0:T(8,128)S(1)} %sent_kernel.1), channel_id=1, source_target_pairs={{0,1},{1,0},{2,3},{3,2},{4,5},{5,4},{6,7},{7,6},{8,9},{9,8},{10,11... | collective-permute-start | bytes 2924552 | tf_op jit(solution)/shard_map/ppermute | solution.py:545
  26.8 0.4 %own_kernel.1.keep = f32[9,136,256]{2,1,0:T(8,128)S(1)} custom-call(bf16[4,2,128,256]{3,2,1,0:T(8,128)(2,1)S(1)} %get-tuple-element.24.images, bf16[4,2,128,256]{3,2,1,0:T(8,128)(2,1)S(1)} %get-tuple-element.25.weights, f32[9,8,128]{2,1,0:T(8,128)S(1)} %get-tuple-element.26.tables), custom_call_target="tpu_custom_call" | custom-call | flops 1048576 | bytes 4194304 | tf_op jit(solution)/shard_map/own_kernel/pallas_call | solution.py:461
  27.2 0.0 collective-permute-done.ends
  27.3 0.4 %fill.1 = (f32[3,160,128]{2,1,0:T(8,128)S(1)}, f32[3,160,128]{2,1,0:T(8,128)S(1)}, f32[9,3,160,128]{3,2,1,0:T(8,128)S(1)}) custom-call(f32[256,256]{1,0:T(8,128)S(1)} %bitcast.18, f32[256,256]{1,0:T(8,128)S(1)} %bitcast.20, f32[9,136,256]{2,1,0:T(8,128)S(1)} %own_kernel.1.keep, f32[256,128]{1,0:T(8,128)S(1)} %get-tuple-element.27.both, ...), custom_call_target="tpu_custom_call" | custom-call | flops 17179869184 | bytes 1048576 | tf_op jit(solution)/shard_map/fill/pallas_call | solution.py:490
  27.6 1.3 %collective-permute-done.1.theirs = f32[7,136,256]{2,1,0:T(8,128)S(1)} collective-permute-done((f32[7,136,256]{2,1,0:T(8,128)S(1)}, f32[7,136,256]{2,1,0:T(8,128)S(1)}, u32[]{:S(2)}, u32[]{:S(2)}) %collective-permute-start.1) | collective-permute-done | bytes 974880 | tf_op jit(solution)/shard_map/ppermute | solution.py:545
  29.0 1.7 %gradient_steps.1 = f32[2,128,256]{2,1,0:T(8,128)S(1)} custom-call(f32[3,160,128]{2,1,0:T(8,128)S(1)} %get-tuple-element.29.hs_in, f32[3,160,128]{2,1,0:T(8,128)S(1)} %get-tuple-element.30.al_in, f32[9,3,160,128]{3,2,1,0:T(8,128)S(1)} %get-tuple-element.31.mo_in, f32[7,136,256]{2,1,0:T(8,128)S(1)} %collective-permute-done.1.theirs, f32[2,280,128]{2,1,0:T(8,128)S(1)} %bitcast.15), custom_call_target="tpu_custom_call" | custom-call | tf_op jit(solution)/shard_map/gradient_steps/pallas_call | solution.py:505
  30.7 2.2 %all-gather.2 = f32[4,128,256]{2,1,0:T(8,128)S(1)} all-gather(f32[2,128,256]{2,1,0:T(8,128)S(1)} %gradient_steps.1), channel_id=4, replica_groups=mesh['gy'=16,'gx'=16,'img'=2] {'img'}, dimensions={0}, use_global_device_ids=true | all-gather | bytes 786432 | tf_op jit(solution)/shard_map/all_gather | solution.py:548
  32.8 0.8 %place.1 = (f32[256,256]{1,0:T(8,128)}, f32[256,256]{1,0:T(8,128)}) custom-call(f32[2,2,128,256]{3,2,1,0:T(8,128)S(1)} %bitcast.16), custom_call_target="tpu_custom_call" | custom-call | tf_op jit(solution)/shard_map/place/pallas_call | solution.py:519
  (2 shorter events, 0.0 us)
Async XLA Ops:
  18.6 8.6 %collective-permute-start = (f32[64,256]{1,0:T(8,128)S(1)}, f32[64,256]{1,0:T(8,128)S(1)}, u32[]{:S(2)}, u32[]{:S(2)}) collective-permute-start(f32[64,256]{1,0:T(8,128)S(1)} %get-tuple-element.28), channel_id=1, source_target_pairs={{1,32},{3,34},{5,36},{7,38},{9,40},{11,42},{13,44},{15,46},{17,48}... | collective-permute-start | bytes 196616 | tf_op jit(solution)/shard_map/ppermute | solution.py:543
  22.3 6.7 %collective-permute-start.1 = (f32[7,136,256]{2,1,0:T(8,128)S(1)}, f32[7,136,256]{2,1,0:T(8,128)S(1)}, u32[]{:S(2)}, u32[]{:S(2)}) collective-permute-start(f32[7,136,256]{2,1,0:T(8,128)S(1)} %sent_kernel.1), channel_id=1, source_target_pairs={{0,1},{1,0},{2,3},{3,2},{4,5},{5,4},{6,7},{7,6},{8,9},{9,8},{10,11... | collective-permute-start | bytes 2924552 | tf_op jit(solution)/shard_map/ppermute | solution.py:545

commit v6 on v5

--- a/solution.py
+++ b/solution.py
@@ -199,12 +199,7 @@
 
 
 def place_kernel(halves, height, albedo, sems):
-    half = halves.shape[2]
-    copies = [
-        pltpu.make_async_copy(halves.at[c, n], out.at[pl.ds(c * half, half), :], sems.at[c, n])
-        for c in range(2)
-        for n, out in enumerate((height, albedo))
-    ]
+    copies = [pltpu.make_async_copy(halves.at[:, n], out, sems.at[n]) for n, out in enumerate((height, albedo))]
     for copy in copies:
         copy.start()
     for copy in copies:
@@ -246,11 +241,43 @@
     out[pl.ds(ROW_STARTS[PLANES], ROW), :] = jnp.concatenate([corner, corner], axis=1)
 
 
+def neighbours_in_ring(blocks, sign, first_x, last_x):
+    lane = lane_ids(blocks[0].shape[0])
+    head = lane == 0
+    tail = lane == LANES - 1
+    fore = [pltpu.roll(b, LANES - 1, 1) for b in blocks]
+    back = [pltpu.roll(b, 1, 1) for b in blocks]
+    easts = [jnp.where(tail, fore[(t + 1) % 3], fore[t]) for t in range(3)]
+    wests = [jnp.where(head, back[(t + 2) % 3], back[t]) for t in range(3)]
+    easts[1] = jnp.where(tail & last_x, sign * blocks[1], easts[1])
+    wests[0] = jnp.where(head & first_x, sign * blocks[0], wests[0])
+    return easts, wests
+
+
+def mirror(ref, sign, top, bottom):
+    core = lax.axis_index("img")
+    first_y = (lax.axis_index("gy") == 0) & (core == 0)
+    last_y = (lax.axis_index("gy") == lax.axis_size("gy") - 1) & (core == 1)
+    for flag, out_row, row in ((first_y, top - 1, top), (last_y, bottom, bottom - 1)):
+        for t in range(3):
+            at = pl.ds(out_row, 1)
+            ref[t, at, :] = jnp.where(flag, sign * ref[t, pl.ds(row, 1), :], ref[t, at, :])
+
+
+def slopes_at(hs, row, size, first_x, last_x):
+    at = pl.ds(row, size)
+    easts, wests = neighbours_in_ring([hs[t, at, :] for t in range(3)], 1.0, first_x, last_x)
+    for t in range(3):
+        p = easts[t] - wests[t]
+        q = hs[t, pl.ds(row + 1, size), :] - hs[t, pl.ds(row - 1, size), :]
+        yield p, q, lax.rsqrt(1.0 + p * p + q * q)
+
+
 def inner_row(core, half):
     return ROW + (1 - core) * (half + ROW)
 
 
-def fill_kernel(height, albedo, keep, both, ends, hs, al, mo):
+def fill_kernel(height, albedo, keep, both, ends, hs, al, mo, ps, qs, cs):
     rows = height.shape[0]
     core = lax.axis_index("img")
 
@@ -266,11 +293,12 @@
             src, dst = pl.ds(pl.multiple_of(core * half + i, ROW), ROW), pl.ds(2 * ROW + i, ROW)
         sides = both[src, :]
         for k in range(PLANES):
-            body = height[src, :] if k == 0 else albedo[src, :] if k == 1 else keep[k - 2, pl.ds(ROW + i, ROW), :]
+            body = 0.5 * height[src, :] if k == 0 else albedo[src, :] if k == 1 else keep[k - 2, pl.ds(ROW + i, ROW), :]
             ref = plane(k)
             ref[0, dst, :] = body[:, :LANES]
             ref[1, dst, :] = body[:, LANES:]
-            ref[2, dst, :] = pltpu.roll(sides, LANES - STARTS[k], 1)
+            side = pltpu.roll(sides, LANES - STARTS[k], 1)
+            ref[2, dst, :] = 0.5 * side if k == 0 else side
     dst = pl.ds(pl.multiple_of(inner_row(1 - core, half), ROW), ROW)
     sides = ends[pl.ds(ROW_STARTS[PLANES], ROW), :LANES]
     for k in range(PLANES):
@@ -278,24 +306,27 @@
         begin, spare = ROW_STARTS[k], ROW - WIDTHS[k]
         after = ends[pl.ds(begin, ROW), :]
         before = pltpu.roll(after, spare, 0) if k == 0 else ends[pl.ds(begin - spare, ROW), :]
-        body = jnp.where(core == 0, before, after)
+        body = jnp.where(core == 0, before, after) * (0.5 if k == 0 else 1.0)
         ref[0, dst, :] = body[:, :LANES]
         ref[1, dst, :] = body[:, LANES:]
-        ref[2, dst, :] = pltpu.roll(sides, LANES - STARTS[k], 1)
-
-
-def steps_kernel(rates, hs_in, al_in, mo_in, theirs, packs, out, hs, al, mo, gps, gqs):
+        side = pltpu.roll(sides, LANES - STARTS[k], 1)
+        ref[2, dst, :] = 0.5 * side if k == 0 else side
+    first_x = lax.axis_index("gx") == 0
+    last_x = lax.axis_index("gx") == lax.axis_size("gx") - 1
+    mirror(hs, 1.0, 2 * ROW, 2 * ROW + half)
+    for row in range(ROW, half + 3 * ROW, 16):
+        for t, (p, q, scale) in enumerate(slopes_at(hs, row, 16, first_x, last_x)):
+            ps[t, pl.ds(row, 16), :], qs[t, pl.ds(row, 16), :], cs[t, pl.ds(row, 16), :] = p, q, scale
+
+
+def steps_kernel(rates, hs_in, al_in, mo_in, ps, qs, cs, theirs, packs, out, hs, al, mo, gps, gqs):
     half = out.shape[1]
     core = lax.axis_index("img")
-    first_y = (lax.axis_index("gy") == 0) & (core == 0)
-    last_y = (lax.axis_index("gy") == lax.axis_size("gy") - 1) & (core == 1)
     first_x = lax.axis_index("gx") == 0
     last_x = lax.axis_index("gx") == lax.axis_size("gx") - 1
     rate_h, rate_a = rates
     top = 2 * ROW
     bottom = top + half
-    hs[...] = 0.5 * hs_in[...]
-    al[...] = al_in[...]
     count = theirs.shape[0] - 3
     table = packs[1 - core, packs.shape[1] - ROW :, :]
     factors = [[jnp.broadcast_to(table[k : k + 1, m : m + 1], (ROW, LANES)) for k in range(count)] for m in range(6)]
@@ -318,32 +349,20 @@
                         mo[m, t, at, :] = jnp.where(core == owner, halo + extra, halo)
 
     def beside(blocks, sign):
-        lane = lane_ids(blocks[0].shape[0])
-        head = lane == 0
-        tail = lane == LANES - 1
-        fore = [pltpu.roll(b, LANES - 1, 1) for b in blocks]
-        back = [pltpu.roll(b, 1, 1) for b in blocks]
-        easts = [jnp.where(tail, fore[(t + 1) % 3], fore[t]) for t in range(3)]
-        wests = [jnp.where(head, back[(t + 2) % 3], back[t]) for t in range(3)]
-        easts[1] = jnp.where(tail & last_x, sign * blocks[1], easts[1])
-        wests[0] = jnp.where(head & first_x, sign * blocks[0], wests[0])
-        return easts, wests
+        return neighbours_in_ring(blocks, sign, first_x, last_x)
 
     def borders(ref, sign):
-        for flag, out_row, row in ((first_y, top - 1, top), (last_y, bottom, bottom - 1)):
-            for t in range(3):
-                at = pl.ds(out_row, 1)
-                ref[t, at, :] = jnp.where(flag, sign * ref[t, pl.ds(row, 1), :], ref[t, at, :])
-
-    def slopes(row, size, last):
+        mirror(ref, sign, top, bottom)
+
+    def slopes(row, size, first, last):
         at = pl.ds(row, size)
-        easts, wests = beside([hs[t, at, :] for t in range(3)], 1.0)
-        for t in range(3):
-            p = easts[t] - wests[t]
-            q = hs[t, pl.ds(row + 1, size), :] - hs[t, pl.ds(row - 1, size), :]
-            scale = lax.rsqrt(1.0 + p * p + q * q)
+        if first:
+            parts = [(ps[t, at, :], qs[t, at, :], cs[t, at, :]) for t in range(3)]
+        else:
+            parts = slopes_at(hs, row, size, first_x, last_x)
+        for t, (p, q, scale) in enumerate(parts):
             xx, xy, xz, yy, yz, zz, vx, vy, vz = [(mo if t < 2 else mo_in)[m, t, at, :] for m in range(MOMENTS)]
-            alb = al[t, at, :]
+            alb = (al_in if first else al)[t, at, :]
             lit = alb * scale
             gx = lit * (xz - p * xx - q * xy) - vx
             gy = lit * (yz - p * xy - q * yy) - vy
@@ -356,12 +375,12 @@
                 gqs[t, at, :] = q * bend - lit * gy
                 al[t, at, :] = alb - rate_a * grad_a
 
-    def descend(row, size, last):
+    def descend(row, size, first, last):
         at = pl.ds(row, size)
         easts, wests = beside([gps[t, at, :] for t in range(3)], -1.0)
         for t in range(2 if last else 3):
             fall = (wests[t] - easts[t]) + (gqs[t, pl.ds(row - 1, size), :] - gqs[t, pl.ds(row + 1, size), :])
-            now = hs[t, at, :] - (0.25 * rate_h) * fall
+            now = (hs_in if first else hs)[t, at, :] - (0.25 * rate_h) * fall
             if last:
                 lanes = slice(t * LANES, (t + 1) * LANES)
                 out[0, row - top : row - top + size, lanes] = 2.0 * now
@@ -369,18 +388,14 @@
             else:
                 hs[t, at, :] = now
 
-    borders(hs, 1.0)
     for n in range(ITERS):
-        last = n == ITERS - 1
+        first, last = n == 0, n == ITERS - 1
         for row in range(ROW, bottom + ROW, 16):
-            slopes(row, 16, last)
+            slopes(row, 16, first, last)
         borders(gqs, -1.0)
-        if last:
-            for row in range(top, bottom, 16):
-                descend(row, 16, True)
-        else:
-            for row in range(ROW, bottom + ROW, 16):
-                descend(row, 16, False)
+        for row in range(top, bottom, 16) if last else range(ROW, bottom + ROW, 16):
+            descend(row, 16, first, last)
+        if not last:
             borders(hs, 1.0)
 
 
@@ -489,42 +504,43 @@
     block = pltpu.VMEM(frame(heights.shape[0]), F32)
     return pl.pallas_call(
         fill_kernel,
-        out_shape=(block, block, pltpu.VMEM((MOMENTS, *block.shape), F32)),
+        out_shape=(block, block, pltpu.VMEM((MOMENTS, *block.shape), F32), block, block, block),
         in_specs=[VMEM] * 5,
-        out_specs=(VMEM,) * 3,
+        out_specs=(VMEM,) * 6,
         compiler_params=params(8),
         cost_estimate=pl.CostEstimate(flops=1 << 34, bytes_accessed=1 << 20, transcendentals=0),
         name="fill",
     )(*in_vmem(heights, albedo, keep, both, ends))
 
 
-def run_steps(total, hs, al, mo, theirs, packs):
-    _, tall, _ = hs.shape
+def run_steps(total, *args):
+    _, tall, _ = args[0].shape
     half = tall - 4 * ROW
-    block = pltpu.VMEM(hs.shape, F32)
+    block = pltpu.VMEM(args[0].shape, F32)
     return pl.pallas_call(
         functools.partial(steps_kernel, (0.2 / total, 0.5 / total)),
         out_shape=pltpu.VMEM((2, half, 2 * LANES), F32),
-        in_specs=[VMEM] * 5,
+        in_specs=[VMEM] * len(args),
         out_specs=VMEM,
         scratch_shapes=[block, block, pltpu.VMEM((MOMENTS, 2, tall, LANES), F32), block, block],
         compiler_params=params(8),
         name="gradient_steps",
-    )(*in_vmem(hs, al, mo, theirs, packs))
+    )(*in_vmem(*args))
 
 
 def run_place(halves):
     _, _, half, cols = halves.shape
-    out = jax.ShapeDtypeStruct((2 * half, cols), F32)
-    return pl.pallas_call(
+    out = jax.ShapeDtypeStruct((2, half, cols), F32)
+    placed = pl.pallas_call(
         place_kernel,
         out_shape=(out, out),
         in_specs=[VMEM],
         out_specs=(HBM, HBM),
-        scratch_shapes=[pltpu.SemaphoreType.DMA((2, 2))],
+        scratch_shapes=[pltpu.SemaphoreType.DMA((2,))],
         compiler_params=params(8),
         name="place",
     )(*in_vmem(halves))
+    return tuple(x.reshape(2 * half, cols) for x in placed)
 
 
 def shards(

time: 33.8 us -> 33.7 us (level)
  transfers between devices with their start and end apart: 2 -> 2, of which waited for: 1 -> 1; matrix products, arithmetic and copies ran while one was open for 0% -> 0% of each run, Pallas kernels for 3% -> 4%
where the time goes in v6:
time: 33.7 us; the launch traced here: 33.5 us
  blocking collectives  18.1 us (54%)
  starting transfers between devices  7.95 us (24%)
  Pallas kernels  5.67 us (17%)
  waiting for transfers between devices  1.13 us (3%)
  between operations  0.71 us (2%)
    all_gather x1, blocking collectives, shards(): sides = lax.all_gather(from_next(fold, core), 'img')  8.61 us
    all_gather x1, blocking collectives, from_next(): both = lax.all_gather(x, AXES, axis_index_groups=groups)  4.94 us
    ppermute x1, starting transfers between devices, shards(): theirs = lax.ppermute(send, 'img', [(0, 1), (1, 0)])  4.51 us
    ppermute x1, starting transfers between devices, shards(): lax.ppermute(ends, AXES, neighbours((lax.axis_size('gy'), lax.axis_size('...  3.44 us
    all_gather x1, blocking collectives, shards(): packs = lax.all_gather(pack, 'img')  2.32 us
    all_gather x1, blocking collectives, shards(): return run_place(lax.all_gather(halves, 'img'))  2.18 us
    pallas_call x1, Pallas kernels, run_edges(): pl.pallas_call(edges_kernel, out_shape=tuple((pltpu.VMEM(x.shape, x.dtype...  1.94 us
    pallas_call x1, Pallas kernels, run_steps(): pl.pallas_call(functools.partial(steps_kernel, (0.2 / total, 0.5 / total)...  1.58 us
  transfers between devices with their start and end apart: 2, of which 1 were waited for; matrix products, arithmetic and copies ran while one was open for 0% of the time, Pallas kernels for 4%

profile of v6, /device:TPU:7, one launch (start us, length us, event | category | flops | bytes accessed | tf_op | source)
XLA Modules:
  0.0 33.5 jit_solution(8760054706517792339)
XLA Ops:
  0.6 1.9 %edges.1 = (f32[2,128,256]{2,1,0:T(8,128)S(1)}, f32[2,128,256]{2,1,0:T(8,128)S(1)}, bf16[4,2,128,256]{3,2,1,0:T(8,128)(2,1)S(1)}, bf16[4,2,128,256]{3,2,1,0:T(8,...) custom-call(s32[4]{0:T(128)} %sun_index_hbm.1, ...), custom_call_target="tpu_custom_call" | custom-call | tf_op jit(solution)/shard_map/edges/pallas_call | solution.py:454
  2.6 2.3 %all-gather = f32[560,128]{1,0:T(8,128)S(1)} all-gather(f32[280,128]{1,0:T(8,128)S(1)} %get-tuple-element.25), channel_id=2, replica_groups=mesh['gy'=16,'gx'=16,'img'=2] {'img'}, dimensions={0}, use_global_device_ids=true | all-gather | bytes 430080 | tf_op jit(solution)/shard_map/all_gather | solution.py:554
  4.9 4.9 %all-gather.1 = f32[256,128]{1,0:T(8,128)S(1)} all-gather(f32[128,128]{1,0:T(8,128)S(1)} %fusion), channel_id=3, replica_groups={{1,2},{3,4},{5,6},{7,8},{9,10},{11,12},{13,14},{15,16},{17,18},{19,20},..., dimensions={0}, use_global_device_ids=true | all-gather | bytes 196608 | tf_op jit(solution)/shard_map/all_gather | solution.py:416
  9.9 8.6 %all_gather.26.sides = f32[2,128,128]{2,1,0:T(8,128)S(1)} all-gather(f32[1,128,128]{2,1,0:T(8,128)S(1)} %constant_dynamic-slice_fusion), channel_id=1, replica_groups=mesh['gy'=16,'gx'=16,'img'=2] {'img'}, dimensions={0}, use_global_device_ids=true | all-gather | bytes 196608 | tf_op jit(solution)/shard_map/all_gather | solution.py:556
  18.5 0.1 edge_rows.1
  18.6 3.4 %collective-permute-start = (f32[64,256]{1,0:T(8,128)S(1)}, f32[64,256]{1,0:T(8,128)S(1)}, u32[]{:S(2)}, u32[]{:S(2)}) collective-permute-start(f32[64,256]{1,0:T(8,128)S(1)} %get-tuple-element.33), channel_id=1, source_target_pairs={{1,32},{3,34},{5,36},{7,38},{9,40},{11,42},{13,44},{15,46},{17,48}... | collective-permute-start | bytes 196616 | tf_op jit(solution)/shard_map/ppermute | solution.py:559
  22.1 0.2 sent_kernel.1
  22.3 4.5 %collective-permute-start.1 = (f32[7,136,256]{2,1,0:T(8,128)S(1)}, f32[7,136,256]{2,1,0:T(8,128)S(1)}, u32[]{:S(2)}, u32[]{:S(2)}) collective-permute-start(f32[7,136,256]{2,1,0:T(8,128)S(1)} %sent_kernel.1), channel_id=1, source_target_pairs={{0,1},{1,0},{2,3},{3,2},{4,5},{5,4},{6,7},{7,6},{8,9},{9,8},{10,11... | collective-permute-start | bytes 2924552 | tf_op jit(solution)/shard_map/ppermute | solution.py:561
  26.8 0.4 %own_kernel.1.keep = f32[9,136,256]{2,1,0:T(8,128)S(1)} custom-call(bf16[4,2,128,256]{3,2,1,0:T(8,128)(2,1)S(1)} %get-tuple-element.29.images, bf16[4,2,128,256]{3,2,1,0:T(8,128)(2,1)S(1)} %get-tuple-element.30.weights, f32[9,8,128]{2,1,0:T(8,128)S(1)} %get-tuple-element.31.tables), custom_call_target="tpu_custom_call" | custom-call | flops 1048576 | bytes 4194304 | tf_op jit(solution)/shard_map/own_kernel/pallas_call | solution.py:476
  27.2 0.0 collective-permute-done.ends
  27.3 0.6 %fill.1 = (f32[3,160,128]{2,1,0:T(8,128)S(1)}, f32[3,160,128]{2,1,0:T(8,128)S(1)}, f32[9,3,160,128]{3,2,1,0:T(8,128)S(1)}, f32[3,160,128]{2,1,0:T(8,128)S(1)}, f...) custom-call(f32[256,256]{1,0:T(8,128)S(1)} %bitcast.20, f32[256,256]{1,0:T(8,128)S(1)} %bitcast.22, ...), custom_call_target="tpu_custom_call" | custom-call | flops 17179869184 | bytes 1048576 | tf_op jit(solution)/shard_map/fill/pallas_call | solution.py:505
  27.8 1.1 %collective-permute-done.1.theirs = f32[7,136,256]{2,1,0:T(8,128)S(1)} collective-permute-done((f32[7,136,256]{2,1,0:T(8,128)S(1)}, f32[7,136,256]{2,1,0:T(8,128)S(1)}, u32[]{:S(2)}, u32[]{:S(2)}) %collective-permute-start.1) | collective-permute-done | bytes 974880 | tf_op jit(solution)/shard_map/ppermute | solution.py:561
  29.0 1.6 %gradient_steps.1 = f32[2,128,256]{2,1,0:T(8,128)S(1)} custom-call(f32[3,160,128]{2,1,0:T(8,128)S(1)} %get-tuple-element.34.hs_in, f32[3,160,128]{2,1,0:T(8,128)S(1)} %get-tuple-element.35.al_in, f32[9,3,160,128]{3,2,1,0:T(8,128)S(1)} %get-tuple-element.36.mo_in, f32[3,160,128]{2,1,0:T(8,128)S(1)} %get-tuple-element.37.ps, ...), custom_call_target="tpu_custom_call" | custom-call | tf_op jit(solution)/shard_map/gradient_steps/pallas_call | solution.py:520
  30.5 2.2 %all-gather.2 = f32[4,128,256]{2,1,0:T(8,128)S(1)} all-gather(f32[2,128,256]{2,1,0:T(8,128)S(1)} %gradient_steps.1), channel_id=4, replica_groups=mesh['gy'=16,'gx'=16,'img'=2] {'img'}, dimensions={0}, use_global_device_ids=true | all-gather | bytes 786432 | tf_op jit(solution)/shard_map/all_gather | solution.py:564
  32.7 0.8 %place.1 = (f32[2,128,256]{2,1,0:T(8,128)}, f32[2,128,256]{2,1,0:T(8,128)}) custom-call(f32[2,2,128,256]{3,2,1,0:T(8,128)S(1)} %bitcast.18), custom_call_target="tpu_custom_call" | custom-call | tf_op jit(solution)/shard_map/place/pallas_call | solution.py:534
  (2 shorter events, 0.0 us)
Async XLA Ops:
  18.6 8.6 %collective-permute-start = (f32[64,256]{1,0:T(8,128)S(1)}, f32[64,256]{1,0:T(8,128)S(1)}, u32[]{:S(2)}, u32[]{:S(2)}) collective-permute-start(f32[64,256]{1,0:T(8,128)S(1)} %get-tuple-element.33), channel_id=1, source_target_pairs={{1,32},{3,34},{5,36},{7,38},{9,40},{11,42},{13,44},{15,46},{17,48}... | collective-permute-start | bytes 196616 | tf_op jit(solution)/shard_map/ppermute | solution.py:559
  22.3 6.7 %collective-permute-start.1 = (f32[7,136,256]{2,1,0:T(8,128)S(1)}, f32[7,136,256]{2,1,0:T(8,128)S(1)}, u32[]{:S(2)}, u32[]{:S(2)}) collective-permute-start(f32[7,136,256]{2,1,0:T(8,128)S(1)} %sent_kernel.1), channel_id=1, source_target_pairs={{0,1},{1,0},{2,3},{3,2},{4,5},{5,4},{6,7},{7,6},{8,9},{9,8},{10,11... | collective-permute-start | bytes 2924552 | tf_op jit(solution)/shard_map/ppermute | solution.py:561

commit v7 on v6

--- a/solution.py
+++ b/solution.py
@@ -18,6 +18,14 @@
 STARTS = tuple(6 if k == 0 else 17 + 10 * (k - 1) for k in range(PLANES))
 ROW_STARTS = tuple(sum(WIDTHS[:k]) for k in range(PLANES + 1))
 F32 = jnp.float32
+
+
+def part_of(core):
+    return (core + 1 + lax.axis_index("gy")) % 2
+
+
+def side_of(core):
+    return (core + 1 + lax.axis_index("gx")) % 2
 
 
 def lane_ids(rows):
@@ -121,11 +129,12 @@
             edge_rows(0)
         if c == CHUNKS - 1:
             edge_rows(1)
-    core = lax.axis_index("img")
+    part = part_of(lax.axis_index("img"))
+    side = side_of(lax.axis_index("img"))
     for m in range(MOMENTS):
-        own_rows[pl.ds(m * ROW, ROW), :] = ends_of_rows[core, m]
+        own_rows[pl.ds(m * ROW, ROW), :] = ends_of_rows[part, m]
         for t in range(2):
-            pack[pl.ds(half + (2 * m + t) * ROW, ROW), :] = ends_of_rows[1 - core, m, :, t * LANES : (t + 1) * LANES]
+            pack[pl.ds(half + (2 * m + t) * ROW, ROW), :] = ends_of_rows[1 - part, m, :, t * LANES : (t + 1) * LANES]
     for copy in large[CHUNKS]:
         copy.wait()
     high = east_lanes(lane)
@@ -140,8 +149,8 @@
         )
         west = jnp.where(high, upper, to_west)
         east = jnp.where(high, to_east, upper)
-        own_fold[at, :] = jnp.where(core == 0, west, east)
-        pack[at, :] = jnp.where(core == 0, east, west)
+        own_fold[at, :] = jnp.where(side == 0, west, east)
+        pack[at, :] = jnp.where(side == 0, east, west)
 
 
 def add_moments(weight, image, count, factor):
@@ -172,7 +181,7 @@
 
 def sent_kernel(images, weights, tables, out):
     count, _, half, _ = images.shape
-    core = 1 - lax.axis_index("img")
+    core = 1 - part_of(lax.axis_index("img"))
     for s, at, dst in part_rows(core, half):
         acc = [None] * 3
         for k in range(count):
@@ -188,7 +197,7 @@
 
 def own_kernel(images, weights, tables, out):
     count, _, half, _ = images.shape
-    core = lax.axis_index("img")
+    core = part_of(lax.axis_index("img"))
     for s, at, dst in part_rows(core, half):
         acc = add_moments(
             lambda k: weights[k, s, at, :].astype(F32), lambda k: images[k, s, at, :].astype(F32), count,
@@ -199,7 +208,12 @@
 
 
 def place_kernel(halves, height, albedo, sems):
-    copies = [pltpu.make_async_copy(halves.at[:, n], out, sems.at[n]) for n, out in enumerate((height, albedo))]
+    half = halves.shape[2]
+    copies = [
+        pltpu.make_async_copy(halves.at[part_of(part), n], out.at[pl.ds(part * half, half), :], sems.at[part, n])
+        for part in range(2)
+        for n, out in enumerate((height, albedo))
+    ]
     for copy in copies:
         copy.start()
     for copy in copies:
@@ -210,20 +224,22 @@
     rows = height.shape[0]
     half = rows // 2
     core = lax.axis_index("img")
+    part = part_of(core)
+    west_core = side_of(0)
     lane = lane_ids(ROW)
     east = east_lanes(lane)
     wide = lane < STARTS[0] + WIDTHS[0]
     for i in range(0, half, ROW):
         at = pl.ds(i, ROW)
-        west_side, east_side = sides[0, at, :], sides[1, at, :]
+        west_side, east_side = sides[west_core, at, :], sides[1 - west_core, at, :]
         both[at, :] = jnp.where(east, east_side, west_side)
         moved_e, moved_w = (
             jnp.where(wide, pltpu.roll(x, 6 * d % LANES, 1), pltpu.roll(x, 5 * d % LANES, 1))
             for x, d in ((east_side, 1), (west_side, -1))
         )
         both[pl.ds(half + i, ROW), :] = jnp.where(east, moved_e, moved_w)
-    at = pl.ds(pl.multiple_of(core * (rows - ROW), ROW), ROW)
-    upper = core == 0
+    at = pl.ds(pl.multiple_of(part * (rows - ROW), ROW), ROW)
+    upper = part == 0
 
     def edge(x, n):
         return jnp.where(upper, x[:n], x[ROW - n :])
@@ -255,9 +271,9 @@
 
 
 def mirror(ref, sign, top, bottom):
-    core = lax.axis_index("img")
-    first_y = (lax.axis_index("gy") == 0) & (core == 0)
-    last_y = (lax.axis_index("gy") == lax.axis_size("gy") - 1) & (core == 1)
+    part = part_of(lax.axis_index("img"))
+    first_y = (lax.axis_index("gy") == 0) & (part == 0)
+    last_y = (lax.axis_index("gy") == lax.axis_size("gy") - 1) & (part == 1)
     for flag, out_row, row in ((first_y, top - 1, top), (last_y, bottom, bottom - 1)):
         for t in range(3):
             at = pl.ds(out_row, 1)
@@ -279,7 +295,7 @@
 
 def fill_kernel(height, albedo, keep, both, ends, hs, al, mo, ps, qs, cs):
     rows = height.shape[0]
-    core = lax.axis_index("img")
+    core = part_of(lax.axis_index("img"))
 
     def plane(k):
         return hs if k == 0 else al if k == 1 else mo.at[k - 2]
@@ -322,6 +338,7 @@
 def steps_kernel(rates, hs_in, al_in, mo_in, ps, qs, cs, theirs, packs, out, hs, al, mo, gps, gqs):
     half = out.shape[1]
     core = lax.axis_index("img")
+    part = part_of(core)
     first_x = lax.axis_index("gx") == 0
     last_x = lax.axis_index("gx") == lax.axis_size("gx") - 1
     rate_h, rate_a = rates
@@ -346,7 +363,7 @@
                 else:
                     for at, owner in ((pl.ds(ROW, ROW), 1), (pl.ds(bottom, ROW), 0)):
                         halo = mo_in[m, t, at, :]
-                        mo[m, t, at, :] = jnp.where(core == owner, halo + extra, halo)
+                        mo[m, t, at, :] = jnp.where(part == owner, halo + extra, halo)
 
     def beside(blocks, sign):
         return neighbours_in_ring(blocks, sign, first_x, last_x)
@@ -399,31 +416,31 @@
             borders(hs, 1.0)
 
 
-def pair_groups(sizes):
+def seams(size):
+    return [(i, i % 2) for i in range(size - 1)]
+
+
+def flat(sizes, y, x, core):
+    return (y * sizes[1] + x) * 2 + core
+
+
+def column_groups(sizes):
     ny, nx = sizes
-
-    def flat(y, x, core):
-        return (y * nx + x) * 2 + core
-
-    groups = [[flat(y, x, 1), flat(y, x + 1, 0)] for y in range(ny) for x in range(nx - 1)]
+    groups = [[flat(sizes, y, x, core), flat(sizes, y, x + 1, core)] for y in range(ny) for x, core in seams(nx)]
     for y in range(0, ny, 2):
-        groups += [[flat(y, x, core), flat(y + 1, x, core)] for x, core in ((0, 0), (nx - 1, 1))]
+        groups += [[flat(sizes, y, x, 1), flat(sizes, y + 1, x, 1)] for x in (0, nx - 1)]
     return groups
 
 
-def from_next(x, core):
-    groups = pair_groups((lax.axis_size("gy"), lax.axis_size("gx")))
+def from_beside(x, core):
+    groups = column_groups((lax.axis_size("gy"), lax.axis_size("gx")))
     both = lax.all_gather(x, AXES, axis_index_groups=groups)
-    return lax.dynamic_index_in_dim(both, core, 0, keepdims=False)
-
-
-def neighbours(sizes):
+    return lax.dynamic_index_in_dim(both, side_of(core), 0, keepdims=False)
+
+
+def row_pairs(sizes):
     ny, nx = sizes
-
-    def flat(y, x, core):
-        return (y * nx + x) * 2 + core
-
-    pairs = [(flat(y, x, 1), flat(y + 1, x, 0)) for y in range(ny - 1) for x in range(nx)]
+    pairs = [(flat(sizes, y, x, core), flat(sizes, y + 1, x, core)) for y, core in seams(ny) for x in range(nx)]
     return pairs + [(b, a) for a, b in pairs]
 
 
@@ -530,17 +547,16 @@
 
 def run_place(halves):
     _, _, half, cols = halves.shape
-    out = jax.ShapeDtypeStruct((2, half, cols), F32)
-    placed = pl.pallas_call(
+    out = jax.ShapeDtypeStruct((2 * half, cols), F32)
+    return pl.pallas_call(
         place_kernel,
         out_shape=(out, out),
         in_specs=[VMEM],
         out_specs=(HBM, HBM),
-        scratch_shapes=[pltpu.SemaphoreType.DMA((2,))],
+        scratch_shapes=[pltpu.SemaphoreType.DMA((2, 2))],
         compiler_params=params(8),
         name="place",
     )(*in_vmem(halves))
-    return tuple(x.reshape(2 * half, cols) for x in placed)
 
 
 def shards(
@@ -553,10 +569,10 @@
     )
     packs = lax.all_gather(pack, "img")
     fold = own_fold + lax.dynamic_index_in_dim(packs, 1 - core, 0, keepdims=False)[: own_fold.shape[0]]
-    sides = lax.all_gather(from_next(fold, core), "img")
+    sides = lax.all_gather(from_beside(fold, core), "img")
     both, ends = run_rows(heights, albedo, own_rows, packs, sides)
     ends, images = lax.optimization_barrier((ends, images))
-    ends = lax.ppermute(ends, AXES, neighbours((lax.axis_size("gy"), lax.axis_size("gx"))))
+    ends = lax.ppermute(ends, AXES, row_pairs((lax.axis_size("gy"), lax.axis_size("gx"))))
     send = run_moments(sent_kernel, images.shape[0] + 3, images, weights, tables)
     theirs = lax.ppermute(send, "img", [(0, 1), (1, 0)])
     keep = run_moments(own_kernel, MOMENTS, images, weights, tables)

time: 33.7 us -> 33.4 us (level)
  blocking collectives: 18.1 us -> 17.7 us
  waiting for transfers between devices: 1.13 us -> 1.51 us
  starting transfers between devices: 7.95 us -> 7.57 us
    ppermute x1, starting transfers between devices: 4.51 us -> 1.92 us  [shards(): theirs = lax.ppermute(send, 'img', [(0, 1), (1, 0)])]
    ppermute x1, starting transfers between devices: 3.44 us -> 5.65 us  [shards(): lax.ppermute(ends, AXES, row_pairs((lax.axis_size('gy'), lax.axis_size('g...]
    ppermute x1, waiting for transfers between devices: 0.01 us -> 0.38 us  [shards(): lax.ppermute(ends, AXES, row_pairs((lax.axis_size('gy'), lax.axis_size('g...]
    all_gather x2, blocking collectives: 13.6 us -> 13.2 us  [the longest x1 11.3 us: from_beside(): both = lax.all_gather(x, AXES, axis_index_groups=groups)]
  transfers between devices with their start and end apart: 2 -> 2, of which waited for: 1 -> 2; matrix products, arithmetic and copies ran while one was open for 0% -> 0% of each run, Pallas kernels for 4% -> 4%
where the time goes in v7:
time: 33.4 us; the launch traced here: 33.2 us
  blocking collectives  17.7 us (53%)
  starting transfers between devices  7.57 us (23%)
  Pallas kernels  5.68 us (17%)
  waiting for transfers between devices  1.51 us (5%)
  between operations  0.71 us (2%)
    all_gather x1, blocking collectives, from_beside(): both = lax.all_gather(x, AXES, axis_index_groups=groups)  11.3 us
    ppermute x1, starting transfers between devices, shards(): lax.ppermute(ends, AXES, row_pairs((lax.axis_size('gy'), lax.axis_size('g...  5.65 us
    all_gather x1, blocking collectives, shards(): packs = lax.all_gather(pack, 'img')  2.32 us
    all_gather x1, blocking collectives, shards(): return run_place(lax.all_gather(halves, 'img'))  2.18 us
    pallas_call x1, Pallas kernels, run_edges(): pl.pallas_call(edges_kernel, out_shape=tuple((pltpu.VMEM(x.shape, x.dtype...  1.94 us
    ppermute x1, starting transfers between devices, shards(): theirs = lax.ppermute(send, 'img', [(0, 1), (1, 0)])  1.92 us
    all_gather x1, blocking collectives, shards(): sides = lax.all_gather(from_beside(fold, core), 'img')  1.89 us
    pallas_call x1, Pallas kernels, run_steps(): pl.pallas_call(functools.partial(steps_kernel, (0.2 / total, 0.5 / total)...  1.59 us
  transfers between devices with their start and end apart: 2, of which 2 were waited for; matrix products, arithmetic and copies ran while one was open for 0% of the time, Pallas kernels for 4%

profile of v7, /device:TPU:7, one launch (start us, length us, event | category | flops | bytes accessed | tf_op | source)
XLA Modules:
  0.0 33.2 jit_solution(7820312484098524796)
XLA Ops:
  0.6 1.9 %edges.1 = (f32[2,128,256]{2,1,0:T(8,128)S(1)}, f32[2,128,256]{2,1,0:T(8,128)S(1)}, bf16[4,2,128,256]{3,2,1,0:T(8,128)(2,1)S(1)}, bf16[4,2,128,256]{3,2,1,0:T(8,...) custom-call(s32[4]{0:T(128)} %sun_index_hbm.1, ...), custom_call_target="tpu_custom_call" | custom-call | tf_op jit(solution)/shard_map/edges/pallas_call | solution.py:471
  2.6 2.3 %all-gather = f32[560,128]{1,0:T(8,128)S(1)} all-gather(f32[280,128]{1,0:T(8,128)S(1)} %get-tuple-element.23), channel_id=2, replica_groups=mesh['gy'=16,'gx'=16,'img'=2] {'img'}, dimensions={0}, use_global_device_ids=true | all-gather | bytes 430080 | tf_op jit(solution)/shard_map/all_gather | solution.py:570
  4.9 11.3 %all-gather.1 = f32[256,128]{1,0:T(8,128)S(1)} all-gather(f32[128,128]{1,0:T(8,128)S(1)} %fusion), channel_id=3, replica_groups={{0,2},{3,5},{4,6},{7,9},{8,10},{11,13},{12,14},{15,17},{16,18},{19,21},..., dimensions={0}, use_global_device_ids=true | all-gather | bytes 196608 | tf_op jit(solution)/shard_map/all_gather | solution.py:437
  16.3 1.9 %all_gather.26.sides = f32[2,128,128]{2,1,0:T(8,128)S(1)} all-gather(f32[1,128,128]{2,1,0:T(8,128)S(1)} %constant_dynamic-slice_fusion), channel_id=1, replica_groups=mesh['gy'=16,'gx'=16,'img'=2] {'img'}, dimensions={0}, use_global_device_ids=true | all-gather | bytes 196608 | tf_op jit(solution)/shard_map/all_gather | solution.py:572
  18.2 0.1 edge_rows.1
  18.3 5.6 %collective-permute-start = (f32[64,256]{1,0:T(8,128)S(1)}, f32[64,256]{1,0:T(8,128)S(1)}, u32[]{:S(2)}, u32[]{:S(2)}) collective-permute-start(f32[64,256]{1,0:T(8,128)S(1)} %get-tuple-element.31), channel_id=1, source_target_pairs={{0,32},{2,34},{4,36},{6,38},{8,40},{10,42},{12,44},{14,46},{16,48}... | collective-permute-start | bytes 196616 | tf_op jit(solution)/shard_map/ppermute | solution.py:575
  24.0 0.2 sent_kernel.1
  24.2 1.9 %collective-permute-start.1 = (f32[7,136,256]{2,1,0:T(8,128)S(1)}, f32[7,136,256]{2,1,0:T(8,128)S(1)}, u32[]{:S(2)}, u32[]{:S(2)}) collective-permute-start(f32[7,136,256]{2,1,0:T(8,128)S(1)} %sent_kernel.1), channel_id=1, source_target_pairs={{0,1},{1,0},{2,3},{3,2},{4,5},{5,4},{6,7},{7,6},{8,9},{9,8},{10,11... | collective-permute-start | bytes 2924552 | tf_op jit(solution)/shard_map/ppermute | solution.py:577
  26.1 0.4 %own_kernel.1.keep = f32[9,136,256]{2,1,0:T(8,128)S(1)} custom-call(bf16[4,2,128,256]{3,2,1,0:T(8,128)(2,1)S(1)} %get-tuple-element.27.images, bf16[4,2,128,256]{3,2,1,0:T(8,128)(2,1)S(1)} %get-tuple-element.28.weights, f32[9,8,128]{2,1,0:T(8,128)S(1)} %get-tuple-element.29.tables), custom_call_target="tpu_custom_call" | custom-call | flops 1048576 | bytes 4194304 | tf_op jit(solution)/shard_map/own_kernel/pallas_call | solution.py:493
  26.6 0.4 %collective-permute-done.ends = f32[64,256]{1,0:T(8,128)S(1)} collective-permute-done((f32[64,256]{1,0:T(8,128)S(1)}, f32[64,256]{1,0:T(8,128)S(1)}, u32[]{:S(2)}, u32[]{:S(2)}) %collective-permute-start) | collective-permute-done | bytes 65568 | tf_op jit(solution)/shard_map/ppermute | solution.py:575
  26.9 0.5 %fill.1 = (f32[3,160,128]{2,1,0:T(8,128)S(1)}, f32[3,160,128]{2,1,0:T(8,128)S(1)}, f32[9,3,160,128]{3,2,1,0:T(8,128)S(1)}, f32[3,160,128]{2,1,0:T(8,128)S(1)}, f...) custom-call(f32[256,256]{1,0:T(8,128)S(1)} %bitcast.18, f32[256,256]{1,0:T(8,128)S(1)} %bitcast.20, ...), custom_call_target="tpu_custom_call" | custom-call | flops 17179869184 | bytes 1048576 | tf_op jit(solution)/shard_map/fill/pallas_call | solution.py:522
  27.5 1.1 %collective-permute-done.1.theirs = f32[7,136,256]{2,1,0:T(8,128)S(1)} collective-permute-done((f32[7,136,256]{2,1,0:T(8,128)S(1)}, f32[7,136,256]{2,1,0:T(8,128)S(1)}, u32[]{:S(2)}, u32[]{:S(2)}) %collective-permute-start.1) | collective-permute-done | bytes 974880 | tf_op jit(solution)/shard_map/ppermute | solution.py:577
  28.6 1.6 %gradient_steps.1 = f32[2,128,256]{2,1,0:T(8,128)S(1)} custom-call(f32[3,160,128]{2,1,0:T(8,128)S(1)} %get-tuple-element.32.hs_in, f32[3,160,128]{2,1,0:T(8,128)S(1)} %get-tuple-element.33.al_in, f32[9,3,160,128]{3,2,1,0:T(8,128)S(1)} %get-tuple-element.34.mo_in, f32[3,160,128]{2,1,0:T(8,128)S(1)} %get-tuple-element.35.ps, ...), custom_call_target="tpu_custom_call" | custom-call | tf_op jit(solution)/shard_map/gradient_steps/pallas_call | solution.py:537
  30.2 2.2 %all-gather.2 = f32[4,128,256]{2,1,0:T(8,128)S(1)} all-gather(f32[2,128,256]{2,1,0:T(8,128)S(1)} %gradient_steps.1), channel_id=4, replica_groups=mesh['gy'=16,'gx'=16,'img'=2] {'img'}, dimensions={0}, use_global_device_ids=true | all-gather | bytes 786432 | tf_op jit(solution)/shard_map/all_gather | solution.py:580
  32.4 0.8 %place.1 = (f32[256,256]{1,0:T(8,128)}, f32[256,256]{1,0:T(8,128)}) custom-call(f32[2,2,128,256]{3,2,1,0:T(8,128)S(1)} %bitcast.16), custom_call_target="tpu_custom_call" | custom-call | tf_op jit(solution)/shard_map/place/pallas_call | solution.py:551
  (2 shorter events, 0.0 us)
Async XLA Ops:
  18.3 8.6 %collective-permute-start = (f32[64,256]{1,0:T(8,128)S(1)}, f32[64,256]{1,0:T(8,128)S(1)}, u32[]{:S(2)}, u32[]{:S(2)}) collective-permute-start(f32[64,256]{1,0:T(8,128)S(1)} %get-tuple-element.31), channel_id=1, source_target_pairs={{0,32},{2,34},{4,36},{6,38},{8,40},{10,42},{12,44},{14,46},{16,48}... | collective-permute-start | bytes 196616 | tf_op jit(solution)/shard_map/ppermute | solution.py:575
  24.2 4.4 %collective-permute-start.1 = (f32[7,136,256]{2,1,0:T(8,128)S(1)}, f32[7,136,256]{2,1,0:T(8,128)S(1)}, u32[]{:S(2)}, u32[]{:S(2)}) collective-permute-start(f32[7,136,256]{2,1,0:T(8,128)S(1)} %sent_kernel.1), channel_id=1, source_target_pairs={{0,1},{1,0},{2,3},{3,2},{4,5},{5,4},{6,7},{7,6},{8,9},{9,8},{10,11... | collective-permute-start | bytes 2924552 | tf_op jit(solution)/shard_map/ppermute | solution.py:577

commit v8 on v7

--- a/solution.py
+++ b/solution.py
@@ -293,7 +293,7 @@
     return ROW + (1 - core) * (half + ROW)
 
 
-def fill_kernel(height, albedo, keep, both, ends, hs, al, mo, ps, qs, cs):
+def fill_kernel(height, albedo, keep, both, ends, packs, hs, al, mo, ps, qs, cs, factors):
     rows = height.shape[0]
     core = part_of(lax.axis_index("img"))
 
@@ -327,6 +327,10 @@
         ref[1, dst, :] = body[:, LANES:]
         side = pltpu.roll(sides, LANES - STARTS[k], 1)
         ref[2, dst, :] = 0.5 * side if k == 0 else side
+    table = packs[1 - lax.axis_index("img"), packs.shape[1] - ROW :, :]
+    for m in range(6):
+        for k in range(factors.shape[1]):
+            factors[m, k] = jnp.broadcast_to(table[k : k + 1, m : m + 1], (ROW, LANES))
     first_x = lax.axis_index("gx") == 0
     last_x = lax.axis_index("gx") == lax.axis_size("gx") - 1
     mirror(hs, 1.0, 2 * ROW, 2 * ROW + half)
@@ -335,18 +339,15 @@
             ps[t, pl.ds(row, 16), :], qs[t, pl.ds(row, 16), :], cs[t, pl.ds(row, 16), :] = p, q, scale
 
 
-def steps_kernel(rates, hs_in, al_in, mo_in, ps, qs, cs, theirs, packs, out, hs, al, mo, gps, gqs):
+def steps_kernel(rates, hs_in, al_in, mo_in, ps, qs, cs, factors, theirs, out, hs, al, mo, gps, gqs):
     half = out.shape[1]
-    core = lax.axis_index("img")
-    part = part_of(core)
+    part = part_of(lax.axis_index("img"))
     first_x = lax.axis_index("gx") == 0
     last_x = lax.axis_index("gx") == lax.axis_size("gx") - 1
     rate_h, rate_a = rates
     top = 2 * ROW
     bottom = top + half
     count = theirs.shape[0] - 3
-    table = packs[1 - core, packs.shape[1] - ROW :, :]
-    factors = [[jnp.broadcast_to(table[k : k + 1, m : m + 1], (ROW, LANES)) for k in range(count)] for m in range(6)]
     for t in range(2):
         lanes = slice(t * LANES, (t + 1) * LANES)
         for i in range(-ROW, half, ROW):
@@ -354,7 +355,7 @@
             w = [theirs[k, src, lanes] for k in range(count)]
             for m in range(MOMENTS):
                 if m < 6:
-                    extra = sum((w[k] * factors[m][k] for k in range(1, count)), w[0] * factors[m][0])
+                    extra = sum((w[k] * factors[m, k] for k in range(1, count)), w[0] * factors[m, 0])
                 else:
                     extra = theirs[count + m - 6, src, lanes]
                 if i >= 0:
@@ -517,17 +518,17 @@
     return (3, rows // 2 + 4 * ROW, LANES)
 
 
-def run_fill(heights, albedo, keep, both, ends):
+def run_fill(heights, albedo, keep, both, ends, packs, count):
     block = pltpu.VMEM(frame(heights.shape[0]), F32)
     return pl.pallas_call(
         fill_kernel,
-        out_shape=(block, block, pltpu.VMEM((MOMENTS, *block.shape), F32), block, block, block),
-        in_specs=[VMEM] * 5,
-        out_specs=(VMEM,) * 6,
+        out_shape=(block, block, pltpu.VMEM((MOMENTS, *block.shape), F32), block, block, block, pltpu.VMEM((6, count, ROW, LANES), F32)),
+        in_specs=[VMEM] * 6,
+        out_specs=(VMEM,) * 7,
         compiler_params=params(8),
         cost_estimate=pl.CostEstimate(flops=1 << 34, bytes_accessed=1 << 20, transcendentals=0),
         name="fill",
-    )(*in_vmem(heights, albedo, keep, both, ends))
+    )(*in_vmem(heights, albedo, keep, both, ends, packs))
 
 
 def run_steps(total, *args):
@@ -576,7 +577,7 @@
     send = run_moments(sent_kernel, images.shape[0] + 3, images, weights, tables)
     theirs = lax.ppermute(send, "img", [(0, 1), (1, 0)])
     keep = run_moments(own_kernel, MOMENTS, images, weights, tables)
-    halves = run_steps(total, *run_fill(heights, albedo, keep, both, ends), theirs, packs)
+    halves = run_steps(total, *run_fill(heights, albedo, keep, both, ends, packs, images.shape[0]), theirs)
     return run_place(lax.all_gather(halves, "img"))
 
 

time: 33.4 us -> 33.3 us (level)
  no operation moved by 1% of the time
where the time goes in v8:
time: 33.3 us; the launch traced here: 33.1 us
  blocking collectives  17.7 us (53%)
  starting transfers between devices  7.57 us (23%)
  Pallas kernels  5.62 us (17%)
  waiting for transfers between devices  1.51 us (5%)
  between operations  0.71 us (2%)
    all_gather x1, blocking collectives, from_beside(): both = lax.all_gather(x, AXES, axis_index_groups=groups)  11.3 us
    ppermute x1, starting transfers between devices, shards(): lax.ppermute(ends, AXES, row_pairs((lax.axis_size('gy'), lax.axis_size('g...  5.65 us
    all_gather x1, blocking collectives, shards(): packs = lax.all_gather(pack, 'img')  2.32 us
    all_gather x1, blocking collectives, shards(): return run_place(lax.all_gather(halves, 'img'))  2.18 us
    pallas_call x1, Pallas kernels, run_edges(): pl.pallas_call(edges_kernel, out_shape=tuple((pltpu.VMEM(x.shape, x.dtype...  1.94 us
    ppermute x1, starting transfers between devices, shards(): theirs = lax.ppermute(send, 'img', [(0, 1), (1, 0)])  1.92 us
    all_gather x1, blocking collectives, shards(): sides = lax.all_gather(from_beside(fold, core), 'img')  1.89 us
    pallas_call x1, Pallas kernels, run_steps(): pl.pallas_call(functools.partial(steps_kernel, (0.2 / total, 0.5 / total)...  1.51 us
  transfers between devices with their start and end apart: 2, of which 2 were waited for; matrix products, arithmetic and copies ran while one was open for 0% of the time, Pallas kernels for 4%

profile of v8, /device:TPU:7, one launch (start us, length us, event | category | flops | bytes accessed | tf_op | source)
XLA Modules:
  0.0 33.1 jit_solution(13733425639887640812)
XLA Ops:
  0.6 1.9 %edges.1 = (f32[2,128,256]{2,1,0:T(8,128)S(1)}, f32[2,128,256]{2,1,0:T(8,128)S(1)}, bf16[4,2,128,256]{3,2,1,0:T(8,128)(2,1)S(1)}, bf16[4,2,128,256]{3,2,1,0:T(8,...) custom-call(s32[4]{0:T(128)} %sun_index_hbm.1, ...), custom_call_target="tpu_custom_call" | custom-call | tf_op jit(solution)/shard_map/edges/pallas_call | solution.py:472
  2.6 2.3 %all-gather = f32[560,128]{1,0:T(8,128)S(1)} all-gather(f32[280,128]{1,0:T(8,128)S(1)} %get-tuple-element.24), channel_id=2, replica_groups=mesh['gy'=16,'gx'=16,'img'=2] {'img'}, dimensions={0}, use_global_device_ids=true | all-gather | bytes 430080 | tf_op jit(solution)/shard_map/all_gather | solution.py:571
  4.9 11.3 %all-gather.1 = f32[256,128]{1,0:T(8,128)S(1)} all-gather(f32[128,128]{1,0:T(8,128)S(1)} %fusion), channel_id=3, replica_groups={{0,2},{3,5},{4,6},{7,9},{8,10},{11,13},{12,14},{15,17},{16,18},{19,21},..., dimensions={0}, use_global_device_ids=true | all-gather | bytes 196608 | tf_op jit(solution)/shard_map/all_gather | solution.py:438
  16.3 1.9 %all_gather.26.sides = f32[2,128,128]{2,1,0:T(8,128)S(1)} all-gather(f32[1,128,128]{2,1,0:T(8,128)S(1)} %constant_dynamic-slice_fusion), channel_id=1, replica_groups=mesh['gy'=16,'gx'=16,'img'=2] {'img'}, dimensions={0}, use_global_device_ids=true | all-gather | bytes 196608 | tf_op jit(solution)/shard_map/all_gather | solution.py:573
  18.2 0.1 edge_rows.1
  18.3 5.6 %collective-permute-start = (f32[64,256]{1,0:T(8,128)S(1)}, f32[64,256]{1,0:T(8,128)S(1)}, u32[]{:S(2)}, u32[]{:S(2)}) collective-permute-start(f32[64,256]{1,0:T(8,128)S(1)} %get-tuple-element.32), channel_id=1, source_target_pairs={{0,32},{2,34},{4,36},{6,38},{8,40},{10,42},{12,44},{14,46},{16,48}... | collective-permute-start | bytes 196616 | tf_op jit(solution)/shard_map/ppermute | solution.py:576
  24.0 0.2 sent_kernel.1
  24.2 1.9 %collective-permute-start.1 = (f32[7,136,256]{2,1,0:T(8,128)S(1)}, f32[7,136,256]{2,1,0:T(8,128)S(1)}, u32[]{:S(2)}, u32[]{:S(2)}) collective-permute-start(f32[7,136,256]{2,1,0:T(8,128)S(1)} %sent_kernel.1), channel_id=1, source_target_pairs={{0,1},{1,0},{2,3},{3,2},{4,5},{5,4},{6,7},{7,6},{8,9},{9,8},{10,11... | collective-permute-start | bytes 2924552 | tf_op jit(solution)/shard_map/ppermute | solution.py:578
  26.1 0.4 %own_kernel.1.keep = f32[9,136,256]{2,1,0:T(8,128)S(1)} custom-call(bf16[4,2,128,256]{3,2,1,0:T(8,128)(2,1)S(1)} %get-tuple-element.28.images, bf16[4,2,128,256]{3,2,1,0:T(8,128)(2,1)S(1)} %get-tuple-element.29.weights, f32[9,8,128]{2,1,0:T(8,128)S(1)} %get-tuple-element.30.tables), custom_call_target="tpu_custom_call" | custom-call | flops 1048576 | bytes 4194304 | tf_op jit(solution)/shard_map/own_kernel/pallas_call | solution.py:494
  26.6 0.4 %collective-permute-done.ends = f32[64,256]{1,0:T(8,128)S(1)} collective-permute-done((f32[64,256]{1,0:T(8,128)S(1)}, f32[64,256]{1,0:T(8,128)S(1)}, u32[]{:S(2)}, u32[]{:S(2)}) %collective-permute-start) | collective-permute-done | bytes 65568 | tf_op jit(solution)/shard_map/ppermute | solution.py:576
  26.9 0.6 %fill.1 = (f32[3,160,128]{2,1,0:T(8,128)S(1)}, f32[3,160,128]{2,1,0:T(8,128)S(1)}, f32[9,3,160,128]{3,2,1,0:T(8,128)S(1)}, f32[3,160,128]{2,1,0:T(8,128)S(1)}, f...) custom-call(f32[256,256]{1,0:T(8,128)S(1)} %bitcast.18, ...), custom_call_target="tpu_custom_call" | custom-call | flops 17179869184 | bytes 1048576 | tf_op jit(solution)/shard_map/fill/pallas_call | solution.py:523
  27.5 1.1 %collective-permute-done.1.theirs = f32[7,136,256]{2,1,0:T(8,128)S(1)} collective-permute-done((f32[7,136,256]{2,1,0:T(8,128)S(1)}, f32[7,136,256]{2,1,0:T(8,128)S(1)}, u32[]{:S(2)}, u32[]{:S(2)}) %collective-permute-start.1) | collective-permute-done | bytes 974880 | tf_op jit(solution)/shard_map/ppermute | solution.py:578
  28.6 1.5 %gradient_steps.1 = f32[2,128,256]{2,1,0:T(8,128)S(1)} custom-call(f32[3,160,128]{2,1,0:T(8,128)S(1)} %get-tuple-element.33.hs_in, f32[3,160,128]{2,1,0:T(8,128)S(1)} %get-tuple-element.34.al_in, f32[9,3,160,128]{3,2,1,0:T(8,128)S(1)} %get-tuple-element.35.mo_in, f32[3,160,128]{2,1,0:T(8,128)S(1)} %get-tuple-element.36.ps, ...), custom_call_target="tpu_custom_call" | custom-call | tf_op jit(solution)/shard_map/gradient_steps/pallas_call | solution.py:538
  30.1 2.2 %all-gather.2 = f32[4,128,256]{2,1,0:T(8,128)S(1)} all-gather(f32[2,128,256]{2,1,0:T(8,128)S(1)} %gradient_steps.1), channel_id=4, replica_groups=mesh['gy'=16,'gx'=16,'img'=2] {'img'}, dimensions={0}, use_global_device_ids=true | all-gather | bytes 786432 | tf_op jit(solution)/shard_map/all_gather | solution.py:581
  32.3 0.8 %place.1 = (f32[256,256]{1,0:T(8,128)}, f32[256,256]{1,0:T(8,128)}) custom-call(f32[2,2,128,256]{3,2,1,0:T(8,128)S(1)} %bitcast.13), custom_call_target="tpu_custom_call" | custom-call | tf_op jit(solution)/shard_map/place/pallas_call | solution.py:552
  (2 shorter events, 0.0 us)
Async XLA Ops:
  18.3 8.6 %collective-permute-start = (f32[64,256]{1,0:T(8,128)S(1)}, f32[64,256]{1,0:T(8,128)S(1)}, u32[]{:S(2)}, u32[]{:S(2)}) collective-permute-start(f32[64,256]{1,0:T(8,128)S(1)} %get-tuple-element.32), channel_id=1, source_target_pairs={{0,32},{2,34},{4,36},{6,38},{8,40},{10,42},{12,44},{14,46},{16,48}... | collective-permute-start | bytes 196616 | tf_op jit(solution)/shard_map/ppermute | solution.py:576
  24.2 4.4 %collective-permute-start.1 = (f32[7,136,256]{2,1,0:T(8,128)S(1)}, f32[7,136,256]{2,1,0:T(8,128)S(1)}, u32[]{:S(2)}, u32[]{:S(2)}) collective-permute-start(f32[7,136,256]{2,1,0:T(8,128)S(1)} %sent_kernel.1), channel_id=1, source_target_pairs={{0,1},{1,0},{2,3},{3,2},{4,5},{5,4},{6,7},{7,6},{8,9},{9,8},{10,11... | collective-permute-start | bytes 2924552 | tf_op jit(solution)/shard_map/ppermute | solution.py:578

commit v9 on v8

--- a/solution.py
+++ b/solution.py
@@ -189,7 +189,7 @@
             put(out, k, dst, w, core)
             u = w * images[k, s, at, :].astype(F32)
             for m in range(3):
-                term = u * tables[6 + m, k : k + 1, :1]
+                term = u * jnp.concatenate([tables[6 + m, k : k + 1, :]] * 2, axis=1)
                 acc[m] = term if k == 0 else acc[m] + term
         for m in range(3):
             put(out, count + m, dst, acc[m], core)

time: 33.3 us -> 33.3 us (level)
  no operation moved by 1% of the time
where the time goes in v9:
time: 33.3 us; the launch traced here: 33.1 us
  blocking collectives  17.7 us (53%)
  starting transfers between devices  7.57 us (23%)
  Pallas kernels  5.6 us (17%)
  waiting for transfers between devices  1.51 us (5%)
  between operations  0.71 us (2%)
    all_gather x1, blocking collectives, from_beside(): both = lax.all_gather(x, AXES, axis_index_groups=groups)  11.3 us
    ppermute x1, starting transfers between devices, shards(): lax.ppermute(ends, AXES, row_pairs((lax.axis_size('gy'), lax.axis_size('g...  5.65 us
    all_gather x1, blocking collectives, shards(): packs = lax.all_gather(pack, 'img')  2.32 us
    all_gather x1, blocking collectives, shards(): return run_place(lax.all_gather(halves, 'img'))  2.18 us
    pallas_call x1, Pallas kernels, run_edges(): pl.pallas_call(edges_kernel, out_shape=tuple((pltpu.VMEM(x.shape, x.dtype...  1.94 us
    ppermute x1, starting transfers between devices, shards(): theirs = lax.ppermute(send, 'img', [(0, 1), (1, 0)])  1.92 us
    all_gather x1, blocking collectives, shards(): sides = lax.all_gather(from_beside(fold, core), 'img')  1.89 us
    pallas_call x1, Pallas kernels, run_steps(): pl.pallas_call(functools.partial(steps_kernel, (0.2 / total, 0.5 / total)...  1.51 us
  transfers between devices with their start and end apart: 2, of which 2 were waited for; matrix products, arithmetic and copies ran while one was open for 0% of the time, Pallas kernels for 4%

profile of v9, /device:TPU:7, one launch (start us, length us, event | category | flops | bytes accessed | tf_op | source)
XLA Modules:
  0.0 33.1 jit_solution(14040069330669603636)
XLA Ops:
  0.6 1.9 %edges.1 = (f32[2,128,256]{2,1,0:T(8,128)S(1)}, f32[2,128,256]{2,1,0:T(8,128)S(1)}, bf16[4,2,128,256]{3,2,1,0:T(8,128)(2,1)S(1)}, bf16[4,2,128,256]{3,2,1,0:T(8,...) custom-call(s32[4]{0:T(128)} %sun_index_hbm.1, ...), custom_call_target="tpu_custom_call" | custom-call | tf_op jit(solution)/shard_map/edges/pallas_call | solution.py:472
  2.6 2.3 %all-gather = f32[560,128]{1,0:T(8,128)S(1)} all-gather(f32[280,128]{1,0:T(8,128)S(1)} %get-tuple-element.24), channel_id=2, replica_groups=mesh['gy'=16,'gx'=16,'img'=2] {'img'}, dimensions={0}, use_global_device_ids=true | all-gather | bytes 430080 | tf_op jit(solution)/shard_map/all_gather | solution.py:571
  4.9 11.3 %all-gather.1 = f32[256,128]{1,0:T(8,128)S(1)} all-gather(f32[128,128]{1,0:T(8,128)S(1)} %fusion), channel_id=3, replica_groups={{0,2},{3,5},{4,6},{7,9},{8,10},{11,13},{12,14},{15,17},{16,18},{19,21},..., dimensions={0}, use_global_device_ids=true | all-gather | bytes 196608 | tf_op jit(solution)/shard_map/all_gather | solution.py:438
  16.3 1.9 %all_gather.26.sides = f32[2,128,128]{2,1,0:T(8,128)S(1)} all-gather(f32[1,128,128]{2,1,0:T(8,128)S(1)} %constant_dynamic-slice_fusion), channel_id=1, replica_groups=mesh['gy'=16,'gx'=16,'img'=2] {'img'}, dimensions={0}, use_global_device_ids=true | all-gather | bytes 196608 | tf_op jit(solution)/shard_map/all_gather | solution.py:573
  18.2 0.1 edge_rows.1
  18.3 5.6 %collective-permute-start = (f32[64,256]{1,0:T(8,128)S(1)}, f32[64,256]{1,0:T(8,128)S(1)}, u32[]{:S(2)}, u32[]{:S(2)}) collective-permute-start(f32[64,256]{1,0:T(8,128)S(1)} %get-tuple-element.32), channel_id=1, source_target_pairs={{0,32},{2,34},{4,36},{6,38},{8,40},{10,42},{12,44},{14,46},{16,48}... | collective-permute-start | bytes 196616 | tf_op jit(solution)/shard_map/ppermute | solution.py:576
  24.0 0.2 sent_kernel.1
  24.2 1.9 %collective-permute-start.1 = (f32[7,136,256]{2,1,0:T(8,128)S(1)}, f32[7,136,256]{2,1,0:T(8,128)S(1)}, u32[]{:S(2)}, u32[]{:S(2)}) collective-permute-start(f32[7,136,256]{2,1,0:T(8,128)S(1)} %sent_kernel.1), channel_id=1, source_target_pairs={{0,1},{1,0},{2,3},{3,2},{4,5},{5,4},{6,7},{7,6},{8,9},{9,8},{10,11... | collective-permute-start | bytes 2924552 | tf_op jit(solution)/shard_map/ppermute | solution.py:578
  26.1 0.4 %own_kernel.1.keep = f32[9,136,256]{2,1,0:T(8,128)S(1)} custom-call(bf16[4,2,128,256]{3,2,1,0:T(8,128)(2,1)S(1)} %get-tuple-element.28.images, bf16[4,2,128,256]{3,2,1,0:T(8,128)(2,1)S(1)} %get-tuple-element.29.weights, f32[9,8,128]{2,1,0:T(8,128)S(1)} %get-tuple-element.30.tables), custom_call_target="tpu_custom_call" | custom-call | flops 1048576 | bytes 4194304 | tf_op jit(solution)/shard_map/own_kernel/pallas_call | solution.py:494
  26.5 0.4 %collective-permute-done.ends = f32[64,256]{1,0:T(8,128)S(1)} collective-permute-done((f32[64,256]{1,0:T(8,128)S(1)}, f32[64,256]{1,0:T(8,128)S(1)}, u32[]{:S(2)}, u32[]{:S(2)}) %collective-permute-start) | collective-permute-done | bytes 65568 | tf_op jit(solution)/shard_map/ppermute | solution.py:576
  26.9 0.6 %fill.1 = (f32[3,160,128]{2,1,0:T(8,128)S(1)}, f32[3,160,128]{2,1,0:T(8,128)S(1)}, f32[9,3,160,128]{3,2,1,0:T(8,128)S(1)}, f32[3,160,128]{2,1,0:T(8,128)S(1)}, f...) custom-call(f32[256,256]{1,0:T(8,128)S(1)} %bitcast.18, ...), custom_call_target="tpu_custom_call" | custom-call | flops 17179869184 | bytes 1048576 | tf_op jit(solution)/shard_map/fill/pallas_call | solution.py:523
  27.5 1.1 %collective-permute-done.1.theirs = f32[7,136,256]{2,1,0:T(8,128)S(1)} collective-permute-done((f32[7,136,256]{2,1,0:T(8,128)S(1)}, f32[7,136,256]{2,1,0:T(8,128)S(1)}, u32[]{:S(2)}, u32[]{:S(2)}) %collective-permute-start.1) | collective-permute-done | bytes 974880 | tf_op jit(solution)/shard_map/ppermute | solution.py:578
  28.6 1.5 %gradient_steps.1 = f32[2,128,256]{2,1,0:T(8,128)S(1)} custom-call(f32[3,160,128]{2,1,0:T(8,128)S(1)} %get-tuple-element.33.hs_in, f32[3,160,128]{2,1,0:T(8,128)S(1)} %get-tuple-element.34.al_in, f32[9,3,160,128]{3,2,1,0:T(8,128)S(1)} %get-tuple-element.35.mo_in, f32[3,160,128]{2,1,0:T(8,128)S(1)} %get-tuple-element.36.ps, ...), custom_call_target="tpu_custom_call" | custom-call | tf_op jit(solution)/shard_map/gradient_steps/pallas_call | solution.py:538
  30.1 2.2 %all-gather.2 = f32[4,128,256]{2,1,0:T(8,128)S(1)} all-gather(f32[2,128,256]{2,1,0:T(8,128)S(1)} %gradient_steps.1), channel_id=4, replica_groups=mesh['gy'=16,'gx'=16,'img'=2] {'img'}, dimensions={0}, use_global_device_ids=true | all-gather | bytes 786432 | tf_op jit(solution)/shard_map/all_gather | solution.py:581
  32.3 0.8 %place.1 = (f32[256,256]{1,0:T(8,128)}, f32[256,256]{1,0:T(8,128)}) custom-call(f32[2,2,128,256]{3,2,1,0:T(8,128)S(1)} %bitcast.13), custom_call_target="tpu_custom_call" | custom-call | tf_op jit(solution)/shard_map/place/pallas_call | solution.py:552
  (2 shorter events, 0.0 us)
Async XLA Ops:
  18.3 8.6 %collective-permute-start = (f32[64,256]{1,0:T(8,128)S(1)}, f32[64,256]{1,0:T(8,128)S(1)}, u32[]{:S(2)}, u32[]{:S(2)}) collective-permute-start(f32[64,256]{1,0:T(8,128)S(1)} %get-tuple-element.32), channel_id=1, source_target_pairs={{0,32},{2,34},{4,36},{6,38},{8,40},{10,42},{12,44},{14,46},{16,48}... | collective-permute-start | bytes 196616 | tf_op jit(solution)/shard_map/ppermute | solution.py:576
  24.2 4.4 %collective-permute-start.1 = (f32[7,136,256]{2,1,0:T(8,128)S(1)}, f32[7,136,256]{2,1,0:T(8,128)S(1)}, u32[]{:S(2)}, u32[]{:S(2)}) collective-permute-start(f32[7,136,256]{2,1,0:T(8,128)S(1)} %sent_kernel.1), channel_id=1, source_target_pairs={{0,1},{1,0},{2,3},{3,2},{4,5},{5,4},{6,7},{7,6},{8,9},{9,8},{10,11... | collective-permute-start | bytes 2924552 | tf_op jit(solution)/shard_map/ppermute | solution.py:578
